TPU v7x, 32 devices: a whole 2x2x4 slice. The times are simulated.
32 devices in a mesh: dp: 2 (over x), ctx: 4 (over z), exp: 4 (over y, core).
Axes of the slice: x: 2, y: 2, z: 4, core: 2. Of those that a mesh axis runs over, the one named last changes fastest.
Arguments:
- tokens: bfloat16 [2, 4, 2048, 1536], P('dp', 'exp', 'ctx'), may hold values from -6 to 6
- cotangent: bfloat16 [2, 4, 2048, 1536], P('dp', 'exp', 'ctx'), may hold values from -6 to 6
- doc_starts: int32 [2, 4, 9], P('dp', 'exp'), may hold values from 0 to 2047, as said below
- routes: int32 [2, 4, 2048, 8], P('dp', 'exp', 'ctx'), may hold values from 0 to 15, all different within a row
- priority: int32 [2, 4, 4, 4096], P('dp', 'exp', 'ctx'), may hold values from 0 to 4095, each once within a row
- attend_master: float32 [1536, 2560], P(('dp', 'ctx', 'exp')), may hold values from -0.15625 to 0.15625
- attend_mean: float32 [1536, 2560], P(('dp', 'ctx', 'exp')), may hold values from -56 to 56
- attend_square: float32 [1536, 2560], P(('dp', 'ctx', 'exp')), may hold values from 409.6 to 1638.4
- outward_master: float32 [1536, 1536], P(None, ('dp', 'ctx', 'exp')), may hold values from -0.625 to 0.625
- outward_mean: float32 [1536, 1536], P(None, ('dp', 'ctx', 'exp')), may hold values from -14 to 14
- outward_square: float32 [1536, 1536], P(None, ('dp', 'ctx', 'exp')), may hold values from 24.576 to 98.304
- router_master: float32 [1536, 16], P(('dp', 'ctx', 'exp')), may hold values from -0.078125 to 0.078125
- router_mean: float32 [1536, 16], P(('dp', 'ctx', 'exp')), may hold values from -896 to 896
- router_square: float32 [1536, 16], P(('dp', 'ctx', 'exp')), may hold values from 98304 to 409600
- gains_master: float32 [2, 1536], P(None, ('dp', 'ctx', 'exp')), may hold values from 0.5 to 1.5
- gains_mean: float32 [2, 1536], P(None, ('dp', 'ctx', 'exp')), may hold values from -80 to 80
- gains_square: float32 [2, 1536], P(None, ('dp', 'ctx', 'exp')), may hold values from 655.36 to 2621.44
- expand_master: float32 [16, 1536, 1024], P('exp', ('dp', 'ctx')), may hold values from -0.15625 to 0.15625
- expand_mean: float32 [16, 1536, 1024], P('exp', ('dp', 'ctx')), may hold values from -40 to 40
- expand_square: float32 [16, 1536, 1024], P('exp', ('dp', 'ctx')), may hold values from 212.992 to 819.2
- shrink_master: float32 [16, 512, 1536], P('exp', ('dp', 'ctx')), may hold values from -1.5 to 1.5
- shrink_mean: float32 [16, 512, 1536], P('exp', ('dp', 'ctx')), may hold values from -4 to 4
- shrink_square: float32 [16, 512, 1536], P('exp', ('dp', 'ctx')), may hold values from 2.4576 to 9.8304
Outputs:
- output: bfloat16 [2, 4, 2048, 1536], P('dp', 'exp', 'ctx')
- input_grad: float32 [2, 4, 2048, 1536], P('dp', 'exp', 'ctx')
- attend_averaged: float32 [1536, 2560], P(('dp', 'ctx', 'exp'))
- attend_squares: float32 [1536, 2560], P(('dp', 'ctx', 'exp'))
- attend_updated: float32 [1536, 2560], P(('dp', 'ctx', 'exp'))
- attend_copy: bfloat16 [1536, 2560], P(('dp', 'ctx', 'exp'))
- outward_averaged: float32 [1536, 1536], P(None, ('dp', 'ctx', 'exp'))
- outward_squares: float32 [1536, 1536], P(None, ('dp', 'ctx', 'exp'))
- outward_updated: float32 [1536, 1536], P(None, ('dp', 'ctx', 'exp'))
- outward_copy: bfloat16 [1536, 1536], P(None, ('dp', 'ctx', 'exp'))
- router_averaged: float32 [1536, 16], P(('dp', 'ctx', 'exp'))
- router_squares: float32 [1536, 16], P(('dp', 'ctx', 'exp'))
- router_updated: float32 [1536, 16], P(('dp', 'ctx', 'exp'))
- router_copy: bfloat16 [1536, 16], P(('dp', 'ctx', 'exp'))
- gains_averaged: float32 [2, 1536], P(None, ('dp', 'ctx', 'exp'))
- gains_squares: float32 [2, 1536], P(None, ('dp', 'ctx', 'exp'))
- gains_updated: float32 [2, 1536], P(None, ('dp', 'ctx', 'exp'))
- gains_copy: bfloat16 [2, 1536], P(None, ('dp', 'ctx', 'exp'))
- expand_averaged: float32 [16, 1536, 1024], P('exp', ('dp', 'ctx'))
- expand_squares: float32 [16, 1536, 1024], P('exp', ('dp', 'ctx'))
- expand_updated: float32 [16, 1536, 1024], P('exp', ('dp', 'ctx'))
- expand_copy: bfloat16 [16, 1536, 1024], P('exp', ('dp', 'ctx'))
- shrink_averaged: float32 [16, 512, 1536], P('exp', ('dp', 'ctx'))
- shrink_squares: float32 [16, 512, 1536], P('exp', ('dp', 'ctx'))
- shrink_updated: float32 [16, 512, 1536], P('exp', ('dp', 'ctx'))
- shrink_copy: bfloat16 [16, 512, 1536], P('exp', ('dp', 'ctx'))
Inputs may be any that keep to these rules, and one draw needn't show every extreme that they name: `doc_starts`: each stream's starts rise strictly from 0; one of its documents runs from rows of the first device along ctx to rows of the last. `priority`: each device's routed rows are ranked once each.
All inputs are finite; a program needn't handle non-finite values.
Results may differ from a plain program's by a relative error of at most 0.019.
Values may be sent and summed in bfloat16 or wider, within the bound.
A program may use at most 384 MiB of HBM per device.

v0:
```python
import math

import jax
import jax.numpy as jnp
from jax import lax
from jax.sharding import PartitionSpec as P

D = 1536
HEADS = 24
KVH = 8
HD = 64
FF = 512
STEP = 10


EPSILON = 1e-05
THETA = 10000.0
BETA_ONE = 0.9
BETA_TWO = 0.95
ADAM_EPSILON = 1e-08
DECAY = 0.1
NEGATIVE = -1e30


def rms_forward(values, gain_vec):
    scale_row = lax.rsqrt(jnp.mean(values * values, axis=-1, keepdims=True) + EPSILON)
    unit_rows = values * scale_row
    return (unit_rows * gain_vec, unit_rows, scale_row)


def rms_backward(grad_rows, unit_rows, scale_row, gain_vec):
    inner = grad_rows * gain_vec
    grad_values = scale_row * (
        inner - unit_rows * jnp.mean(inner * unit_rows, axis=-1, keepdims=True)
    )
    return (grad_values, jnp.sum(grad_rows * unit_rows, axis=0))


def rotate_heads(values, positions, turn_sign):
    half_dim = values.shape[-1] // 2
    frequency = THETA ** (-jnp.arange(half_dim, dtype=jnp.float32) / half_dim)
    angles = positions.astype(jnp.float32)[:, None] * frequency[None, :]
    cosine = jnp.cos(angles)[:, None, :]
    sine_part = turn_sign * jnp.sin(angles)[:, None, :]
    lead_part = values[..., :half_dim]
    tail_part = values[..., half_dim:]
    return jnp.concatenate(
        [lead_part * cosine - tail_part * sine_part, lead_part * sine_part + tail_part * cosine],
        axis=-1,
    )


def slot_targets(route_ids, priority_row, experts, capacity):
    flat_ids = route_ids.reshape(-1)
    row_count = flat_ids.shape[0]
    ranked_rows = (
        jnp.zeros((row_count,), jnp.int32)
        .at[priority_row]
        .set(jnp.arange(row_count, dtype=jnp.int32))
    )
    ranked_ids = flat_ids[ranked_rows]
    matches = (ranked_ids[:, None] == jnp.arange(experts, dtype=jnp.int32)[None, :]).astype(
        jnp.int32
    )
    earlier = jnp.sum((jnp.cumsum(matches, axis=0) - matches) * matches, axis=1)
    slot_rank = earlier[priority_row]
    return jnp.where(slot_rank < capacity, flat_ids * capacity + slot_rank, experts * capacity)


def scores_of(queries, pairs_all, block_id, block_cols, positions, own_docs, all_docs, score_scale):
    offset = block_id * block_cols
    piece = lax.dynamic_slice_in_dim(pairs_all, offset, block_cols, 0)
    key_pos = offset + jnp.arange(block_cols, dtype=jnp.int32)
    key_docs = lax.dynamic_slice_in_dim(all_docs, offset, block_cols, 0)
    scores = (
        jnp.einsum("qgrd,kgd->grqk", queries, piece[:, 0], preferred_element_type=jnp.float32)
        * score_scale
    )
    allowed = (key_pos[None, :] <= positions[:, None]) & (key_docs[None, :] == own_docs[:, None])
    return (scores, allowed, piece)


def adam_update(master, first_mom, second_mom, grad, rate, decay):
    first_new = BETA_ONE * first_mom + (1.0 - BETA_ONE) * grad
    second_new = BETA_TWO * second_mom + (1.0 - BETA_TWO) * grad * grad
    first_hat = first_new / (1.0 - BETA_ONE**STEP)
    second_hat = second_new / (1.0 - BETA_TWO**STEP)
    master_new = master - rate * (
        first_hat / (jnp.sqrt(second_hat) + ADAM_EPSILON) + decay * master
    )
    return (first_new, second_new, master_new, master_new.astype(jnp.bfloat16))


def body(
    tokens,
    cotangent,
    doc_starts,
    routes,
    priority,
    attend_master,
    attend_mean,
    attend_square,
    outward_master,
    outward_mean,
    outward_square,
    router_master,
    router_mean,
    router_square,
    gains_master,
    gains_mean,
    gains_square,
    expand_master,
    expand_mean,
    expand_square,
    shrink_master,
    shrink_mean,
    shrink_square,
):
    local_rows = tokens[0, 0].astype(jnp.float32)
    rows_dev = local_rows.shape[0]
    model_width = local_rows.shape[1]
    ctx_count = lax.axis_size("ctx")
    ctx_place = lax.axis_index("ctx")
    stream_len = rows_dev * ctx_count
    group_size = HEADS // KVH
    experts = router_master.shape[1]
    exp_count = lax.axis_size("exp")
    local_experts = experts // exp_count
    top_count = routes.shape[-1]
    capacity = rows_dev * top_count * 9 // (8 * experts)
    score_scale = HD ** (-0.5)
    block_cols = math.gcd(stream_len, 512)
    total_blocks = stream_len // block_cols
    dense_copies = (
        attend_master.astype(jnp.bfloat16),
        outward_master.astype(jnp.bfloat16),
        router_master.astype(jnp.bfloat16),
        gains_master.astype(jnp.bfloat16),
    )
    expert_copies = (expand_master.astype(jnp.bfloat16), shrink_master.astype(jnp.bfloat16))
    attend_w, outward_w, router_w, gains_w = (
        lax.all_gather(dense_copies[0], ("dp", "ctx", "exp"), axis=0, tiled=True),
        lax.all_gather(dense_copies[1], ("dp", "ctx", "exp"), axis=1, tiled=True),
        lax.all_gather(dense_copies[2], ("dp", "ctx", "exp"), axis=0, tiled=True),
        lax.all_gather(dense_copies[3], ("dp", "ctx", "exp"), axis=1, tiled=True),
    )
    expand_w, shrink_w = (
        lax.all_gather(expert_copies[0], ("dp", "ctx"), axis=1, tiled=True),
        lax.all_gather(expert_copies[1], ("dp", "ctx"), axis=1, tiled=True),
    )
    gains_f = gains_w.astype(jnp.float32)
    positions = ctx_place * rows_dev + jnp.arange(rows_dev, dtype=jnp.int32)
    all_positions = jnp.arange(stream_len, dtype=jnp.int32)
    starts = doc_starts[0, 0]
    all_docs = jnp.sum((starts[None, :] <= all_positions[:, None]).astype(jnp.int32), axis=1) - 1
    own_docs = lax.dynamic_slice_in_dim(all_docs, ctx_place * rows_dev, rows_dev, 0)
    first_norm, first_unit, first_scale = rms_forward(local_rows, gains_f[0])
    first_low = first_norm.astype(jnp.bfloat16)
    project = jnp.dot(first_low, attend_w, preferred_element_type=jnp.float32)
    query_end = HEADS * HD
    key_end = query_end + KVH * HD
    queries = rotate_heads(project[:, :query_end].reshape(rows_dev, HEADS, HD), positions, 1.0)
    queries = queries.astype(jnp.bfloat16).reshape(rows_dev, KVH, group_size, HD)
    keys_own = rotate_heads(
        project[:, query_end:key_end].reshape(rows_dev, KVH, HD), positions, 1.0
    ).astype(jnp.bfloat16)
    values_own = project[:, key_end:].astype(jnp.bfloat16)
    pairs = jnp.concatenate([keys_own.reshape(rows_dev, KVH * HD), values_own], axis=1)
    pairs_all = lax.all_gather(pairs, "ctx", axis=0, tiled=True).reshape(stream_len, 2, KVH, HD)

    def blocks_for():
        return total_blocks

    group_q = queries
    group_rows = group_q.shape[0]
    block_count = blocks_for()

    def stats_step(block_id, carry):
        run_max, run_sum = carry
        scores, allowed, piece = scores_of(
            group_q, pairs_all, block_id, block_cols, positions, own_docs, all_docs, score_scale
        )
        masked = jnp.where(allowed, scores, NEGATIVE)
        new_max = jnp.maximum(run_max, jnp.max(masked, axis=-1))
        terms = jnp.where(allowed, jnp.exp(masked - new_max[..., None]), 0.0)
        return (new_max, run_sum * jnp.exp(run_max - new_max) + jnp.sum(terms, axis=-1))

    stats_start = (
        jnp.full((KVH, group_size, group_rows), NEGATIVE, jnp.float32),
        jnp.zeros((KVH, group_size, group_rows), jnp.float32),
    )
    run_max, run_sum = lax.fori_loop(0, block_count, stats_step, stats_start)
    log_total = run_max + jnp.log(run_sum)

    def value_step(block_id, running):
        scores, allowed, piece = scores_of(
            group_q, pairs_all, block_id, block_cols, positions, own_docs, all_docs, score_scale
        )
        probs = jnp.where(allowed, jnp.exp(scores - log_total[..., None]), 0.0).astype(jnp.bfloat16)
        return running + jnp.einsum(
            "grqk,kgd->qgrd", probs, piece[:, 1], preferred_element_type=jnp.float32
        )

    attended = lax.fori_loop(
        0, block_count, value_step, jnp.zeros((group_rows, KVH, group_size, HD), jnp.float32)
    )
    attended, log_total = (attended, log_total)
    mixed_low = attended.reshape(rows_dev, HEADS * HD).astype(jnp.bfloat16)
    branch = jnp.dot(mixed_low, outward_w, preferred_element_type=jnp.float32)
    middle = local_rows + branch
    second_norm, second_unit, second_scale = rms_forward(middle, gains_f[1])
    second_low = second_norm.astype(jnp.bfloat16)
    logits = jnp.dot(second_low, router_w, preferred_element_type=jnp.float32)
    route_ids = routes[0, 0]
    choose = (route_ids[:, :, None] == jnp.arange(experts, dtype=jnp.int32)[None, None, :]).astype(
        jnp.float32
    )
    chosen = jnp.einsum("tke,te->tk", choose, logits)
    gates = jax.nn.softmax(chosen, axis=-1)
    targets = slot_targets(route_ids, priority[0, 0, 0], experts, capacity)
    spread = jnp.repeat(second_low, top_count, axis=0)
    send_rows = (
        jnp.zeros((experts * capacity + 1, model_width), jnp.bfloat16).at[targets].set(spread)
    )
    send_rows = send_rows[: experts * capacity].reshape(
        exp_count, local_experts, capacity, model_width
    )
    received = lax.all_to_all(send_rows, "exp", split_axis=0, concat_axis=0, tiled=True)
    gate_up = jnp.einsum("nicd,idf->nicf", received, expand_w, preferred_element_type=jnp.float32)
    gate_part = gate_up[..., :FF]
    up_part = gate_up[..., FF:]
    hidden_low = (jax.nn.silu(gate_part) * up_part).astype(jnp.bfloat16)
    results_low = jnp.einsum(
        "nicf,ifd->nicd", hidden_low, shrink_w, preferred_element_type=jnp.float32
    ).astype(jnp.bfloat16)
    came_back = lax.all_to_all(results_low, "exp", split_axis=0, concat_axis=0, tiled=True).reshape(
        experts * capacity, model_width
    )
    came_back = jnp.concatenate([came_back, jnp.zeros((1, model_width), jnp.bfloat16)], axis=0)
    picked = came_back[targets].astype(jnp.float32).reshape(rows_dev, top_count, model_width)
    mixture = jnp.einsum("tk,tkd->td", gates, picked)
    output = (middle + mixture).astype(jnp.bfloat16)
    grad_out = cotangent[0, 0].astype(jnp.float32)
    grad_gates = jnp.einsum("td,tkd->tk", grad_out, picked)
    grad_results = (
        (gates[:, :, None] * grad_out[:, None, :])
        .reshape(rows_dev * top_count, model_width)
        .astype(jnp.bfloat16)
    )
    grad_slots = (
        jnp.zeros((experts * capacity + 1, model_width), jnp.bfloat16).at[targets].set(grad_results)
    )
    grad_slots = grad_slots[: experts * capacity].reshape(
        exp_count, local_experts, capacity, model_width
    )
    grad_received = lax.all_to_all(grad_slots, "exp", split_axis=0, concat_axis=0, tiled=True)
    grad_hidden = jnp.einsum(
        "nicd,ifd->nicf", grad_received, shrink_w, preferred_element_type=jnp.float32
    )
    shrink_grad = jnp.einsum(
        "nicf,nicd->ifd", hidden_low, grad_received, preferred_element_type=jnp.float32
    )
    sigma = jax.nn.sigmoid(gate_part)
    grad_gate = grad_hidden * up_part * sigma * (1.0 + gate_part * (1.0 - sigma))
    grad_up = grad_hidden * gate_part * sigma
    grad_gate_up = jnp.concatenate([grad_gate, grad_up], axis=-1).astype(jnp.bfloat16)
    expand_grad = jnp.einsum(
        "nicd,nicf->idf", received, grad_gate_up, preferred_element_type=jnp.float32
    )
    grad_rows = jnp.einsum(
        "nicf,idf->nicd", grad_gate_up, expand_w, preferred_element_type=jnp.float32
    ).astype(jnp.bfloat16)
    rows_home = lax.all_to_all(grad_rows, "exp", split_axis=0, concat_axis=0, tiled=True).reshape(
        experts * capacity, model_width
    )
    rows_home = jnp.concatenate([rows_home, jnp.zeros((1, model_width), jnp.bfloat16)], axis=0)
    row_grads = jnp.sum(
        rows_home[targets].astype(jnp.float32).reshape(rows_dev, top_count, model_width), axis=1
    )
    mean_term = jnp.sum(gates * grad_gates, axis=-1, keepdims=True)
    grad_chosen = gates * (grad_gates - mean_term)
    grad_logits = jnp.einsum("tk,tke->te", grad_chosen, choose).astype(jnp.bfloat16)
    router_grad = jnp.einsum(
        "td,te->de", second_low, grad_logits, preferred_element_type=jnp.float32
    )
    grad_second = row_grads + jnp.einsum(
        "te,de->td", grad_logits, router_w, preferred_element_type=jnp.float32
    )
    grad_middle_norm, gain_two_grad = rms_backward(
        grad_second, second_unit, second_scale, gains_f[1]
    )
    grad_middle = grad_out + grad_middle_norm
    grad_branch = grad_middle.astype(jnp.bfloat16)
    outward_grad = jnp.einsum(
        "tc,td->cd", mixed_low, grad_branch, preferred_element_type=jnp.float32
    )
    grad_mixed = jnp.einsum(
        "td,cd->tc", grad_branch, outward_w, preferred_element_type=jnp.float32
    ).astype(jnp.bfloat16)
    grad_mixed = grad_mixed.reshape(rows_dev, KVH, group_size, HD)
    key_zero = jnp.zeros((stream_len, 2, KVH, HD), jnp.float32)
    backward_group_q = queries
    group_grad = grad_mixed
    group_rows = backward_group_q.shape[0]
    block_count = blocks_for()
    delta = jnp.einsum("qgrd,qgrd->grq", group_grad.astype(jnp.float32), attended)

    def back_step(block_id, carry):
        grad_query, terms_now = carry
        scores, allowed, piece = scores_of(
            backward_group_q,
            pairs_all,
            block_id,
            block_cols,
            positions,
            own_docs,
            all_docs,
            score_scale,
        )
        probs = jnp.where(allowed, jnp.exp(scores - log_total[..., None]), 0.0)
        value_grad = jnp.einsum(
            "grqk,qgrd->kgd",
            probs.astype(jnp.bfloat16),
            group_grad,
            preferred_element_type=jnp.float32,
        )
        prob_grad = jnp.einsum(
            "qgrd,kgd->grqk", group_grad, piece[:, 1], preferred_element_type=jnp.float32
        )
        score_grad = (probs * (prob_grad - delta[..., None])).astype(jnp.bfloat16)
        grad_query = (
            grad_query
            + jnp.einsum(
                "grqk,kgd->qgrd", score_grad, piece[:, 0], preferred_element_type=jnp.float32
            )
            * score_scale
        )
        key_grad = (
            jnp.einsum(
                "grqk,qgrd->kgd", score_grad, backward_group_q, preferred_element_type=jnp.float32
            )
            * score_scale
        )
        current = lax.dynamic_slice_in_dim(terms_now, block_id * block_cols, block_cols, 0)
        terms_now = lax.dynamic_update_slice_in_dim(
            terms_now, current + jnp.stack([key_grad, value_grad], axis=1), block_id * block_cols, 0
        )
        return (grad_query, terms_now)

    back_start = (jnp.zeros((group_rows, KVH, group_size, HD), jnp.float32), key_zero)
    grad_query, key_terms = lax.fori_loop(0, block_count, back_step, back_start)
    key_sum = lax.psum_scatter(
        key_terms.reshape(stream_len, 2 * KVH * HD).astype(jnp.bfloat16),
        "ctx",
        scatter_dimension=0,
        tiled=True,
    ).astype(jnp.float32)
    key_sum = key_sum.reshape(rows_dev, 2, KVH, HD)
    grad_query_raw = rotate_heads(grad_query.reshape(rows_dev, HEADS, HD), positions, -1.0)
    grad_key_raw = rotate_heads(key_sum[:, 0], positions, -1.0)
    grad_project = jnp.concatenate(
        [
            grad_query_raw.reshape(rows_dev, HEADS * HD),
            grad_key_raw.reshape(rows_dev, KVH * HD),
            key_sum[:, 1].reshape(rows_dev, KVH * HD),
        ],
        axis=1,
    ).astype(jnp.bfloat16)
    attend_grad = jnp.einsum(
        "tc,tp->cp", first_low, grad_project, preferred_element_type=jnp.float32
    )
    grad_first = jnp.einsum("tp,cp->tc", grad_project, attend_w, preferred_element_type=jnp.float32)
    grad_input_norm, gain_one_grad = rms_backward(grad_first, first_unit, first_scale, gains_f[0])
    input_grad = grad_middle + grad_input_norm
    gains_grad = jnp.stack([gain_one_grad, gain_two_grad], axis=0)
    attend_sum, outward_sum, router_sum, gains_sum = (
        lax.psum_scatter(attend_grad, ("dp", "ctx", "exp"), scatter_dimension=0, tiled=True),
        lax.psum_scatter(outward_grad, ("dp", "ctx", "exp"), scatter_dimension=1, tiled=True),
        lax.psum_scatter(router_grad, ("dp", "ctx", "exp"), scatter_dimension=0, tiled=True),
        lax.psum_scatter(gains_grad, ("dp", "ctx", "exp"), scatter_dimension=1, tiled=True),
    )
    expand_sum, shrink_sum = (
        lax.psum_scatter(
            expand_grad.astype(jnp.bfloat16), ("dp", "ctx"), scatter_dimension=1, tiled=True
        ).astype(jnp.float32),
        lax.psum_scatter(
            shrink_grad.astype(jnp.bfloat16), ("dp", "ctx"), scatter_dimension=1, tiled=True
        ).astype(jnp.float32),
    )
    attend_new = adam_update(
        attend_master, attend_mean, attend_square, attend_sum, D ** (-0.5), DECAY
    )
    outward_new = adam_update(
        outward_master, outward_mean, outward_square, outward_sum, 4.0 * D ** (-0.5), DECAY
    )
    router_new = adam_update(
        router_master, router_mean, router_square, router_sum, 0.5 * D ** (-0.5), DECAY
    )
    gains_new = adam_update(gains_master, gains_mean, gains_square, gains_sum, 0.6, 0.0)
    expand_new = adam_update(
        expand_master, expand_mean, expand_square, expand_sum, D ** (-0.5), DECAY
    )
    shrink_new = adam_update(
        shrink_master, shrink_mean, shrink_square, shrink_sum, (FF // 32) ** (-0.5), DECAY
    )
    return (
        output[None, None],
        input_grad[None, None],
        attend_new[0],
        attend_new[1],
        attend_new[2],
        attend_new[3],
        outward_new[0],
        outward_new[1],
        outward_new[2],
        outward_new[3],
        router_new[0],
        router_new[1],
        router_new[2],
        router_new[3],
        gains_new[0],
        gains_new[1],
        gains_new[2],
        gains_new[3],
        expand_new[0],
        expand_new[1],
        expand_new[2],
        expand_new[3],
        shrink_new[0],
        shrink_new[1],
        shrink_new[2],
        shrink_new[3],
    )


def solution(mesh):
    in_specs = (
        P("dp", "exp", "ctx", None),
        P("dp", "exp", "ctx", None),
        P("dp", "exp", None),
        P("dp", "exp", "ctx", None),
        P("dp", "exp", "ctx", None),
        P(("dp", "ctx", "exp"), None),
        P(("dp", "ctx", "exp"), None),
        P(("dp", "ctx", "exp"), None),
        P(None, ("dp", "ctx", "exp")),
        P(None, ("dp", "ctx", "exp")),
        P(None, ("dp", "ctx", "exp")),
        P(("dp", "ctx", "exp"), None),
        P(("dp", "ctx", "exp"), None),
        P(("dp", "ctx", "exp"), None),
        P(None, ("dp", "ctx", "exp")),
        P(None, ("dp", "ctx", "exp")),
        P(None, ("dp", "ctx", "exp")),
        P("exp", ("dp", "ctx"), None),
        P("exp", ("dp", "ctx"), None),
        P("exp", ("dp", "ctx"), None),
        P("exp", ("dp", "ctx"), None),
        P("exp", ("dp", "ctx"), None),
        P("exp", ("dp", "ctx"), None),
    )
    out_specs = (
        P("dp", "exp", "ctx", None),
        P("dp", "exp", "ctx", None),
        P(("dp", "ctx", "exp"), None),
        P(("dp", "ctx", "exp"), None),
        P(("dp", "ctx", "exp"), None),
        P(("dp", "ctx", "exp"), None),
        P(None, ("dp", "ctx", "exp")),
        P(None, ("dp", "ctx", "exp")),
        P(None, ("dp", "ctx", "exp")),
        P(None, ("dp", "ctx", "exp")),
        P(("dp", "ctx", "exp"), None),
        P(("dp", "ctx", "exp"), None),
        P(("dp", "ctx", "exp"), None),
        P(("dp", "ctx", "exp"), None),
        P(None, ("dp", "ctx", "exp")),
        P(None, ("dp", "ctx", "exp")),
        P(None, ("dp", "ctx", "exp")),
        P(None, ("dp", "ctx", "exp")),
        P("exp", ("dp", "ctx"), None),
        P("exp", ("dp", "ctx"), None),
        P("exp", ("dp", "ctx"), None),
        P("exp", ("dp", "ctx"), None),
        P("exp", ("dp", "ctx"), None),
        P("exp", ("dp", "ctx"), None),
        P("exp", ("dp", "ctx"), None),
        P("exp", ("dp", "ctx"), None),
    )
    return jax.shard_map(body, mesh=mesh, in_specs=in_specs, out_specs=out_specs, check_vma=False)
```

profile of v0, /device:TPU:0, one launch (start us, length us, event | category | flops | bytes accessed | tf_op | source)
XLA Modules:
  0.0 2512.1 jit_solution(12774930556794045988)
XLA Ops:
  9.8 43.0 %all-gather = bf16[32,48,2]{1,2,0:T(2,128)(2,1)S(1)} all-gather(bf16[1,48,2]{1,2,0:T(2,128)(2,1)S(1)} %convert_bitcast_fusion.3), channel_id=1, replica_groups=mesh['dp'=2,'ctx'=4,'exp'=4] {'dp','ctx','exp'}, dimensions={0}, use_global_device_ids=true | all-gather | bytes 6336 | tf_op jit(solution)/shard_map/all_gather | solution.py:145
  56.3 33.2 %all-gather.8.cloned.1.call-done = bf16[1536,2560]{1,0:T(8,128)(2,1)} async-done(((bf16[48,2560]{1,0:T(8,128)(2,1)}), bf16[1536,2560]{1,0:T(8,128)(2,1)}) %all-gather.8.cloned.1.call-update) | async-done | bytes 7864336 | tf_op jit(solution)/shard_map/all_gather | solution.py:142
  109.4 15.7 scatter_custom_fusion
  125.3 23.0 gather_fusion
  154.4 23.0 gather_fusion.1
  191.8 95.7 %while.46 = (s32[]{:T(128)}, f32[8,3,512]{2,1,0:T(4,128)S(1)}, f32[8,3,512]{2,1,0:T(4,128)S(1)}, s32[2048]{0:T(1024)S(1)}, s32[512]{0:T(512)S(1)}, /*index=5*/bf...) while((s32[]{:T(128)}, f32[8,3,512]{2,1,0:T(4,128)S(1)}, ...), condition=%wide.region_5.6_spmd.clone, body=%wide.region_2.5_spmd.clone.sunk | while | flops 856486912 | bytes 53870780 | solution.py:192
  192.1 11.4 fusion.190
  203.6 11.7 select_reduce_fusion.3
  215.7 11.4 fusion.190
  227.2 12.0 select_reduce_fusion.3
  239.7 11.7 fusion.190
  251.4 12.3 select_reduce_fusion.3
  264.2 11.5 fusion.190
  275.7 11.6 select_reduce_fusion.3
  287.5 40.6 %while.47 = (s32[]{:T(128)}, f32[512,8,3,64]{0,3,2,1:T(8,128)}, bf16[2048,2,8,64]{0,3,2,1:T(8,128)(2,1)}, s32[2048]{0:T(1024)S(1)}, s32[512]{0:T(512)S(1)}, /*in...) while((s32[]{:T(128)}, f32[512,8,3,64]{0,3,2,1:T(8,128)}, ...), condition=%wide.region_7.8_spmd.clone, body=%wide.region_6.7_spmd.clone.sunk | while | flops 1638138880 | bytes 9504972 | solution.py:204
  339.1 27.6 %scatter_custom_fusion.1 = bf16[4609,1536]{1,0:T(8,128)(2,1)} fusion(s32[4096]{0:T(1024)S(1)} %bitcast.370, bf16[]{:T(256)} %constant.247.clone.1, bf16[512,1536]{1,0:T(8,128)(2,1)S(1)} %multiply_convert_fusion.1), kind=kCustom, calls=%fused_computation.82 | custom fusion | bytes 15731714 | tf_op jit(solution)/shard_map/scatter | solution.py:223
  366.7 12.8 slice.149
  387.3 41.4 %all-gather.14.cloned.1.call-done = bf16[4,1536,1024]{2,1,0:T(8,128)(2,1)} async-done(((bf16[4,192,1024]{2,1,0:T(8,128)(2,1)}), bf16[4,1536,1024]{2,1,0:T(8,128)(2,1)}) %all-gather.14.cloned.1.call-update) | async-done | bytes 12582928 | tf_op jit(solution)/shard_map/all_gather | solution.py:148
  428.7 112.5 %all-to-all-done = bf16[4,4,288,1536]{3,2,1,0:T(8,128)(2,1)} async-done(((bf16[4,4,288,1536]{3,2,1,0:T(8,128)(2,1)}), bf16[4,4,288,1536]{3,2,1,0:T(8,128)(2,1)}, u32[]{:S(2)}, u32[]{:S(2)}) %all-to-all-start) | async-done | bytes 14155808 | tf_op jit(solution)/shard_map/all_to_all | solution.py:228
  541.2 23.9 fusion.74
  575.4 14.0 convert_bitcast_fusion.1
  606.6 184.9 %all-gather.1 = bf16[32,48,16]{1,2,0:T(8,128)(2,1)S(1)} all-gather(bf16[1,48,16]{1,2,0:T(8,128)(2,1)S(1)} %convert_bitcast_fusion.2), channel_id=1, replica_groups=mesh['dp'=2,'ctx'=4,'exp'=4] {'dp','ctx','exp'}, dimensions={0}, use_global_device_ids=true | all-gather | bytes 50688 | tf_op jit(solution)/shard_map/all_gather | solution.py:144
  794.8 12.8 concatenate.43
  807.5 32.2 %gather_fusion.2 = bf16[4096,1536]{1,0:T(8,128)(2,1)} fusion(bf16[4609,1536]{1,0:T(8,128)(2,1)} %concatenate.43, s32[4096]{0:T(1024)S(1)} %broadcast_clamp_fusion), kind=kCustom, calls=%fused_computation.2 | custom fusion | bytes 25182208 | tf_op jit(solution)/shard_map/gather | solution.py:240
  849.2 28.9 %scatter_custom_fusion.2 = bf16[4609,1536]{1,0:T(8,128)(2,1)} fusion(s32[4096]{0:T(1024)S(1)} %bitcast.372, f32[512,1536]{1,0:T(8,128)S(1)} %copy-done.9, f32[4096]{0:T(1024)S(1)} %mul.648, bf16[]{:T(256)} %constant.247.clone.1), kind=kCustom, calls=%fused_computation.73 | custom fusion | flops 12582912 | bytes 17320962 | tf_op jit(solution)/shard_map/scatter | solution.py:251
  883.2 159.1 %all_to_all.20 = bf16[4,4,288,1536]{3,2,1,0:T(8,128)(2,1)} all-to-all(bf16[4,4,288,1536]{3,2,1,0:T(8,128)(2,1)S(1)} %bitcast.338), channel_id=1, replica_groups=mesh['dp'=2,'ctx'=4,'exp'=4] {'exp'}, dimensions={0} | all-to-all | bytes 28311552 | tf_op jit(solution)/shard_map/all_to_all | solution.py:256
  1042.2 20.9 fusion.68
  1063.1 22.6 convert_bitcast_fusion
  1112.2 145.7 %all-to-all-done.3 = bf16[4,4,288,1536]{3,2,1,0:T(8,128)(2,1)} async-done(((bf16[4,4,288,1536]{3,2,1,0:T(8,128)(2,1)}), bf16[4,4,288,1536]{3,2,1,0:T(8,128)(2,1)}, u32[]{:S(2)}, u32[]{:S(2)}) %all-to-all-start.3) | async-done | bytes 14155808 | tf_op jit(solution)/shard_map/all_to_all | solution.py:273
  1257.9 12.8 concatenate.45
  1270.6 32.2 %gather_fusion.3 = bf16[4096,1536]{1,0:T(8,128)(2,1)} fusion(bf16[4609,1536]{1,0:T(8,128)(2,1)} %concatenate.45, s32[4096]{0:T(1024)S(1)} %broadcast_clamp_fusion), kind=kCustom, calls=%fused_computation.3 | custom fusion | bytes 25182208 | tf_op jit(solution)/shard_map/gather | solution.py:278
  1332.2 239.2 %while.48 = (s32[]{:T(128)}, f32[512,8,3,64]{0,3,2,1:T(8,128)}, f32[2048,2,8,64]{0,3,2,1:T(8,128)}, bf16[2048,2,8,64]{0,3,2,1:T(8,128)(2,1)}, s32[2048]{0:T(1024...) while((s32[]{:T(128)}, f32[512,8,3,64]{0,3,2,1:T(8,128)}, ...), condition=%wide.region_21.22_spmd.clone, body=%wide.region_20.21_spmd.clone.sunk | while | flops 4093903872 | bytes 136741120 | solution.py:351
  1333.4 11.3 fusion.201
  1344.7 15.1 fusion.202
  1392.5 11.3 fusion.201
  1403.8 15.1 fusion.202
  1463.8 15.1 fusion.202
  1523.7 15.1 fusion.202
  1580.4 16.1 bitcast_convert_fusion.1
  1600.2 50.7 %reduce-scatter.12.cloned.1.call-done = bf16[512,1024]{0,1:T(8,128)(2,1)} async-done(((bf16[2048,1024]{0,1:T(8,128)(2,1)}), bf16[512,1024]{0,1:T(8,128)(2,1)}) %reduce-scatter.12.cloned.1.call-update) | async-done | bytes 1048592 | tf_op jit(solution)/shard_map/reduce_scatter | solution.py:352
  1671.3 24.1 bitcast_convert_fusion
  1695.7 12.3 fusion.104
  1708.0 45.4 %reduce-scatter.22.cloned.1.call-done = f32[48,16]{1,0:T(8,128)} async-done(((f32[1536,16]{1,0:T(8,128)}), f32[48,16]{1,0:T(8,128)}) %reduce-scatter.22.cloned.1.call-update) | async-done | bytes 3088
  1754.8 119.6 %reduce-scatter.20.cloned.1.call-done = bf16[4,64,1536]{2,1,0:T(8,128)(2,1)} async-done(((bf16[4,512,1536]{2,1,0:T(8,128)(2,1)}), bf16[4,64,1536]{2,1,0:T(8,128)(2,1)}) %reduce-scatter.20.cloned.1.call-update) | async-done | bytes 786448 | tf_op jit(solution)/shard_map/reduce_scatter | solution.py:386
  1883.1 92.6 %reduce-scatter.24.cloned.1.call-done = f32[48,2]{1,0:T(8,128)} async-done(((f32[1536,2]{1,0:T(8,128)}), f32[48,2]{1,0:T(8,128)}) %reduce-scatter.24.cloned.1.call-update) | async-done | bytes 400
  1977.1 140.1 %reduce-scatter.16.cloned.1.call-done = f32[1536,48]{0,1:T(8,128)} async-done(((f32[1536,1536]{0,1:T(8,128)}), f32[1536,48]{0,1:T(8,128)}) %reduce-scatter.16.cloned.1.call-update) | async-done | bytes 294928 | tf_op jit(solution)/shard_map/reduce_scatter | solution.py:378
  2119.4 207.6 %reduce-scatter.18.cloned.1.call-done = bf16[4,192,1024]{2,1,0:T(8,128)(2,1)} async-done(((bf16[4,1536,1024]{2,1,0:T(8,128)(2,1)}), bf16[4,192,1024]{2,1,0:T(8,128)(2,1)}) %reduce-scatter.18.cloned.1.call-update) | async-done | bytes 1572880 | tf_op jit(solution)/shard_map/reduce_scatter | solution.py:383
  2334.9 167.7 %reduce-scatter.14.cloned.1.call-done = f32[48,2560]{1,0:T(8,128)} async-done(((f32[1536,2560]{1,0:T(8,128)}), f32[48,2560]{1,0:T(8,128)}) %reduce-scatter.14.cloned.1.call-update) | async-done | bytes 491536 | tf_op jit(solution)/shard_map/reduce_scatter | solution.py:377
  (342 shorter events, 421.0 us)
Async XLA Ops:
  7.2 82.3 %all-gather.8.cloned.1.call-start = ((), (), s32[]{:S(2)}) async-start(), calls=%async_computation.11 | async-start | bytes 8110080 | tf_op jit(solution)/shard_map/all_gather | solution.py:142
  9.0 176.3 %all-gather.10.cloned.1.call-start = ((), (), s32[]{:S(2)}) async-start(), calls=%async_computation.12 | async-start | bytes 5242880 | tf_op jit(solution)/shard_map/all_gather | solution.py:169
  53.5 36.0 %copy-start.52 = (f32[1536]{0:T(1024)}, f32[1536]{0:T(1024)S(1)}, u32[]{:S(2)}) copy-start(f32[1536]{0:T(1024)S(1)} %get-tuple-element.634) | copy-start | bytes 18436
  55.3 34.2 %copy-start.56 = (f32[512]{0:T(512)}, f32[512]{0:T(512)S(1)}, u32[]{:S(2)}) copy-start(f32[512]{0:T(512)S(1)} %add_rsqrt_fusion.1) | copy-start | bytes 6148
  56.3 127.9 %copy-start.23 = (f32[512,32]{0,1:T(8,128)}, f32[512,32]{0,1:T(8,128)S(1)}, u32[]{:S(2)}) copy-start(f32[512,32]{0,1:T(8,128)S(1)} %get-tuple-element.739) | copy-start | bytes 196612
  105.8 225.1 %all-gather.12.cloned.1.call-start = ((), (), s32[]{:S(2)}) async-start(), calls=%async_computation.13 | async-start | bytes 4866048 | tf_op jit(solution)/shard_map/all_gather | solution.py:143
  107.6 321.1 %all-gather.14.cloned.1.call-start = ((), (), s32[]{:S(2)}) async-start(), calls=%async_computation.14 | async-start | bytes 14155776 | tf_op jit(solution)/shard_map/all_gather | solution.py:148
  328.1 8.9 copy-start
  328.1 8.9 copy-start.32
  328.1 8.9 copy-start.42
  328.1 8.9 copy-start.45
  337.1 29.6 %copy-start.48 = (f32[512]{0:T(512)}, f32[512]{0:T(512)S(1)}, u32[]{:S(2)}) copy-start(f32[512]{0:T(512)S(1)} %add_rsqrt_fusion) | copy-start | bytes 6148
  339.1 454.7 %copy-start.7 = (bf16[512,1536]{1,0:T(8,128)(2,1)}, bf16[512,1536]{1,0:T(8,128)(2,1)S(1)}, u32[]{:S(2)}) copy-start(bf16[512,1536]{1,0:T(8,128)(2,1)S(1)} %multiply_convert_fusion.1) | copy-start | bytes 4718596
  379.5 161.7 %all-to-all-start = ((bf16[4,4,288,1536]{3,2,1,0:T(8,128)(2,1)}), bf16[4,4,288,1536]{3,2,1,0:T(8,128)(2,1)}, u32[]{:S(2)}, u32[]{:S(2)}) async-start(bf16[4,4,288,1536]{3,2,1,0:T(8,128)(2,1)} %bitcast.339), calls=%async_computation | async-start | bytes 28311552 | tf_op jit(solution)/shard_map/all_to_all | solution.py:228
  386.2 189.2 %all-gather.16.cloned.1.call-start = ((), (), s32[]{:S(2)}) async-start(), calls=%async_computation.15 | async-start | bytes 7077888 | tf_op jit(solution)/shard_map/all_gather | solution.py:149
  599.9 191.8 %copy-start.16 = (bf16[1,1,512,1536]{3,2,1,0:T(8,128)(2,1)S(1)}, bf16[1,1,512,1536]{3,2,1,0:T(8,128)(2,1)}, u32[]{:S(2)}) copy-start(bf16[1,1,512,1536]{3,2,1,0:T(8,128)(2,1)} %param.30) | copy-start | bytes 4718596
  599.9 194.9 %all-to-all-start.1 = ((bf16[4,4,288,1536]{3,2,1,0:T(8,128)(2,1)}), bf16[4,4,288,1536]{3,2,1,0:T(8,128)(2,1)}, u32[]{:S(2)}, u32[]{:S(2)}) async-start(bf16[4,4,288,1536]{3,2,1,0:T(8,128)(2,1)} %copy.132), calls=%async_computation.1 | async-start | bytes 28311552 | tf_op jit(solution)/shard_map/all_to_all | solution.py:236
  794.5 13.1 copy-start.20
  839.7 8.7 copy-start.21
  839.7 9.5 copy-start.9
  1096.2 161.7 %all-to-all-start.3 = ((bf16[4,4,288,1536]{3,2,1,0:T(8,128)(2,1)}), bf16[4,4,288,1536]{3,2,1,0:T(8,128)(2,1)}, u32[]{:S(2)}, u32[]{:S(2)}) async-start(bf16[4,4,288,1536]{3,2,1,0:T(8,128)(2,1)} %copy.134), calls=%async_computation.3 | async-start | bytes 28311552 | tf_op jit(solution)/shard_map/all_to_all | solution.py:273
  1102.9 547.9 %reduce-scatter.12.cloned.1.call-start = ((), (), s32[]{:S(2)}) async-start(), calls=%async_computation.16 | async-start | bytes 5242880 | tf_op jit(solution)/shard_map/reduce_scatter | solution.py:352
  1302.9 10.7 copy-start.4
  1302.9 10.7 copy-start.27
  1302.9 10.7 copy-start.39
  1302.9 10.7 copy-start.44
  1302.9 10.7 copy-start.49
  1577.4 176.0 %reduce-scatter.22.cloned.1.call-start = ((), (), s32[]{:S(2)}) async-start(), calls=%async_computation.21 | async-start | bytes 811008
  1580.3 294.1 %reduce-scatter.20.cloned.1.call-start = ((), (), s32[]{:S(2)}) async-start(), calls=%async_computation.20 | async-start | bytes 7077888 | tf_op jit(solution)/shard_map/reduce_scatter | solution.py:386
  1596.5 379.2 %reduce-scatter.24.cloned.1.call-start = ((), (), s32[]{:S(2)}) async-start(), calls=%async_computation.22 | async-start | bytes 811008
  1600.2 52.5 %copy-start.53 = (f32[1536]{0:T(1024)S(1)}, f32[1536]{0:T(1024)}, u32[]{:S(2)}) copy-start(f32[1536]{0:T(1024)} %copy-done.52) | copy-start | bytes 18436
  1600.2 52.5 %copy-start.57 = (f32[512]{0:T(512)S(1)}, f32[512]{0:T(512)}, u32[]{:S(2)}) copy-start(f32[512]{0:T(512)} %copy-done.56) | copy-start | bytes 6148
  1652.4 10.7 copy-start.34
  1652.6 10.4 copy-start.35
  1653.0 11.7 copy-start.6
  1664.3 452.9 %reduce-scatter.16.cloned.1.call-start = ((), (), s32[]{:S(2)}) async-start(), calls=%async_computation.18 | async-start | bytes 9732096 | tf_op jit(solution)/shard_map/reduce_scatter | solution.py:378
  1671.3 655.7 %reduce-scatter.18.cloned.1.call-start = ((), (), s32[]{:S(2)}) async-start(), calls=%async_computation.19 | async-start | bytes 14155776 | tf_op jit(solution)/shard_map/reduce_scatter | solution.py:383
  1695.4 807.1 %reduce-scatter.14.cloned.1.call-start = ((), (), s32[]{:S(2)}) async-start(), calls=%async_computation.17 | async-start | bytes 16220160 | tf_op jit(solution)/shard_map/reduce_scatter | solution.py:377
  1708.0 46.2 %copy-start.51 = (f32[48,16]{0,1:T(8,128)S(1)}, f32[48,16]{0,1:T(8,128)}, u32[]{:S(2)}) copy-start(f32[48,16]{0,1:T(8,128)} %param.40) | copy-start | bytes 9220
  1708.0 46.2 %copy-start.58 = (f32[48,16]{0,1:T(8,128)S(1)}, f32[48,16]{0,1:T(8,128)}, u32[]{:S(2)}) copy-start(f32[48,16]{0,1:T(8,128)} %param.42) | copy-start | bytes 9220
  1708.0 46.2 %copy-start.59 = (f32[48,16]{0,1:T(8,128)S(1)}, f32[48,16]{0,1:T(8,128)}, u32[]{:S(2)}) copy-start(f32[48,16]{0,1:T(8,128)} %param.41) | copy-start | bytes 9220
  1880.5 95.9 %copy-start.60 = (f32[2,48]{1,0:T(2,128)S(1)}, f32[2,48]{1,0:T(2,128)}, u32[]{:S(2)}) copy-start(f32[2,48]{1,0:T(2,128)} %param.43) | copy-start | bytes 1156
  1880.5 95.9 %copy-start.61 = (f32[2,48]{1,0:T(2,128)S(1)}, f32[2,48]{1,0:T(2,128)}, u32[]{:S(2)}) copy-start(f32[2,48]{1,0:T(2,128)} %param.45) | copy-start | bytes 1156
  1880.5 95.9 %copy-start.62 = (f32[2,48]{1,0:T(2,128)S(1)}, f32[2,48]{1,0:T(2,128)}, u32[]{:S(2)}) copy-start(f32[2,48]{1,0:T(2,128)} %param.44) | copy-start | bytes 1156
  1880.6 236.6 %copy-start.26 = (f32[1536,48]{0,1:T(8,128)S(1)}, f32[1536,48]{0,1:T(8,128)}, u32[]{:S(2)}) copy-start(f32[1536,48]{0,1:T(8,128)} %param.37) | copy-start | bytes 884740
  2119.4 383.2 %copy-start.22 = (f32[48,2560]{1,0:T(8,128)S(1)}, f32[48,2560]{1,0:T(8,128)}, u32[]{:S(2)}) copy-start(f32[48,2560]{1,0:T(8,128)} %param.34) | copy-start | bytes 1474564
  2119.4 383.2 %copy-start.36 = (f32[48,2560]{1,0:T(8,128)S(1)}, f32[48,2560]{1,0:T(8,128)}, u32[]{:S(2)}) copy-start(f32[48,2560]{1,0:T(8,128)} %param.36) | copy-start | bytes 1474564
  2119.4 383.2 %copy-start.37 = (f32[48,2560]{1,0:T(8,128)S(1)}, f32[48,2560]{1,0:T(8,128)}, u32[]{:S(2)}) copy-start(f32[48,2560]{1,0:T(8,128)} %param.35) | copy-start | bytes 1474564
  (34 other events, 118.8 us)
Sparse Core Ops, SparseCore 0:
  11.5 77.9 all-gather.7
  105.9 79.3 all-gather.9
  188.8 62.0 all-gather.11
  253.4 175.2 all-gather.13
  431.3 97.2 all-gather.15
  1577.5 73.2 reduce-scatter.11
  1657.3 95.9 reduce-scatter.21
  1757.4 117.0 reduce-scatter.19
  1880.9 94.6 reduce-scatter.23
  1982.4 134.6 reduce-scatter.15
  2120.7 206.2 reduce-scatter.17
  2332.9 169.6 reduce-scatter.13
where the time goes:
time: 2520 us; the launch traced here: 2510 us
  waiting for transfers between devices  1160 us (46%)
  matrix products  494 us (20%)
  blocking collectives  387 us (15%)
  local copies, waits for them, and re-layouts  261 us (10%)
  other arithmetic  176 us (7%)
    reduce_scatter x1, waiting for transfers between devices, body(): lax.psum_scatter(expand_grad.astype(jnp.bfloat16), ('dp', 'ctx'), scatter...  208 us
    all_gather x1, blocking collectives, body(): lax.all_gather(dense_copies[2], ('dp', 'ctx', 'exp'), axis=0, tiled=True)  185 us
    reduce_scatter x1, waiting for transfers between devices, body(): lax.psum_scatter(attend_grad, ('dp', 'ctx', 'exp'), scatter_dimension=0,...  168 us
    all_to_all x1, blocking collectives, body(): lax.all_to_all(grad_slots, 'exp', split_axis=0, concat_axis=0, tiled=True)  159 us
    all_to_all x1, waiting for transfers between devices, body(): lax.all_to_all(grad_rows, 'exp', split_axis=0, concat_axis=0, tiled=True)  146 us
    reduce_scatter x1, waiting for transfers between devices, body(): lax.psum_scatter(outward_grad, ('dp', 'ctx', 'exp'), scatter_dimension=1,...  140 us
    unnamed x14, waiting for transfers between devices  138 us
    reduce_scatter x1, waiting for transfers between devices, body(): lax.psum_scatter(shrink_grad.astype(jnp.bfloat16), ('dp', 'ctx'), scatter...  120 us
  transfers between devices with their start and end apart: 15, of which 12 were waited for; matrix products, arithmetic and copies ran while one was open for 17% of the time, Pallas kernels for 0%

commit v1 on v0

v1 whole, which is shorter than its diff:
```python
import functools
import math

import jax
import jax.numpy as jnp
from jax import lax
from jax.experimental import pallas as pl
from jax.experimental.pallas import tpu as pltpu
from jax.sharding import PartitionSpec as P

D = 1536
HEADS = 24
KVH = 8
HD = 64
FF = 512
STEP = 10
GROUP = HEADS // KVH
PAIRS = KVH // 2
LANES = 2 * HD
SCALE = HD**-0.5


EPSILON = 1e-05
THETA = 10000.0
BETA_ONE = 0.9
BETA_TWO = 0.95
ADAM_EPSILON = 1e-08
DECAY = 0.1
NEGATIVE = -1e30
BF16 = jnp.bfloat16
F32 = jnp.float32
NT = (((1,), (1,)), ((), ()))


def rms_forward(values, gain_vec):
    scale_row = lax.rsqrt(jnp.mean(values * values, axis=-1, keepdims=True) + EPSILON)
    unit_rows = values * scale_row
    return (unit_rows * gain_vec, unit_rows, scale_row)


def rms_backward(grad_rows, unit_rows, scale_row, gain_vec):
    inner = grad_rows * gain_vec
    grad_values = scale_row * (
        inner - unit_rows * jnp.mean(inner * unit_rows, axis=-1, keepdims=True)
    )
    return (grad_values, jnp.sum(grad_rows * unit_rows, axis=0))


def adam_update(master, first_mom, second_mom, grad, rate, decay):
    first_new = BETA_ONE * first_mom + (1.0 - BETA_ONE) * grad
    second_new = BETA_TWO * second_mom + (1.0 - BETA_TWO) * grad * grad
    first_hat = first_new / (1.0 - BETA_ONE**STEP)
    second_hat = second_new / (1.0 - BETA_TWO**STEP)
    master_new = master - rate * (
        first_hat / (jnp.sqrt(second_hat) + ADAM_EPSILON) + decay * master
    )
    return (first_new, second_new, master_new, master_new.astype(jnp.bfloat16))


def pair_heads(block, axis):
    shape = block.shape
    split = shape[:axis] + (PAIRS, 2, GROUP, HD) + shape[axis + 1 :]
    return jnp.swapaxes(block.reshape(split), axis + 1, axis + 2).reshape(shape)


def unpair_heads(block, axis):
    shape = block.shape
    split = shape[:axis] + (PAIRS, GROUP, 2, HD) + shape[axis + 1 :]
    return jnp.swapaxes(block.reshape(split), axis + 1, axis + 2).reshape(shape)


def turn_tables(positions):
    half = HD // 2
    frequency = THETA ** (-jnp.arange(half, dtype=F32) / half)
    angles = positions.astype(F32)[:, None] * frequency[None, :]
    cosine = jnp.cos(angles)
    sine = jnp.sin(angles)
    return (
        jnp.concatenate([cosine] * 4, axis=1),
        jnp.concatenate([-sine, sine, -sine, sine], axis=1),
    )


def swap_halves(block):
    half = HD // 2
    lane = lax.broadcasted_iota(jnp.int32, block.shape, 1)
    ahead = pltpu.roll(block, LANES - half, 1)
    behind = pltpu.roll(block, half, 1)
    return jnp.where(lane % HD < half, ahead, behind)


def project_kernel(x_ref, gain_ref, w_ref, cos_ref, sin_ref, q_ref, kv_ref, h_ref):
    step = pl.program_id(0)
    query_tiles = HEADS * HD // 256
    key_tiles = KVH * HD // 256

    @pl.when(step == 0)
    def _():
        rows = x_ref[...].astype(F32)
        scale_row = lax.rsqrt(jnp.mean(rows * rows, axis=-1, keepdims=True) + EPSILON)
        h_ref[...] = (rows * scale_row * gain_ref[...]).astype(BF16)

    acc = jnp.dot(h_ref[...], w_ref[...], preferred_element_type=F32)

    def turned(half):
        part = acc[:, half * LANES : (half + 1) * LANES]
        return part * cos_ref[...] + swap_halves(part) * sin_ref[...]

    @pl.when(step < query_tiles)
    def _():
        for half in range(2):
            q_ref[:, half * LANES : (half + 1) * LANES] = (turned(half) * SCALE).astype(BF16)

    @pl.when((step >= query_tiles) & (step < query_tiles + key_tiles))
    def _():
        for half in range(2):
            kv_ref[:, half * LANES : (half + 1) * LANES] = turned(half).astype(BF16)

    @pl.when(step >= query_tiles + key_tiles)
    def _():
        kv_ref[...] = acc.astype(BF16)


def project(x, gain, weights, cosine, sine):
    rows = x.shape[0]
    query_tiles = HEADS * HD // 256
    tiles = (HEADS + 2 * KVH) * HD // 256
    return pl.pallas_call(
        project_kernel,
        grid=(tiles,),
        in_specs=[
            pl.BlockSpec((rows, D), lambda j: (0, 0)),
            pl.BlockSpec((1, D), lambda j: (0, 0)),
            pl.BlockSpec((D, 256), lambda j: (0, j)),
            pl.BlockSpec((rows, LANES), lambda j: (0, 0)),
            pl.BlockSpec((rows, LANES), lambda j: (0, 0)),
        ],
        out_specs=[
            pl.BlockSpec((rows, 256), lambda j: (0, jnp.minimum(j, query_tiles - 1))),
            pl.BlockSpec((rows, 256), lambda j: (0, jnp.maximum(j - query_tiles, 0))),
            pl.BlockSpec((rows, D), lambda j: (0, 0)),
        ],
        out_shape=[
            jax.ShapeDtypeStruct((rows, HEADS * HD), BF16),
            jax.ShapeDtypeStruct((rows, 2 * KVH * HD), BF16),
            jax.ShapeDtypeStruct((rows, D), BF16),
        ],
        compiler_params=pltpu.CompilerParams(vmem_limit_bytes=40 * 1024 * 1024),
        cost_estimate=pl.CostEstimate(
            flops=2 * rows * D * tiles * 256, bytes_accessed=D * tiles * 512, transcendentals=0
        ),
    )(x, gain, weights, cosine, sine)


def masked_pair(block):
    lane = lax.broadcasted_iota(jnp.int32, block.shape, 1)
    zero = jnp.zeros_like(block)
    return jnp.concatenate(
        [jnp.where(lane < HD, block, zero), jnp.where(lane >= HD, block, zero)], axis=0
    )


def key_loops(bounds_ref, sub, step):
    low = bounds_ref[sub, 0]
    full_low = bounds_ref[sub, 1]
    full_high = bounds_ref[sub, 2]
    high = bounds_ref[sub, 3]
    lax.fori_loop(low, full_low, functools.partial(step, True), 0)
    lax.fori_loop(full_low, full_high, functools.partial(step, False), 0)
    lax.fori_loop(full_high, high, functools.partial(step, True), 0)


def allowed_keys(block_id, key_rows, columns, place_ref):
    key_pos = block_id * key_rows + lax.broadcasted_iota(jnp.int32, (key_rows, columns), 0)
    query_pos = jnp.concatenate([place_ref[0:1, :]] * 2, axis=1)
    first_pos = jnp.concatenate([place_ref[1:2, :]] * 2, axis=1)
    return (key_pos <= query_pos) & (key_pos >= first_pos)


def attend_kernel(
    bounds_ref, place_ref, q_ref, k_ref, v_ref, o_ref, ot_ref, lse_ref, qq, vt, top, total, acc
):
    sub = pl.program_id(1)
    query_rows = q_ref.shape[0]
    columns = 2 * query_rows
    key_rows = min(256, k_ref.shape[0])

    @pl.when(sub == 0)
    def _():
        vt[...] = v_ref[...].astype(F32).T.astype(BF16)

    for r in range(GROUP):
        qq[r] = masked_pair(q_ref[:, r * LANES : (r + 1) * LANES])
    top[...] = jnp.full(top.shape, NEGATIVE, F32)
    total[...] = jnp.zeros(total.shape, F32)
    acc[...] = jnp.zeros(acc.shape, F32)

    def step(masked, block_id, carry):
        start = pl.multiple_of(block_id * key_rows, key_rows)
        keys = k_ref[pl.ds(start, key_rows), :]
        turned = vt[:, pl.ds(start, key_rows)]
        if masked:
            allowed = allowed_keys(block_id, key_rows, columns, place_ref)
        for r in range(GROUP):
            scores = lax.dot_general(keys, qq[r], NT, preferred_element_type=F32)
            if masked:
                scores = jnp.where(allowed, scores, NEGATIVE)
            before = top[r]
            now = jnp.maximum(before, jnp.max(scores, axis=0, keepdims=True))
            shrinking = jnp.exp(before - now)
            terms = jnp.exp(scores - now)
            top[r] = now
            total[r] = total[r] * shrinking + jnp.sum(terms, axis=0, keepdims=True)
            acc[r] = acc[r] * shrinking + jnp.dot(
                turned, terms.astype(BF16), preferred_element_type=F32
            )
        return carry

    key_loops(bounds_ref, sub, step)
    for r in range(GROUP):
        mixed = acc[r] / total[r]
        lse = top[r] + jnp.log(total[r])
        for i in range(2):
            lse_ref[0, 2 * r + i : 2 * r + i + 1, :] = lse[
                :, i * query_rows : (i + 1) * query_rows
            ]
        both = jnp.concatenate([mixed[:HD, :query_rows], mixed[HD:, query_rows:]], axis=0)
        ot_ref[0, r] = both
        o_ref[:, r * LANES : (r + 1) * LANES] = both.T.astype(BF16)


def attend_forward(bounds, place, q, kv):
    rows = q.shape[0]
    stream = kv.shape[0]
    sub_rows = min(256, rows)
    subs = rows // sub_rows
    columns = 2 * sub_rows
    wide = GROUP * LANES
    return pl.pallas_call(
        attend_kernel,
        grid_spec=pltpu.PrefetchScalarGridSpec(
            num_scalar_prefetch=1,
            grid=(PAIRS, subs),
            in_specs=[
                pl.BlockSpec((2, sub_rows), lambda p, s, b: (0, s)),
                pl.BlockSpec((sub_rows, wide), lambda p, s, b: (s, p)),
                pl.BlockSpec((stream, LANES), lambda p, s, b: (0, p)),
                pl.BlockSpec((stream, LANES), lambda p, s, b: (0, PAIRS + p)),
            ],
            out_specs=[
                pl.BlockSpec((sub_rows, wide), lambda p, s, b: (s, p)),
                pl.BlockSpec((1, GROUP, LANES, sub_rows), lambda p, s, b: (p, 0, 0, s)),
                pl.BlockSpec((1, 2 * GROUP, sub_rows), lambda p, s, b: (p, 0, s)),
            ],
            scratch_shapes=[
                pltpu.VMEM((GROUP, columns, LANES), BF16),
                pltpu.VMEM((LANES, stream), BF16),
                pltpu.VMEM((GROUP, 1, columns), F32),
                pltpu.VMEM((GROUP, 1, columns), F32),
                pltpu.VMEM((GROUP, LANES, columns), F32),
            ],
        ),
        out_shape=[
            jax.ShapeDtypeStruct((rows, HEADS * HD), BF16),
            jax.ShapeDtypeStruct((PAIRS, GROUP, LANES, rows), F32),
            jax.ShapeDtypeStruct((PAIRS, 2 * GROUP, rows), F32),
        ],
        compiler_params=pltpu.CompilerParams(vmem_limit_bytes=40 * 1024 * 1024),
        cost_estimate=pl.CostEstimate(
            flops=16 * rows * stream * D, bytes_accessed=2 * stream * 1024, transcendentals=0
        ),
    )(bounds, place, q, kv, kv)


def attend_back_kernel(
    bounds_ref,
    place_ref,
    q_ref,
    do_ref,
    ot_ref,
    lse_ref,
    k_ref,
    v_ref,
    cos_ref,
    sin_ref,
    own_cos_ref,
    own_sin_ref,
    dq_ref,
    dk_ref,
    dv_ref,
    qq,
    dd,
    kt,
    stats,
    acc,
    dk,
    dv,
):
    sub = pl.program_id(1)
    query_rows = q_ref.shape[0]
    columns = 2 * query_rows
    key_rows = min(256, k_ref.shape[0])

    @pl.when(sub == 0)
    def _():
        kt[...] = k_ref[...].astype(F32).T.astype(BF16)
        dk[...] = jnp.zeros(dk.shape, F32)
        dv[...] = jnp.zeros(dv.shape, F32)

    for r in range(GROUP):
        lanes = slice(r * LANES, (r + 1) * LANES)
        qq[r] = masked_pair(q_ref[:, lanes])
        dd[r] = masked_pair(do_ref[:, lanes])
        product = do_ref[:, lanes].astype(F32).T * ot_ref[0, r]
        for i in range(2):
            own = slice(i * query_rows, (i + 1) * query_rows)
            stats[r, 0:1, own] = lse_ref[0, 2 * r + i : 2 * r + i + 1, :]
            stats[r, 1:2, own] = jnp.sum(product[i * HD : (i + 1) * HD], axis=0, keepdims=True)
    acc[...] = jnp.zeros(acc.shape, F32)

    def step(masked, block_id, carry):
        start = pl.multiple_of(block_id * key_rows, key_rows)
        keys = k_ref[pl.ds(start, key_rows), :]
        values = v_ref[pl.ds(start, key_rows), :]
        turned = kt[:, pl.ds(start, key_rows)]
        key_grad = dk[pl.ds(start, key_rows), :]
        value_grad = dv[pl.ds(start, key_rows), :]
        if masked:
            allowed = allowed_keys(block_id, key_rows, columns, place_ref)
        for r in range(GROUP):
            scores = lax.dot_general(keys, qq[r], NT, preferred_element_type=F32)
            probs = jnp.exp(scores - stats[r, 0:1, :])
            if masked:
                probs = jnp.where(allowed, probs, 0.0)
            value_grad += jnp.dot(probs.astype(BF16), dd[r], preferred_element_type=F32)
            prob_grad = lax.dot_general(values, dd[r], NT, preferred_element_type=F32)
            score_grad = (probs * (prob_grad - stats[r, 1:2, :])).astype(BF16)
            key_grad += jnp.dot(score_grad, qq[r], preferred_element_type=F32)
            acc[r] += jnp.dot(turned, score_grad, preferred_element_type=F32)
        dk[pl.ds(start, key_rows), :] = key_grad
        dv[pl.ds(start, key_rows), :] = value_grad
        return carry

    key_loops(bounds_ref, sub, step)
    for r in range(GROUP):
        both = jnp.concatenate([acc[r, :HD, :query_rows], acc[r, HD:, query_rows:]], axis=0)
        grad = both.T * SCALE
        grad = grad * own_cos_ref[...] - swap_halves(grad) * own_sin_ref[...]
        dq_ref[:, r * LANES : (r + 1) * LANES] = grad.astype(BF16)

    @pl.when(sub == pl.num_programs(1) - 1)
    def _():
        dk_ref[...] = (dk[...] * cos_ref[...] - swap_halves(dk[...]) * sin_ref[...]).astype(BF16)
        dv_ref[...] = dv[...].astype(BF16)


def attend_backward(bounds, place, q, do, ot, lse, kv, tables, own_tables):
    rows = q.shape[0]
    stream = kv.shape[0]
    sub_rows = min(256, rows)
    subs = rows // sub_rows
    columns = 2 * sub_rows
    wide = GROUP * LANES
    return pl.pallas_call(
        attend_back_kernel,
        grid_spec=pltpu.PrefetchScalarGridSpec(
            num_scalar_prefetch=1,
            grid=(PAIRS, subs),
            in_specs=[
                pl.BlockSpec((2, sub_rows), lambda p, s, b: (0, s)),
                pl.BlockSpec((sub_rows, wide), lambda p, s, b: (s, p)),
                pl.BlockSpec((sub_rows, wide), lambda p, s, b: (s, p)),
                pl.BlockSpec((1, GROUP, LANES, sub_rows), lambda p, s, b: (p, 0, 0, s)),
                pl.BlockSpec((1, 2 * GROUP, sub_rows), lambda p, s, b: (p, 0, s)),
                pl.BlockSpec((stream, LANES), lambda p, s, b: (0, p)),
                pl.BlockSpec((stream, LANES), lambda p, s, b: (0, PAIRS + p)),
                pl.BlockSpec((stream, LANES), lambda p, s, b: (0, 0)),
                pl.BlockSpec((stream, LANES), lambda p, s, b: (0, 0)),
                pl.BlockSpec((sub_rows, LANES), lambda p, s, b: (s, 0)),
                pl.BlockSpec((sub_rows, LANES), lambda p, s, b: (s, 0)),
            ],
            out_specs=[
                pl.BlockSpec((sub_rows, wide), lambda p, s, b: (s, p)),
                pl.BlockSpec((stream, LANES), lambda p, s, b: (0, p)),
                pl.BlockSpec((stream, LANES), lambda p, s, b: (0, p)),
            ],
            scratch_shapes=[
                pltpu.VMEM((GROUP, columns, LANES), BF16),
                pltpu.VMEM((GROUP, columns, LANES), BF16),
                pltpu.VMEM((LANES, stream), BF16),
                pltpu.VMEM((GROUP, 2, columns), F32),
                pltpu.VMEM((GROUP, LANES, columns), F32),
                pltpu.VMEM((stream, LANES), F32),
                pltpu.VMEM((stream, LANES), F32),
            ],
        ),
        out_shape=[
            jax.ShapeDtypeStruct((rows, HEADS * HD), BF16),
            jax.ShapeDtypeStruct((stream, KVH * HD), BF16),
            jax.ShapeDtypeStruct((stream, KVH * HD), BF16),
        ],
        compiler_params=pltpu.CompilerParams(vmem_limit_bytes=40 * 1024 * 1024),
        cost_estimate=pl.CostEstimate(
            flops=40 * rows * stream * D, bytes_accessed=4 * stream * 1024, transcendentals=0
        ),
    )(bounds, place, q, do, ot, lse, kv, kv, *tables, *own_tables)


def slot_codes(route_ids, priority_row, experts, capacity):
    rows, top_count = route_ids.shape
    ranks = priority_row.reshape(rows, top_count)
    routed = route_ids[:, :, None] == jnp.arange(experts, dtype=jnp.int32)[None, None, :]
    unused = rows * top_count
    rank = jnp.min(jnp.where(routed, ranks[:, :, None], unused), axis=1).T
    earlier = jnp.sum((rank[:, None, :] < rank[:, :, None]).astype(jnp.int32), axis=2)
    return jnp.where(rank < unused, jnp.minimum(earlier, capacity) + 1, 0).T


def swap_rows(block):
    return lax.all_gather(block, "exp", axis=0, tiled=False)


def body(
    tokens,
    cotangent,
    doc_starts,
    routes,
    priority,
    attend_master,
    attend_mean,
    attend_square,
    outward_master,
    outward_mean,
    outward_square,
    router_master,
    router_mean,
    router_square,
    gains_master,
    gains_mean,
    gains_square,
    expand_master,
    expand_mean,
    expand_square,
    shrink_master,
    shrink_mean,
    shrink_square,
):
    local_low = tokens[0, 0]
    local_rows = local_low.astype(F32)
    rows_dev, width = local_rows.shape
    ctx_count = lax.axis_size("ctx")
    ctx_place = lax.axis_index("ctx")
    exp_count = lax.axis_size("exp")
    exp_place = lax.axis_index("exp")
    stream_len = rows_dev * ctx_count
    experts = router_master.shape[1]
    local_experts = experts // exp_count
    top_count = routes.shape[-1]
    capacity = rows_dev * top_count * 9 // (8 * experts)
    every = ("dp", "ctx", "exp")
    query_end = HEADS * HD
    qkv = (HEADS + 2 * KVH) * HD
    shard = attend_master.shape[0]

    attend_own = jnp.concatenate(
        [pair_heads(attend_master[:, :query_end], 1), attend_master[:, query_end:]], axis=1
    )
    rest = LANES - experts - 2
    first_own = jnp.concatenate(
        [attend_own, router_master, gains_master.T, jnp.zeros((shard, rest), F32)], axis=1
    ).astype(BF16)
    first_w = lax.all_gather(first_own, every, axis=0, tiled=True)
    attend_w = first_w[:, :qkv]
    router_w = first_w[:, qkv : qkv + experts]
    gains_f = first_w[:, qkv + experts : qkv + experts + 2].T.astype(F32)
    outward_w = lax.all_gather(
        pair_heads(outward_master, 0).T.astype(BF16), every, axis=0, tiled=True
    )
    expand_w = lax.all_gather(expand_master.astype(BF16), ("dp", "ctx"), axis=1, tiled=True)
    shrink_w = lax.all_gather(shrink_master.astype(BF16), ("dp", "ctx"), axis=1, tiled=True)

    codes = slot_codes(routes[0, 0], priority[0, 0, 0], experts, capacity)
    known = jnp.concatenate(
        [
            cotangent[0, 0],
            (codes // 256).astype(BF16),
            (codes % 256).astype(BF16),
            jnp.zeros((rows_dev, LANES - 2 * experts), BF16),
        ],
        axis=1,
    )
    known = swap_rows(known)
    grad_out_all = known[:, :, :width]
    codes_all = 256 * known[:, :, width : width + experts].astype(jnp.int32) + known[
        :, :, width + experts : width + 2 * experts
    ].astype(jnp.int32)

    positions = ctx_place * rows_dev + jnp.arange(rows_dev, dtype=jnp.int32)
    all_positions = jnp.arange(stream_len, dtype=jnp.int32)
    starts = doc_starts[0, 0]
    first_pos = jnp.max(jnp.where(starts[None, :] <= positions[:, None], starts[None, :], 0), axis=1)
    place = jnp.stack([positions, first_pos], axis=0)
    sub_rows = min(256, rows_dev)
    key_rows = min(256, stream_len)
    sub_first = positions[::sub_rows]
    sub_last = positions[sub_rows - 1 :: sub_rows]
    low = first_pos[::sub_rows] // key_rows
    high = sub_last // key_rows + 1
    full_low = jnp.clip((first_pos[sub_rows - 1 :: sub_rows] + key_rows - 1) // key_rows, low, high)
    full_high = jnp.clip((sub_first + 1) // key_rows, full_low, high)
    bounds = jnp.stack([low, full_low, full_high, high], axis=1)
    tables = turn_tables(all_positions)
    own_tables = tuple(
        lax.dynamic_slice_in_dim(table, ctx_place * rows_dev, rows_dev, 0) for table in tables
    )
    queries, pairs, first_low = project(local_low, gains_f[0:1], first_w, *own_tables)
    pairs_all = lax.all_gather(pairs, "ctx", axis=0, tiled=True)
    mixed_low, mixed_turned, log_total = attend_forward(bounds, place, queries, pairs_all)
    branch = lax.dot_general(mixed_low, outward_w, NT, preferred_element_type=F32)
    middle = local_rows + branch
    second_norm, second_unit, second_scale = rms_forward(middle, gains_f[1])
    second_low = second_norm.astype(BF16)

    second_all = swap_rows(second_low)
    logits_all = jnp.einsum("ntd,de->nte", second_all, router_w, preferred_element_type=F32)
    gates_all = jax.nn.softmax(jnp.where(codes_all > 0, logits_all, NEGATIVE), axis=-1)
    gates_all = jnp.where(codes_all > 0, gates_all, 0.0)
    first_expert = exp_place * local_experts
    own_codes = lax.dynamic_slice_in_dim(codes_all, first_expert, local_experts, 2)
    own_gates = lax.dynamic_slice_in_dim(gates_all, first_expert, local_experts, 2)
    slots = jnp.arange(1, capacity + 1, dtype=jnp.int32)
    hot = jnp.swapaxes(own_codes, 1, 2)[:, :, None, :] == slots[None, None, :, None]
    hot_low = hot.astype(BF16)
    slot_gates = jnp.sum(
        jnp.where(hot, jnp.swapaxes(own_gates, 1, 2)[:, :, None, :], 0.0), axis=-1, keepdims=True
    )
    received = jnp.einsum("nist,ntd->nisd", hot_low, second_all, preferred_element_type=F32).astype(
        BF16
    )
    gate_up = jnp.einsum("nisd,idf->nisf", received, expand_w, preferred_element_type=F32)
    gate_part = gate_up[..., :FF]
    up_part = gate_up[..., FF:]
    hidden_low = (jax.nn.silu(gate_part) * up_part).astype(BF16)
    results = jnp.einsum("nisf,ifd->nisd", hidden_low, shrink_w, preferred_element_type=F32)
    results_low = (slot_gates * results).astype(BF16)
    mixture = jnp.einsum("nist,nisd->ntd", hot_low, results_low, preferred_element_type=F32)
    mixture = lax.psum_scatter(
        mixture.astype(BF16).reshape(exp_count * rows_dev, width),
        "exp",
        scatter_dimension=0,
        tiled=True,
    )
    output = (middle + mixture.astype(F32)).astype(BF16)

    grad_received = jnp.einsum("nist,ntd->nisd", hot_low, grad_out_all, preferred_element_type=F32)
    grad_slot_gates = jnp.sum(grad_received * results, axis=-1)
    grad_results = (slot_gates * grad_received).astype(BF16)
    grad_gates = jnp.einsum(
        "nist,nis->nti", hot.astype(F32), grad_slot_gates, precision=lax.Precision.HIGHEST
    )
    grad_gates = lax.all_to_all(grad_gates, "exp", split_axis=0, concat_axis=0, tiled=True)
    grad_gates = jnp.swapaxes(grad_gates, 0, 1).reshape(rows_dev, experts)
    grad_hidden = jnp.einsum("nisd,ifd->nisf", grad_results, shrink_w, preferred_element_type=F32)
    sigma = jax.nn.sigmoid(gate_part)
    grad_gate = grad_hidden * up_part * sigma * (1.0 + gate_part * (1.0 - sigma))
    grad_up = grad_hidden * gate_part * sigma
    grad_gate_up = jnp.concatenate([grad_gate, grad_up], axis=-1).astype(BF16)
    grad_rows = jnp.einsum(
        "nisf,idf->nisd", grad_gate_up, expand_w, preferred_element_type=F32
    ).astype(BF16)
    row_grads = jnp.einsum("nist,nisd->ntd", hot_low, grad_rows, preferred_element_type=F32)
    row_grads = lax.psum_scatter(
        row_grads.astype(BF16).reshape(exp_count * rows_dev, width),
        "exp",
        scatter_dimension=0,
        tiled=True,
    ).astype(F32)
    shrink_grad = jnp.einsum(
        "nisf,nisd->ifd", hidden_low, grad_results, preferred_element_type=F32
    ).astype(BF16)
    expand_grad = jnp.einsum(
        "nisd,nisf->idf", received, grad_gate_up, preferred_element_type=F32
    ).astype(BF16)
    shrink_sum = lax.psum_scatter(shrink_grad, ("dp", "ctx"), scatter_dimension=1, tiled=True)
    expand_sum = lax.psum_scatter(expand_grad, ("dp", "ctx"), scatter_dimension=1, tiled=True)

    gates = lax.dynamic_index_in_dim(gates_all, exp_place, 0, keepdims=False)
    mean_term = jnp.sum(gates * grad_gates, axis=-1, keepdims=True)
    grad_logits = (gates * (grad_gates - mean_term)).astype(BF16)
    router_grad = jnp.einsum("td,te->de", second_low, grad_logits, preferred_element_type=F32)
    grad_second = row_grads + jnp.einsum(
        "te,de->td", grad_logits, router_w, preferred_element_type=F32
    )
    grad_middle_norm, gain_two_grad = rms_backward(
        grad_second, second_unit, second_scale, gains_f[1]
    )
    grad_middle = cotangent[0, 0].astype(F32) + grad_middle_norm
    grad_branch = grad_middle.astype(BF16)

    grad_mixed = jnp.dot(grad_branch, outward_w, preferred_element_type=F32).astype(BF16)
    grad_query, grad_keys, grad_values = attend_backward(
        bounds,
        place,
        queries,
        grad_mixed,
        mixed_turned,
        log_total,
        pairs_all,
        tables,
        own_tables,
    )
    key_sum = lax.psum_scatter(
        jnp.concatenate([grad_keys, grad_values], axis=1), "ctx", scatter_dimension=0, tiled=True
    )
    outward_grad = jnp.einsum("td,tc->dc", grad_branch, mixed_low, preferred_element_type=F32)
    outward_sum = lax.psum_scatter(outward_grad.astype(BF16), every, scatter_dimension=0, tiled=True)
    grad_project = jnp.concatenate([grad_query, key_sum], axis=1)
    attend_grad = jnp.einsum("tc,tp->cp", first_low, grad_project, preferred_element_type=F32)
    grad_first = lax.dot_general(grad_project, attend_w, NT, preferred_element_type=F32)
    first_norm, first_unit, first_scale = rms_forward(local_rows, gains_f[0])
    grad_input_norm, gain_one_grad = rms_backward(grad_first, first_unit, first_scale, gains_f[0])
    input_grad = grad_middle + grad_input_norm
    first_grad = jnp.concatenate(
        [
            attend_grad.astype(BF16),
            router_grad.astype(BF16),
            jnp.stack([gain_one_grad, gain_two_grad], axis=1).astype(BF16),
            jnp.zeros((width, rest), BF16),
        ],
        axis=1,
    )
    first_sum = lax.psum_scatter(first_grad, every, scatter_dimension=0, tiled=True).astype(F32)
    attend_sum = jnp.concatenate(
        [unpair_heads(first_sum[:, :query_end], 1), first_sum[:, query_end:qkv]], axis=1
    )
    router_sum = first_sum[:, qkv : qkv + experts]
    gains_sum = first_sum[:, qkv + experts : qkv + experts + 2].T
    outward_sum = unpair_heads(outward_sum.astype(F32).T, 0)
    expand_sum = expand_sum.astype(F32)
    shrink_sum = shrink_sum.astype(F32)
    attend_new = adam_update(
        attend_master, attend_mean, attend_square, attend_sum, D ** (-0.5), DECAY
    )
    outward_new = adam_update(
        outward_master, outward_mean, outward_square, outward_sum, 4.0 * D ** (-0.5), DECAY
    )
    router_new = adam_update(
        router_master, router_mean, router_square, router_sum, 0.5 * D ** (-0.5), DECAY
    )
    gains_new = adam_update(gains_master, gains_mean, gains_square, gains_sum, 0.6, 0.0)
    expand_new = adam_update(
        expand_master, expand_mean, expand_square, expand_sum, D ** (-0.5), DECAY
    )
    shrink_new = adam_update(
        shrink_master, shrink_mean, shrink_square, shrink_sum, (FF // 32) ** (-0.5), DECAY
    )
    return (
        output[None, None],
        input_grad[None, None],
        attend_new[0],
        attend_new[1],
        attend_new[2],
        attend_new[3],
        outward_new[0],
        outward_new[1],
        outward_new[2],
        outward_new[3],
        router_new[0],
        router_new[1],
        router_new[2],
        router_new[3],
        gains_new[0],
        gains_new[1],
        gains_new[2],
        gains_new[3],
        expand_new[0],
        expand_new[1],
        expand_new[2],
        expand_new[3],
        shrink_new[0],
        shrink_new[1],
        shrink_new[2],
        shrink_new[3],
    )


def solution(mesh):
    in_specs = (
        P("dp", "exp", "ctx", None),
        P("dp", "exp", "ctx", None),
        P("dp", "exp", None),
        P("dp", "exp", "ctx", None),
        P("dp", "exp", "ctx", None),
        P(("dp", "ctx", "exp"), None),
        P(("dp", "ctx", "exp"), None),
        P(("dp", "ctx", "exp"), None),
        P(None, ("dp", "ctx", "exp")),
        P(None, ("dp", "ctx", "exp")),
        P(None, ("dp", "ctx", "exp")),
        P(("dp", "ctx", "exp"), None),
        P(("dp", "ctx", "exp"), None),
        P(("dp", "ctx", "exp"), None),
        P(None, ("dp", "ctx", "exp")),
        P(None, ("dp", "ctx", "exp")),
        P(None, ("dp", "ctx", "exp")),
        P("exp", ("dp", "ctx"), None),
        P("exp", ("dp", "ctx"), None),
        P("exp", ("dp", "ctx"), None),
        P("exp", ("dp", "ctx"), None),
        P("exp", ("dp", "ctx"), None),
        P("exp", ("dp", "ctx"), None),
    )
    out_specs = (
        P("dp", "exp", "ctx", None),
        P("dp", "exp", "ctx", None),
        P(("dp", "ctx", "exp"), None),
        P(("dp", "ctx", "exp"), None),
        P(("dp", "ctx", "exp"), None),
        P(("dp", "ctx", "exp"), None),
        P(None, ("dp", "ctx", "exp")),
        P(None, ("dp", "ctx", "exp")),
        P(None, ("dp", "ctx", "exp")),
        P(None, ("dp", "ctx", "exp")),
        P(("dp", "ctx", "exp"), None),
        P(("dp", "ctx", "exp"), None),
        P(("dp", "ctx", "exp"), None),
        P(("dp", "ctx", "exp"), None),
        P(None, ("dp", "ctx", "exp")),
        P(None, ("dp", "ctx", "exp")),
        P(None, ("dp", "ctx", "exp")),
        P(None, ("dp", "ctx", "exp")),
        P("exp", ("dp", "ctx"), None),
        P("exp", ("dp", "ctx"), None),
        P("exp", ("dp", "ctx"), None),
        P("exp", ("dp", "ctx"), None),
        P("exp", ("dp", "ctx"), None),
        P("exp", ("dp", "ctx"), None),
        P("exp", ("dp", "ctx"), None),
        P("exp", ("dp", "ctx"), None),
    )
    return jax.shard_map(body, mesh=mesh, in_specs=in_specs, out_specs=out_specs, check_vma=False)
```

time: 2520 us -> 1580 us (0.63)
  blocking collectives: 387 us -> 0 us
  matrix products: 494 us -> 243 us
  local copies, waits for them, and re-layouts: 261 us -> 54.7 us
  other arithmetic: 176 us -> 57.8 us
  Pallas kernels: 0 us -> 63 us
  waiting for transfers between devices: 1160 us -> 1130 us
    all_gather x5 -> x7, waiting for transfers between devices: 75.1 us -> 483 us  [the longest x1 160 us: body(): lax.all_gather(expand_master.astype(BF16), ('dp', 'ctx'), axis=1, tiled=T...]
    all_to_all x3 -> x1, waiting for transfers between devices: 258 us -> 3.78 us  [body(): lax.all_to_all(grad_gates, 'exp', split_axis=0, concat_axis=0, tiled=True)]
    dot_general x45 -> x18, matrix products: 492 us -> 238 us  [the longest x1 24.3 us: body(): jnp.einsum('nisd,ifd->nisf', grad_results, shrink_w, preferred_element_ty...]
    all_gather x2 -> x0, blocking collectives: 228 us -> none  [the longest x1 185 us: body(): lax.all_gather(dense_copies[2], ('dp', 'ctx', 'exp'), axis=0, tiled=True)]
    reduce_scatter x5 -> x6, waiting for transfers between devices: 686 us -> 521 us  [the longest x1 201 us: body(): lax.psum_scatter(expand_grad, ('dp', 'ctx'), scatter_dimension=1, tiled=T...]
    all_to_all x1 -> x0, blocking collectives: 159 us -> none  [body(): lax.all_to_all(grad_slots, 'exp', split_axis=0, concat_axis=0, tiled=True)]
    gather x4 -> x0, local copies, waits for them, and re-layouts: 110 us -> none  [the longest x1 32.2 us: body(): rows_home[targets].astype(jnp.float32)]
    pallas_call x0 -> x3, Pallas kernels: none -> 63 us  [the longest x1 32 us: attend_backward(): pl.pallas_call(attend_back_kernel, grid_spec=pltpu.PrefetchScalarGridSpec...]
  transfers between devices with their start and end apart: 15 -> 15, of which waited for: 12 -> 15; matrix products, arithmetic and copies ran while one was open for 17% -> 15% of each run, Pallas kernels for 0% -> 1%
where the time goes in v1:
time: 1580 us; the launch traced here: 1570 us
  waiting for transfers between devices  1130 us (72%)
  matrix products  243 us (15%)
  Pallas kernels  63 us (4%)
  other arithmetic  57.8 us (4%)
  local copies, waits for them, and re-layouts  54.7 us (3%)
    reduce_scatter x1, waiting for transfers between devices, body(): lax.psum_scatter(expand_grad, ('dp', 'ctx'), scatter_dimension=1, tiled=T...  201 us
    all_gather x1, waiting for transfers between devices, body(): lax.all_gather(expand_master.astype(BF16), ('dp', 'ctx'), axis=1, tiled=T...  160 us
    unnamed x15, waiting for transfers between devices  127 us
    reduce_scatter x1, waiting for transfers between devices, body(): lax.psum_scatter(outward_grad.astype(BF16), every, scatter_dimension=0, t...  107 us
    reduce_scatter x1, waiting for transfers between devices, body(): lax.psum_scatter(shrink_grad, ('dp', 'ctx'), scatter_dimension=1, tiled=T...  89.9 us
    all_gather x1, waiting for transfers between devices, body(): lax.all_gather(shrink_master.astype(BF16), ('dp', 'ctx'), axis=1, tiled=T...  76.2 us
    all_gather x1, waiting for transfers between devices, body(): first_w = lax.all_gather(first_own, every, axis=0, tiled=True)  72 us
    all_gather x1, waiting for transfers between devices, body(): pairs_all = lax.all_gather(pairs, 'ctx', axis=0, tiled=True)  67.2 us
  transfers between devices with their start and end apart: 15, of which 15 were waited for; matrix products, arithmetic and copies ran while one was open for 15% of the time, Pallas kernels for 1%

profile of v1, /device:TPU:0, one launch (start us, length us, event | category | flops | bytes accessed | tf_op | source)
XLA Modules:
  0.0 1573.1 jit_solution(18381963314049768434)
XLA Ops:
  11.7 3.7 fusion.82
  19.2 72.0 %all-gather.10.cloned.1.call-done.w_ref = bf16[1536,2688]{1,0:T(8,128)(2,1)} async-done(((bf16[48,2688]{1,0:T(8,128)(2,1)}), bf16[1536,2688]{1,0:T(8,128)(2,1)}) %all-gather.10.cloned.1.call-update) | async-done | bytes 8257552 | tf_op jit(solution)/shard_map/all_gather | solution.py:472
  95.6 3.4 copy-done.10
  98.9 11.1 shard_map.422
  115.7 2.7 convert_reduce_fusion
  119.8 3.8 concatenate.33
  124.7 67.2 %all-gather.12.cloned.1.call-done.k_ref.v_ref = bf16[2048,1024]{1,0:T(8,128)(2,1)} async-done(((bf16[512,1024]{1,0:T(8,128)(2,1)}), bf16[2048,1024]{1,0:T(8,128)(2,1)}) %all-gather.12.cloned.1.call-update) | async-done | bytes 4194320 | tf_op jit(solution)/shard_map/all_gather | solution.py:517
  194.0 19.9 %shard_map.423 = (bf16[512,1536]{1,0:T(8,128)(2,1)S(1)}, f32[4,3,128,512]{3,2,1,0:T(8,128)S(1)}, f32[4,6,512]{2,1,0:T(8,128)S(1)}) custom-call(s32[2,4]{1,0:T(2,128)S(1)} %pad_add_fusion.1.bounds_ref, s32[2,512]{1,0:T(2,128)S(1)} %pad_add_fusion.place_ref, bf16[512,1536]{1,0:T(8,128)(2,1)S(1)} %copy-done.15, bf16[2048,1024]{1,0:T(8,128)(2,1)S(1)} %copy-done.11, ...), custom_call_target="tpu_custom_call" | custom-call | flops 25769803776 | bytes 4194304 | tf_op jit(solution)/shard_map/pallas_call | solution.py:239
  216.7 40.8 %all-gather.14.cloned.1.call-done = bf16[1536,1536]{1,0:T(8,128)(2,1)} async-done(((bf16[48,1536]{1,0:T(8,128)(2,1)}), bf16[1536,1536]{1,0:T(8,128)(2,1)}) %all-gather.14.cloned.1.call-update) | async-done | bytes 4718608 | tf_op jit(solution)/shard_map/all_gather | solution.py:476
  257.5 5.2 multiply_reduce_fusion.2
  265.9 3.8 convert_element_type.178
  271.3 36.5 %all-gather.20.cloned.1.call-done = bf16[2048,1664]{1,0:T(8,128)(2,1)} async-done(((bf16[512,1664]{1,0:T(8,128)(2,1)}), bf16[2048,1664]{1,0:T(8,128)(2,1)}) %all-gather.20.cloned.1.call-update) | async-done | bytes 6815760 | tf_op jit(solution)/shard_map/all_gather | solution.py:420
  309.7 16.5 %fusion.28 = f32[4,4,288,1536]{3,2,0,1:T(8,128)} fusion(bf16[4,512,1664]{2,1,0:T(8,128)(2,1)} %bitcast.186, s32[4,4,512]{2,1,0:T(4,128)S(1)} %dynamic-slice_bitcast_fusion.1, s32[288]{0:T(512)S(1)} %iota_add_fusion), kind=kOutput, calls=%fused_computation.41 | convolution fusion | flops 7250116608 | bytes 34636928 | tf_op jit(solution)/shard_map/nist,ntd->nisd/dot_general | solution.py:555
  326.2 29.9 %all-gather.22.cloned.1.call-done = bf16[2048,1536]{1,0:T(8,128)(2,1)} async-done(((bf16[512,1536]{1,0:T(8,128)(2,1)}), bf16[2048,1536]{1,0:T(8,128)(2,1)}) %all-gather.22.cloned.1.call-update) | async-done | bytes 6291472 | tf_op jit(solution)/shard_map/all_gather | solution.py:420
  356.1 4.6 divide_select_fusion
  361.9 13.0 fusion.19
  374.9 160.3 %all-gather.16.cloned.1.call-done = bf16[4,1536,1024]{2,1,0:T(8,128)(2,1)} async-done(((bf16[4,192,1024]{2,1,0:T(8,128)(2,1)}), bf16[4,1536,1024]{2,1,0:T(8,128)(2,1)}) %all-gather.16.cloned.1.call-update) | async-done | bytes 12582928 | tf_op jit(solution)/shard_map/all_gather | solution.py:479
  535.2 23.7 %fusion.34 = f32[4,4,288,1024]{3,2,0,1:T(8,128)} fusion(bf16[4,1536,1024]{2,1,0:T(8,128)(2,1)} %all-gather.16.cloned.1.call-done, bf16[4,4,288,1536]{3,2,1,0:T(8,128)(2,1)} %fusion.19), kind=kOutput, calls=%fused_computation.48 | convolution fusion | flops 14495514624 | bytes 45613056 | tf_op jit(solution)/shard_map/nisd,idf->nisf/dot_general | solution.py:540
  558.9 76.2 %all-gather.18.cloned.1.call-done = bf16[4,512,1536]{2,1,0:T(8,128)(2,1)} async-done(((bf16[4,64,1536]{2,1,0:T(8,128)(2,1)}), bf16[4,512,1536]{2,1,0:T(8,128)(2,1)}) %all-gather.18.cloned.1.call-update) | async-done | bytes 6291472 | tf_op jit(solution)/shard_map/all_gather | solution.py:480
  635.2 24.3 %fusion.25 = (bf16[4,4,288,512]{3,2,0,1:T(8,128)(2,1)}, bf16[4,4,288,512]{3,2,0,1:T(8,128)(2,1)}, bf16[4,4,288,512]{3,2,0,1:T(8,128)(2,1)}) fusion(f32[4,4,288,1024]{3,2,0,1:T(8,128)} %fusion.34, bf16[4,512,1536]{2,1,0:T(8,128)(2,1)} %all-gather.18.cloned.1.call-done, f32[4,4,288,1536]{3,2,0,1:T(8,128)} %fusion.28, f32[4,4,288]{2,0,1:T(4,128)S(1)} %copy.284), kind=kOutput, calls=%fused_computation.36 | convolution fusion | flops 7299661824 | bytes 67651584 | tf_op jit(solution)/shard_map/nisd,ifd->nisf/dot_general | solution.py:563
  659.5 22.6 %fusion.11 = bf16[4,4,288,1536]{3,2,0,1:T(8,128)(2,1)} fusion(bf16[4,1536,1024]{2,1,0:T(8,128)(2,1)} %all-gather.16.cloned.1.call-done, bf16[4,4,288,512]{3,2,0,1:T(8,128)(2,1)} %get-tuple-element.183, bf16[4,4,288,512]{3,2,0,1:T(8,128)(2,1)} %get-tuple-element.182), kind=kOutput, calls=%fused_computation.19 | convolution fusion | flops 14514388992 | bytes 36175872 | tf_op jit(solution)/shard_map/nisf,idf->nisd/dot_general | solution.py:568
  682.1 15.9 %bitcast_convert_fusion.2 = bf16[4,512,1536]{2,1,0:T(8,128)(2,1)} fusion(bf16[4,4,288,1536]{3,2,0,1:T(8,128)(2,1)} %fusion.11, s32[4,4,512]{2,1,0:T(4,128)S(1)} %dynamic-slice_bitcast_fusion.1, s32[288]{0:T(512)S(1)} %iota_add_fusion), kind=kOutput, calls=%fused_computation.17 | convolution fusion | flops 7253262336 | bytes 20481152 | tf_op jit(solution)/shard_map/nist,nisd->ntd/dot_general | solution.py:571
  698.1 22.0 %fusion.2 = (f32[4,4,288]{2,0,1:T(4,128)S(1)}, bf16[4,4,288,1536]{3,2,0,1:T(8,128)(2,1)}) fusion(f32[4,4,288,1536]{3,2,0,1:T(8,128)} %fusion.28, f32[4,4,288]{2,0,1:T(4,128)S(1)} %copy.284, bf16[4,4,288,512]{3,2,0,1:T(8,128)(2,1)} %get-tuple-element.186, bf16[4,512,1536]{2,1,0:T(8,128)(2,1)} %all-gather.18.cloned.1.call-done), kind=kOutput, calls=%fused_computation.4 | convolution fusion | flops 7276064256 | bytes 53514240 | tf_op jit(solution)/shard_map/nisf,ifd->nisd/dot_general | solution.py:544
  720.1 15.4 bitcast_convert_fusion.3
  735.5 2.8 fusion.13
  739.0 3.3 all-to-all-start
  742.7 3.8 all-to-all-done
  746.6 8.5 reduce-scatter.12.cloned.1.call-done
  755.1 5.3 multiply_reduce_fusion
  760.4 55.8 %reduce-scatter.10.cloned.1.call-done = bf16[512,1536]{1,0:T(8,128)(2,1)} async-done(((bf16[2048,1536]{1,0:T(8,128)(2,1)}), bf16[512,1536]{1,0:T(8,128)(2,1)}) %reduce-scatter.10.cloned.1.call-update) | async-done | bytes 1572880 | tf_op jit(solution)/shard_map/reduce_scatter | solution.py:547
  816.2 5.5 multiply_add_fusion
  821.8 6.1 convolution_convert_fusion.2.do_ref
  827.9 32.0 %shard_map.424 = (bf16[512,1536]{1,0:T(8,128)(2,1)S(1)}, bf16[2048,512]{1,0:T(8,128)(2,1)S(1)}, bf16[2048,512]{1,0:T(8,128)(2,1)S(1)}) custom-call(s32[2,4]{1,0:T(2,128)S(1)} %pad_add_fusion.1.bounds_ref, s32[2,512]{1,0:T(2,128)S(1)} %pad_add_fusion.place_ref, bf16[512,1536]{1,0:T(8,128)(2,1)S(1)} %copy-done.15, ...), custom_call_target="tpu_custom_call" | custom-call | flops 64424509440 | bytes 8388608 | tf_op jit(solution)/shard_map/pallas_call | solution.py:364
  859.9 2.6 pad_maximum_fusion.1
  862.8 16.5 %bitcast_convert_fusion.1 = bf16[4,512,1536]{2,1,0:T(8,128)(2,1)} fusion(bf16[4,4,288,512]{3,2,0,1:T(8,128)(2,1)} %get-tuple-element.186, f32[4,4,288,1536]{3,2,0,1:T(8,128)} %fusion.28, f32[4,4,288]{2,0,1:T(4,128)S(1)} %copy.284), kind=kOutput, calls=%fused_computation.16 | convolution fusion | flops 7265058816 | bytes 39340032 | tf_op jit(solution)/shard_map/nisf,nisd->ifd/dot_general | solution.py:578
  880.8 6.3 convolution_convert_fusion.1
  887.1 24.1 %bitcast_convert_fusion = bf16[4,1536,1024]{2,1,0:T(8,128)(2,1)} fusion(bf16[4,4,288,1536]{3,2,1,0:T(8,128)(2,1)} %fusion.19, bf16[4,4,288,512]{3,2,0,1:T(8,128)(2,1)} %get-tuple-element.183, bf16[4,4,288,512]{3,2,0,1:T(8,128)(2,1)} %get-tuple-element.182), kind=kOutput, calls=%fused_computation.6 | convolution fusion | flops 14520680448 | bytes 36175872 | tf_op jit(solution)/shard_map/nisd,nisf->idf/dot_general | solution.py:581
  918.0 58.8 %reduce-scatter.14.cloned.1.call-done = bf16[512,1024]{1,0:T(8,128)(2,1)} async-done(((bf16[2048,1024]{1,0:T(8,128)(2,1)}), bf16[512,1024]{1,0:T(8,128)(2,1)}) %reduce-scatter.14.cloned.1.call-update) | async-done | bytes 1048592 | tf_op jit(solution)/shard_map/reduce_scatter | solution.py:612
  979.0 10.2 fusion.68
  989.6 6.6 convolution_convert_fusion
  996.3 13.2 concatenate.37
  1009.5 89.9 %reduce-scatter.20.cloned.1.call-done = bf16[4,64,1536]{2,1,0:T(8,128)(2,1)} async-done(((bf16[4,512,1536]{2,1,0:T(8,128)(2,1)}), bf16[4,64,1536]{2,1,0:T(8,128)(2,1)}) %reduce-scatter.20.cloned.1.call-update) | async-done | bytes 786448 | tf_op jit(solution)/shard_map/reduce_scatter | solution.py:584
  1099.3 5.4 fusion.95
  1104.8 106.9 %reduce-scatter.16.cloned.1.call-done = bf16[48,1536]{1,0:T(8,128)(2,1)} async-done(((bf16[1536,1536]{1,0:T(8,128)(2,1)}), bf16[48,1536]{1,0:T(8,128)(2,1)}) %reduce-scatter.16.cloned.1.call-update) | async-done | bytes 147472 | tf_op jit(solution)/shard_map/reduce_scatter | solution.py:616
  1215.8 5.3 fusion.67
  1221.1 200.6 %reduce-scatter.18.cloned.1.call-done = bf16[4,192,1024]{2,1,0:T(8,128)(2,1)} async-done(((bf16[4,1536,1024]{2,1,0:T(8,128)(2,1)}), bf16[4,192,1024]{2,1,0:T(8,128)(2,1)}) %reduce-scatter.18.cloned.1.call-update) | async-done | bytes 1572880 | tf_op jit(solution)/shard_map/reduce_scatter | solution.py:585
  1421.8 7.9 fusion.98
  1429.7 127.1 %reduce-scatter.22.cloned.1.call-done = bf16[48,2688]{1,0:T(8,128)(2,1)} async-done(((bf16[1536,2688]{1,0:T(8,128)(2,1)}), bf16[48,2688]{1,0:T(8,128)(2,1)}) %reduce-scatter.22.cloned.1.call-update) | async-done | bytes 258064
  (211 shorter events, 59.1 us)
Async XLA Ops:
  7.2 84.0 %all-gather.10.cloned.1.call-start = ((), (), s32[]{:S(2)}) async-start(), calls=%async_computation.8 | async-start | bytes 8515584 | tf_op jit(solution)/shard_map/all_gather | solution.py:472
  11.6 180.2 %all-gather.12.cloned.1.call-start = ((), (), s32[]{:S(2)}) async-start(), calls=%async_computation.9 | async-start | bytes 5242880 | tf_op jit(solution)/shard_map/all_gather | solution.py:517
  17.1 78.5 %copy-start = (bf16[1,1,512,1536]{3,2,1,0:T(8,128)(2,1)S(1)}, bf16[1,1,512,1536]{3,2,1,0:T(8,128)(2,1)}, u32[]{:S(2)}) copy-start(bf16[1,1,512,1536]{3,2,1,0:T(8,128)(2,1)} %param.23) | copy-start | bytes 4718596
  18.1 91.9 %copy-start.6 = (f32[512,128]{1,0:T(8,128)}, f32[512,128]{1,0:T(8,128)S(1)}, u32[]{:S(2)}) copy-start(f32[512,128]{1,0:T(8,128)S(1)} %constant_dynamic-slice_fusion.sin_ref.own_sin_ref) | copy-start | bytes 786436
  19.2 90.8 %copy-start.8 = (f32[512,128]{1,0:T(8,128)}, f32[512,128]{1,0:T(8,128)S(1)}, u32[]{:S(2)}) copy-start(f32[512,128]{1,0:T(8,128)S(1)} %constant_dynamic-slice_fusion.1.cos_ref.own_cos_ref) | copy-start | bytes 786436
  94.2 168.5 %copy-start.33 = (f32[1536]{0:T(1024)}, f32[1536]{0:T(1024)S(1)}, u32[]{:S(2)}) copy-start(f32[1536]{0:T(1024)S(1)} %get-tuple-element.153) | copy-start | bytes 18436
  95.6 3.4 copy-start.10
  98.9 13.4 copy-start.27
  112.3 3.4 copy-start.40
  112.3 145.2 %all-gather.14.cloned.1.call-start = ((), (), s32[]{:S(2)}) async-start(), calls=%async_computation.10 | async-start | bytes 4866048 | tf_op jit(solution)/shard_map/all_gather | solution.py:476
  114.0 193.8 %all-gather.20.cloned.1.call-start = ((), (), s32[]{:S(2)}) async-start(), calls=%async_computation.19 | async-start | bytes 8519680 | tf_op jit(solution)/shard_map/all_gather | solution.py:420
  118.6 5.2 copy-start.46
  118.6 73.3 %copy-start.15 = (bf16[512,1536]{1,0:T(8,128)(2,1)S(1)}, bf16[512,1536]{1,0:T(8,128)(2,1)}, u32[]{:S(2)}) copy-start(bf16[512,1536]{1,0:T(8,128)(2,1)} %copy-done.14) | copy-start | bytes 4718596
  123.7 232.5 %all-gather.22.cloned.1.call-start = ((), (), s32[]{:S(2)}) async-start(), calls=%async_computation.20 | async-start | bytes 7864320 | tf_op jit(solution)/shard_map/all_gather | solution.py:420
  262.7 3.1 copy-start.37
  265.9 4.0 copy-start.22
  265.9 269.3 %all-gather.16.cloned.1.call-start = ((), (), s32[]{:S(2)}) async-start(), calls=%async_computation.11 | async-start | bytes 14155776 | tf_op jit(solution)/shard_map/all_gather | solution.py:479
  269.8 365.4 %all-gather.18.cloned.1.call-start = ((), (), s32[]{:S(2)}) async-start(), calls=%async_computation.12 | async-start | bytes 7077888 | tf_op jit(solution)/shard_map/all_gather | solution.py:480
  270.8 484.3 %reduce-scatter.12.cloned.1.call-start = ((), (), s32[]{:S(2)}) async-start(), calls=%async_computation.14 | async-start | bytes 7864320 | tf_op jit(solution)/shard_map/reduce_scatter | solution.py:572
  360.7 14.2 copy-start.30
  698.0 118.2 %reduce-scatter.10.cloned.1.call-start = ((), (), s32[]{:S(2)}) async-start(), calls=%async_computation.13 | async-start | bytes 7864320 | tf_op jit(solution)/shard_map/reduce_scatter | solution.py:547
  735.5 11.0 copy-start.31
  735.5 19.6 %copy-start.34 = (f32[1536]{0:T(1024)S(1)}, f32[1536]{0:T(1024)}, u32[]{:S(2)}) copy-start(f32[1536]{0:T(1024)} %copy-done.33) | copy-start | bytes 18436
  735.5 19.6 %copy-start.38 = (f32[512]{0:T(512)S(1)}, f32[512]{0:T(512)}, u32[]{:S(2)}) copy-start(f32[512]{0:T(512)} %copy-done.37) | copy-start | bytes 6148
  739.0 7.5 all-to-all-start
  742.2 234.5 %reduce-scatter.14.cloned.1.call-start = ((), (), s32[]{:S(2)}) async-start(), calls=%async_computation.15 | async-start | bytes 5242880 | tf_op jit(solution)/shard_map/reduce_scatter | solution.py:612
  746.5 69.6 %copy-start.21 = (bf16[1,1,512,1536]{3,2,1,0:T(8,128)(2,1)S(1)}, bf16[1,1,512,1536]{3,2,1,0:T(8,128)(2,1)}, u32[]{:S(2)}) copy-start(bf16[1,1,512,1536]{3,2,1,0:T(8,128)(2,1)} %param.24) | copy-start | bytes 4718596
  821.7 6.1 copy-start.20
  821.7 6.1 copy-start.3
  821.7 6.2 copy-start.5
  821.7 6.2 copy-start.7
  821.7 6.2 copy-start.9
  862.6 236.7 %reduce-scatter.20.cloned.1.call-start = ((), (), s32[]{:S(2)}) async-start(), calls=%async_computation.18 | async-start | bytes 7077888 | tf_op jit(solution)/shard_map/reduce_scatter | solution.py:584
  879.4 332.3 %reduce-scatter.16.cloned.1.call-start = ((), (), s32[]{:S(2)}) async-start(), calls=%async_computation.16 | async-start | bytes 4866048 | tf_op jit(solution)/shard_map/reduce_scatter | solution.py:616
  887.0 534.7 %reduce-scatter.18.cloned.1.call-start = ((), (), s32[]{:S(2)}) async-start(), calls=%async_computation.17 | async-start | bytes 14155776 | tf_op jit(solution)/shard_map/reduce_scatter | solution.py:585
  911.3 645.5 %reduce-scatter.22.cloned.1.call-start = ((), (), s32[]{:S(2)}) async-start(), calls=%async_computation.21 | async-start | bytes 8515584
  914.8 64.3 %copy-start.36 = (f32[1536]{0:T(1024)S(1)}, f32[1536]{0:T(1024)}, u32[]{:S(2)}) copy-start(f32[1536]{0:T(1024)} %get-tuple-element.152) | copy-start | bytes 18436
  979.0 10.5 copy-start.13
  979.0 10.5 copy-start.29
  989.5 6.7 copy-start.25
  989.5 6.7 copy-start.26
  1009.4 89.9 %copy-start.23 = (f32[4,64,1536]{2,1,0:T(8,128)S(1)}, f32[4,64,1536]{2,1,0:T(8,128)}, u32[]{:S(2)}) copy-start(f32[4,64,1536]{2,1,0:T(8,128)} %param.43) | copy-start | bytes 4718596
  1104.8 109.0 %copy-start.28 = (f32[1536,48]{0,1:T(8,128)S(1)}, f32[1536,48]{0,1:T(8,128)}, u32[]{:S(2)}) copy-start(f32[1536,48]{0,1:T(8,128)} %param.31) | copy-start | bytes 884740
  1104.8 109.0 %copy-start.32 = (f32[1536,48]{0,1:T(8,128)S(1)}, f32[1536,48]{0,1:T(8,128)}, u32[]{:S(2)}) copy-start(f32[1536,48]{0,1:T(8,128)} %param.33) | copy-start | bytes 884740
  1558.2 4.2 copy-start.43
  1558.2 4.2 copy-start.44
  1558.3 4.2 copy-start.45
  1558.3 5.4 copy-start.24
  (14 other events, 24.8 us)
Sparse Core Ops, SparseCore 0:
  11.7 79.3 all-gather.9
  112.4 79.3 all-gather.11
  195.3 62.1 all-gather.13
  259.5 48.1 all-gather.19
  309.7 46.3 all-gather.21
  358.7 176.4 all-gather.15
  537.9 97.2 all-gather.17
  698.1 56.8 reduce-scatter.11
  757.8 58.3 reduce-scatter.9
  862.7 113.9 reduce-scatter.13
  980.8 118.4 reduce-scatter.19
  1105.5 106.0 reduce-scatter.15
  1215.3 206.4 reduce-scatter.17
  1427.5 129.2 reduce-scatter.21

commit v2 on v1

--- a/solution.py
+++ b/solution.py
@@ -177,9 +177,22 @@
     return (key_pos <= query_pos) & (key_pos >= first_pos)
 
 
-def attend_kernel(
-    bounds_ref, place_ref, q_ref, k_ref, v_ref, o_ref, ot_ref, lse_ref, qq, vt, top, total, acc
-):
+def lay_keys(owner_ref, pieces, k_ref, v_ref):
+    for index, (key_piece, value_piece) in enumerate(pieces):
+        rows = key_piece.shape[0]
+        owner = owner_ref[index]
+
+        @pl.when(owner >= 0)
+        def _():
+            start = pl.multiple_of(owner * rows, rows)
+            k_ref[pl.ds(start, rows), :] = key_piece[...]
+            v_ref[pl.ds(start, rows), :] = value_piece[...]
+
+
+def attend_kernel(bounds_ref, owner_ref, place_ref, q_ref, *refs):
+    count = owner_ref.shape[0]
+    pieces = [(refs[2 * i], refs[2 * i + 1]) for i in range(count)]
+    o_ref, ot_ref, lse_ref, k_ref, v_ref, qq, vt, top, total, acc = refs[2 * count :]
     sub = pl.program_id(1)
     query_rows = q_ref.shape[0]
     columns = 2 * query_rows
@@ -187,6 +200,7 @@
 
     @pl.when(sub == 0)
     def _():
+        lay_keys(owner_ref, pieces, k_ref, v_ref)
         vt[...] = v_ref[...].astype(F32).T.astype(BF16)
 
     for r in range(GROUP):
@@ -229,9 +243,21 @@
         o_ref[:, r * LANES : (r + 1) * LANES] = both.T.astype(BF16)
 
 
-def attend_forward(bounds, place, q, kv):
+def piece_specs(pieces):
+    specs = []
+    operands = []
+    for piece in pieces:
+        rows = piece.shape[0]
+        specs.append(pl.BlockSpec((rows, LANES), lambda p, s, *_: (0, p)))
+        specs.append(pl.BlockSpec((rows, LANES), lambda p, s, *_: (0, PAIRS + p)))
+        operands += [piece, piece]
+    return (specs, operands)
+
+
+def attend_forward(bounds, owners, place, q, pieces):
     rows = q.shape[0]
-    stream = kv.shape[0]
+    stream = rows * len(pieces)
+    specs, operands = piece_specs(pieces)
     sub_rows = min(256, rows)
     subs = rows // sub_rows
     columns = 2 * sub_rows
@@ -239,20 +265,21 @@
     return pl.pallas_call(
         attend_kernel,
         grid_spec=pltpu.PrefetchScalarGridSpec(
-            num_scalar_prefetch=1,
+            num_scalar_prefetch=2,
             grid=(PAIRS, subs),
             in_specs=[
-                pl.BlockSpec((2, sub_rows), lambda p, s, b: (0, s)),
-                pl.BlockSpec((sub_rows, wide), lambda p, s, b: (s, p)),
-                pl.BlockSpec((stream, LANES), lambda p, s, b: (0, p)),
-                pl.BlockSpec((stream, LANES), lambda p, s, b: (0, PAIRS + p)),
+                pl.BlockSpec((2, sub_rows), lambda p, s, *_: (0, s)),
+                pl.BlockSpec((sub_rows, wide), lambda p, s, *_: (s, p)),
+                *specs,
             ],
             out_specs=[
-                pl.BlockSpec((sub_rows, wide), lambda p, s, b: (s, p)),
-                pl.BlockSpec((1, GROUP, LANES, sub_rows), lambda p, s, b: (p, 0, 0, s)),
-                pl.BlockSpec((1, 2 * GROUP, sub_rows), lambda p, s, b: (p, 0, s)),
+                pl.BlockSpec((sub_rows, wide), lambda p, s, *_: (s, p)),
+                pl.BlockSpec((1, GROUP, LANES, sub_rows), lambda p, s, *_: (p, 0, 0, s)),
+                pl.BlockSpec((1, 2 * GROUP, sub_rows), lambda p, s, *_: (p, 0, s)),
             ],
             scratch_shapes=[
+                pltpu.VMEM((stream, LANES), BF16),
+                pltpu.VMEM((stream, LANES), BF16),
                 pltpu.VMEM((GROUP, columns, LANES), BF16),
                 pltpu.VMEM((LANES, stream), BF16),
                 pltpu.VMEM((GROUP, 1, columns), F32),
@@ -269,33 +296,26 @@
         cost_estimate=pl.CostEstimate(
             flops=16 * rows * stream * D, bytes_accessed=2 * stream * 1024, transcendentals=0
         ),
-    )(bounds, place, q, kv, kv)
+    )(bounds, owners, place, q, *operands)
 
 
 def attend_back_kernel(
     bounds_ref,
+    owner_ref,
     place_ref,
     q_ref,
     do_ref,
     ot_ref,
     lse_ref,
-    k_ref,
-    v_ref,
     cos_ref,
     sin_ref,
     own_cos_ref,
     own_sin_ref,
-    dq_ref,
-    dk_ref,
-    dv_ref,
-    qq,
-    dd,
-    kt,
-    stats,
-    acc,
-    dk,
-    dv,
+    *refs,
 ):
+    count = owner_ref.shape[0]
+    pieces = [(refs[2 * i], refs[2 * i + 1]) for i in range(count)]
+    dq_ref, dk_ref, dv_ref, k_ref, v_ref, qq, dd, kt, stats, acc, dk, dv = refs[2 * count :]
     sub = pl.program_id(1)
     query_rows = q_ref.shape[0]
     columns = 2 * query_rows
@@ -303,6 +323,7 @@
 
     @pl.when(sub == 0)
     def _():
+        lay_keys(owner_ref, pieces, k_ref, v_ref)
         kt[...] = k_ref[...].astype(F32).T.astype(BF16)
         dk[...] = jnp.zeros(dk.shape, F32)
         dv[...] = jnp.zeros(dv.shape, F32)
@@ -354,9 +375,10 @@
         dv_ref[...] = dv[...].astype(BF16)
 
 
-def attend_backward(bounds, place, q, do, ot, lse, kv, tables, own_tables):
+def attend_backward(bounds, owners, place, q, do, ot, lse, pieces, tables, own_tables):
     rows = q.shape[0]
-    stream = kv.shape[0]
+    stream = rows * len(pieces)
+    specs, operands = piece_specs(pieces)
     sub_rows = min(256, rows)
     subs = rows // sub_rows
     columns = 2 * sub_rows
@@ -364,27 +386,28 @@
     return pl.pallas_call(
         attend_back_kernel,
         grid_spec=pltpu.PrefetchScalarGridSpec(
-            num_scalar_prefetch=1,
+            num_scalar_prefetch=2,
             grid=(PAIRS, subs),
             in_specs=[
-                pl.BlockSpec((2, sub_rows), lambda p, s, b: (0, s)),
-                pl.BlockSpec((sub_rows, wide), lambda p, s, b: (s, p)),
-                pl.BlockSpec((sub_rows, wide), lambda p, s, b: (s, p)),
-                pl.BlockSpec((1, GROUP, LANES, sub_rows), lambda p, s, b: (p, 0, 0, s)),
-                pl.BlockSpec((1, 2 * GROUP, sub_rows), lambda p, s, b: (p, 0, s)),
-                pl.BlockSpec((stream, LANES), lambda p, s, b: (0, p)),
-                pl.BlockSpec((stream, LANES), lambda p, s, b: (0, PAIRS + p)),
-                pl.BlockSpec((stream, LANES), lambda p, s, b: (0, 0)),
-                pl.BlockSpec((stream, LANES), lambda p, s, b: (0, 0)),
-                pl.BlockSpec((sub_rows, LANES), lambda p, s, b: (s, 0)),
-                pl.BlockSpec((sub_rows, LANES), lambda p, s, b: (s, 0)),
+                pl.BlockSpec((2, sub_rows), lambda p, s, *_: (0, s)),
+                pl.BlockSpec((sub_rows, wide), lambda p, s, *_: (s, p)),
+                pl.BlockSpec((sub_rows, wide), lambda p, s, *_: (s, p)),
+                pl.BlockSpec((1, GROUP, LANES, sub_rows), lambda p, s, *_: (p, 0, 0, s)),
+                pl.BlockSpec((1, 2 * GROUP, sub_rows), lambda p, s, *_: (p, 0, s)),
+                pl.BlockSpec((stream, LANES), lambda p, s, *_: (0, 0)),
+                pl.BlockSpec((stream, LANES), lambda p, s, *_: (0, 0)),
+                pl.BlockSpec((sub_rows, LANES), lambda p, s, *_: (s, 0)),
+                pl.BlockSpec((sub_rows, LANES), lambda p, s, *_: (s, 0)),
+                *specs,
             ],
             out_specs=[
-                pl.BlockSpec((sub_rows, wide), lambda p, s, b: (s, p)),
-                pl.BlockSpec((stream, LANES), lambda p, s, b: (0, p)),
-                pl.BlockSpec((stream, LANES), lambda p, s, b: (0, p)),
+                pl.BlockSpec((sub_rows, wide), lambda p, s, *_: (s, p)),
+                pl.BlockSpec((stream, LANES), lambda p, s, *_: (0, p)),
+                pl.BlockSpec((stream, LANES), lambda p, s, *_: (0, p)),
             ],
             scratch_shapes=[
+                pltpu.VMEM((stream, LANES), BF16),
+                pltpu.VMEM((stream, LANES), BF16),
                 pltpu.VMEM((GROUP, columns, LANES), BF16),
                 pltpu.VMEM((GROUP, columns, LANES), BF16),
                 pltpu.VMEM((LANES, stream), BF16),
@@ -403,7 +426,7 @@
         cost_estimate=pl.CostEstimate(
             flops=40 * rows * stream * D, bytes_accessed=4 * stream * 1024, transcendentals=0
         ),
-    )(bounds, place, q, do, ot, lse, kv, kv, *tables, *own_tables)
+    )(bounds, owners, place, q, do, ot, lse, *tables, *own_tables, *operands)
 
 
 def slot_codes(route_ids, priority_row, experts, capacity):
@@ -413,11 +436,473 @@
     unused = rows * top_count
     rank = jnp.min(jnp.where(routed, ranks[:, :, None], unused), axis=1).T
     earlier = jnp.sum((rank[:, None, :] < rank[:, :, None]).astype(jnp.int32), axis=2)
-    return jnp.where(rank < unused, jnp.minimum(earlier, capacity) + 1, 0).T
-
-
-def swap_rows(block):
-    return lax.all_gather(block, "exp", axis=0, tiled=False)
+    return jnp.where(rank < unused, jnp.where(earlier < capacity, 2, 1), 0).T
+
+
+def pack_experts(expand, shrink):
+    parts = [expand[:, :, :FF], expand[:, :, FF:]]
+    parts += [shrink[:, :, j * FF : (j + 1) * FF] for j in range(D // FF)]
+    return jnp.concatenate(parts, axis=1)
+
+
+def after(value, *others):
+    return lax.optimization_barrier((value, *others))[0]
+
+
+def split_devices():
+    return (lax.axis_size("dp"), lax.axis_size("ctx"), lax.axis_size("exp")) == (2, 4, 4)
+
+
+def greet(partners):
+    barrier = pltpu.get_barrier_semaphore()
+    for partner in partners:
+        pl.semaphore_signal(
+            barrier, inc=1, device_id=partner, device_id_type=pl.DeviceIdType.MESH
+        )
+    pl.semaphore_wait(barrier, len(partners))
+
+
+def neighbours():
+    x = lax.axis_index("dp")
+    z = lax.axis_index("ctx")
+    spot = lax.axis_index("exp")
+    y = spot // 2
+    core = spot % 2
+    other_core = {"exp": 2 * y + 1 - core}
+    other_x = {"dp": 1 - x}
+    other_y = {"exp": 2 * (1 - y) + core}
+    along = [{"ctx": lax.rem(z + d, 4)} for d in range(1, 4)]
+    return (x, y, z, core, other_core, other_x, other_y, along)
+
+
+def send_to(source, target, sems, number, device):
+    copy = pltpu.make_async_remote_copy(
+        src_ref=source,
+        dst_ref=target,
+        send_sem=sems[0].at[number],
+        recv_sem=sems[1].at[number],
+        device_id=device,
+        device_id_type=pl.DeviceIdType.MESH,
+    )
+    copy.start()
+    return copy
+
+
+def dense_gather_kernel(first_ref, second_ref, all_first, all_second, local_sem, *sems):
+    x, y, z, core, other_core, other_x, other_y, along = neighbours()
+    greet([other_core, other_x, other_y] + along)
+    spread = [
+        (
+            send_to(first_ref, all_first.at[x, z, y, core], sems, 2 * d, along[d]),
+            send_to(second_ref, all_second.at[x, z, y, core], sems, 2 * d + 1, along[d]),
+        )
+        for d in range(3)
+    ]
+    local = [
+        pltpu.make_async_copy(first_ref, all_first.at[x, z, y, core], local_sem.at[0]),
+        pltpu.make_async_copy(second_ref, all_second.at[x, z, y, core], local_sem.at[1]),
+    ]
+    for copy in local:
+        copy.start()
+    steps = [[], [], []]
+
+    def send_near(index):
+        if index == 0:
+            for copy in local:
+                copy.wait()
+        else:
+            for copy in spread[index - 1]:
+                copy.wait_recv()
+        spot = lax.rem(z - index + 4, 4)
+        base = 6 + 6 * index
+        block = all_first.at[x, spot, y, core]
+        other = all_second.at[x, spot, y, core]
+        steps[0].append(
+            (
+                send_to(block, block, sems, base, other_y),
+                send_to(other, other, sems, base + 1, other_x),
+            )
+        )
+
+    def send_far(index):
+        for copy in steps[0][index]:
+            copy.wait_recv()
+        spot = lax.rem(z - index + 4, 4)
+        base = 6 + 6 * index
+        block = all_first.at[x, spot, :, core]
+        other = all_second.at[:, spot, y, core]
+        steps[1].append(
+            (
+                send_to(block, block, sems, base + 2, other_x),
+                send_to(other, other, sems, base + 3, other_y),
+            )
+        )
+
+    def send_core(index):
+        for copy in steps[1][index]:
+            copy.wait_recv()
+        spot = lax.rem(z - index + 4, 4)
+        base = 6 + 6 * index
+        block = all_first.at[:, spot, :, core]
+        other = all_second.at[:, spot, :, core]
+        steps[2].append(
+            (
+                send_to(block, block, sems, base + 4, other_core),
+                send_to(other, other, sems, base + 5, other_core),
+            )
+        )
+
+    send_near(0)
+    send_far(0)
+    send_near(1)
+    send_core(0)
+    send_far(1)
+    send_near(2)
+    send_core(1)
+    send_far(2)
+    send_near(3)
+    send_core(2)
+    send_far(3)
+    send_core(3)
+    for pair in steps[2]:
+        for copy in pair:
+            copy.wait_recv()
+    for pair in spread + steps[0] + steps[1] + steps[2]:
+        for copy in pair:
+            copy.wait_send()
+
+
+def dense_gather(first, second):
+    if not split_devices():
+        every = ("dp", "ctx", "exp")
+        return tuple(
+            lax.all_gather(part, every, axis=0, tiled=True) for part in (first, second)
+        )
+    shapes = [(2, 4, 2, 2) + part.shape for part in (first, second)]
+    gathered = pl.pallas_call(
+        dense_gather_kernel,
+        in_specs=[pl.BlockSpec(memory_space=pl.ANY)] * 2,
+        out_specs=[pl.BlockSpec(memory_space=pl.ANY)] * 2,
+        out_shape=[jax.ShapeDtypeStruct(shape, BF16) for shape in shapes],
+        scratch_shapes=[
+            pltpu.SemaphoreType.DMA((2,)),
+            pltpu.SemaphoreType.DMA((30,)),
+            pltpu.SemaphoreType.DMA((30,)),
+        ],
+        compiler_params=pltpu.CompilerParams(collective_id=2, has_side_effects=True),
+        cost_estimate=pl.CostEstimate(
+            flops=0, bytes_accessed=64 * (first.size + second.size), transcendentals=0
+        ),
+    )(first, second)
+    return tuple(part.reshape(-1, part.shape[-1]) for part in gathered)
+
+
+def dense_sum_kernel(starts, *refs):
+    count = len(starts)
+    parts = refs[:count]
+    (
+        out_ref,
+        own,
+        got_core,
+        got_x,
+        got_y,
+        late_x,
+        late_y,
+        got_z,
+        load_sem,
+        send_sem,
+        recv_sem,
+    ) = refs[count:]
+    x, y, z, core, other_core, other_x, other_y, along = neighbours()
+    half = got_x.shape[-1]
+    greet([other_core, other_x, other_y] + along)
+    sems = (send_sem, recv_sem)
+    first = []
+    loads = []
+    for index in range(count):
+        columns = slice(starts[index], starts[index] + parts[index].shape[-1])
+        first.append(
+            send_to(
+                parts[index].at[:, :, :, 1 - core],
+                got_core.at[:, :, :, :, columns],
+                sems,
+                7 + index,
+                other_core,
+            )
+        )
+        loads.append(
+            pltpu.make_async_copy(
+                parts[index].at[:, :, :, core], own.at[:, :, :, :, columns], load_sem.at[index]
+            )
+        )
+    for copy in loads:
+        copy.start()
+    for copy in loads + first:
+        copy.wait()
+
+    def add_core(index, carry):
+        i = index // 8
+        j = (index // 2) % 4
+        k = index % 2
+        own[i, j, k] = (own[i, j, k].astype(F32) + got_core[i, j, k].astype(F32)).astype(BF16)
+        return carry
+
+    lax.fori_loop(0, 16, add_core, 0)
+    by_x = send_to(own.at[1 - x, :, :, :, :half], got_x, sems, 0, other_x)
+    by_y = send_to(own.at[:, :, 1 - y, :, half:], got_y, sems, 1, other_y)
+    by_x.wait()
+
+    def add_x(index, carry):
+        j = index // 2
+        k = index % 2
+        own[x, j, k, :, :half] = (
+            own[x, j, k, :, :half].astype(F32) + got_x[j, k].astype(F32)
+        ).astype(BF16)
+        return carry
+
+    lax.fori_loop(0, 8, add_x, 0)
+    next_y = send_to(own.at[x, :, 1 - y, :, :half], late_y, sems, 2, other_y)
+    by_y.wait()
+
+    def add_y(index, carry):
+        i = index // 4
+        j = index % 4
+        own[i, j, y, :, half:] = (
+            own[i, j, y, :, half:].astype(F32) + got_y[i, j].astype(F32)
+        ).astype(BF16)
+        return carry
+
+    lax.fori_loop(0, 8, add_y, 0)
+    next_x = send_to(own.at[1 - x, :, y, :, half:], late_x, sems, 3, other_x)
+    next_y.wait()
+    next_x.wait()
+
+    def add_late(j, carry):
+        own[x, j, y, :, :half] = (
+            own[x, j, y, :, :half].astype(F32) + late_y[j].astype(F32)
+        ).astype(BF16)
+        own[x, j, y, :, half:] = (
+            own[x, j, y, :, half:].astype(F32) + late_x[j].astype(F32)
+        ).astype(BF16)
+        return carry
+
+    lax.fori_loop(0, 4, add_late, 0)
+    last = [
+        send_to(own.at[x, lax.rem(z + d + 1, 4), y], got_z.at[d], sems, 4 + d, along[d])
+        for d in range(3)
+    ]
+    for copy in last:
+        copy.wait()
+    total = own[x, z, y].astype(F32)
+    for d in range(3):
+        total += got_z[d].astype(F32)
+    out_ref[...] = total
+
+
+def dense_sum(*parts):
+    if not split_devices():
+        every = ("dp", "ctx", "exp")
+        sums = [lax.psum_scatter(part, every, scatter_dimension=0, tiled=True) for part in parts]
+        return jnp.concatenate(sums, axis=1).astype(F32)
+    rows = parts[0].shape[0] // 32
+    starts = []
+    columns = 0
+    for part in parts:
+        starts.append(columns)
+        columns += part.shape[1]
+    half = columns // 2 // LANES * LANES
+    rest = columns - half
+    return pl.pallas_call(
+        functools.partial(dense_sum_kernel, tuple(starts)),
+        in_specs=[pl.BlockSpec(memory_space=pl.ANY)] * len(parts),
+        out_specs=pl.BlockSpec(memory_space=pltpu.VMEM),
+        out_shape=jax.ShapeDtypeStruct((rows, columns), F32),
+        scratch_shapes=[
+            pltpu.VMEM((2, 4, 2, rows, columns), BF16),
+            pltpu.VMEM((2, 4, 2, rows, columns), BF16),
+            pltpu.VMEM((4, 2, rows, half), BF16),
+            pltpu.VMEM((2, 4, rows, rest), BF16),
+            pltpu.VMEM((4, rows, rest), BF16),
+            pltpu.VMEM((4, rows, half), BF16),
+            pltpu.VMEM((3, rows, columns), BF16),
+            pltpu.SemaphoreType.DMA((len(parts),)),
+            pltpu.SemaphoreType.DMA((7 + len(parts),)),
+            pltpu.SemaphoreType.DMA((7 + len(parts),)),
+        ],
+        compiler_params=pltpu.CompilerParams(
+            collective_id=1, has_side_effects=True, vmem_limit_bytes=48 * 1024 * 1024
+        ),
+        cost_estimate=pl.CostEstimate(
+            flops=0, bytes_accessed=64 * 1536 * columns, transcendentals=0
+        ),
+    )(*[part.reshape(2, 4, 2, 2, rows, part.shape[1]) for part in parts])
+
+
+def scatter_keys(grads, rows):
+    count = lax.axis_size("ctx")
+    place = lax.axis_index("ctx")
+
+    def own(spot):
+        return lax.dynamic_slice_in_dim(grads, jnp.maximum(spot, 0) * rows, rows, 0).astype(F32)
+
+    got = jnp.zeros((rows, grads.shape[1]), F32)
+    for step in range(1, count):
+        send = (own(place - count + step) + got).astype(BF16)
+        got = lax.ppermute(
+            send, "ctx", [(i, i - 1) for i in range(count - step, count)]
+        ).astype(F32)
+    return own(place) + got
+
+
+def experts_kernel(has_before, first_ref, h_ref, do_ref, code_ref, router_ref, weights, *refs):
+    if has_before:
+        back_before, mix_before = refs[:2]
+        refs = refs[2:]
+    refs = refs[len(refs) - 7 :]
+    gh_ref, dgu_ref, back_ref, mix_ref, table, back_acc, mix_acc = refs
+    expert = pl.program_id(0)
+    chunk = pl.program_id(1)
+    tokens = h_ref.shape[0]
+    owners = weights.shape[0]
+    rows = D // owners
+    thin = FF // owners
+    own = pl.ds(pl.multiple_of(chunk * tokens, tokens), tokens)
+    lane = lax.broadcasted_iota(jnp.int32, (tokens, LANES), 1)
+    codes = code_ref[...].astype(F32)
+
+    @pl.when(expert == 0)
+    def _():
+        logits = jnp.dot(h_ref[...], router_ref[...], preferred_element_type=F32)
+        routed = codes > 0.5
+        top = jnp.max(jnp.where(routed, logits, NEGATIVE), axis=1, keepdims=True)
+        terms = jnp.where(routed, jnp.exp(jnp.where(routed, logits - top, 0.0)), 0.0)
+        shares = terms / jnp.sum(terms, axis=1, keepdims=True)
+        table[own, :] = jnp.where(codes > 1.5, shares, 0.0)
+        back_acc[own, :] = jnp.zeros((tokens, D), F32)
+        mix_acc[own, :] = jnp.zeros((tokens, D), F32)
+
+    mine = lane == first_ref[0] + expert
+    kept = jnp.sum(jnp.where(mine, codes, 0.0), axis=1, keepdims=True) > 1.5
+    gate = jnp.sum(jnp.where(mine, table[own, :], 0.0), axis=1, keepdims=True)
+    gate_w = weights[:, 0, :rows].reshape(D, FF)
+    up_w = weights[:, 0, rows : 2 * rows].reshape(D, FF)
+    thirds = [
+        weights[:, 0, 2 * rows + j * thin : 2 * rows + (j + 1) * thin].reshape(FF, FF)
+        for j in range(D // FF)
+    ]
+    hidden_rows = h_ref[...]
+    gated = jnp.dot(hidden_rows, gate_w, preferred_element_type=F32)
+    upper = jnp.dot(hidden_rows, up_w, preferred_element_type=F32)
+    grad_hidden = jnp.zeros((tokens, FF), F32)
+    for j in range(D // FF):
+        grad_hidden += lax.dot_general(
+            do_ref[:, j * FF : (j + 1) * FF], thirds[j], NT, preferred_element_type=F32
+        )
+    sigma = 1.0 / (1.0 + jnp.exp(-gated))
+    silu = gated * sigma
+    hidden = silu * upper
+    gated_hidden = (gate * hidden).astype(BF16)
+    grad_gate = jnp.sum(grad_hidden * hidden, axis=1, keepdims=True)
+    spot = lane == first_ref[0] + expert + LANES // 2
+    table[own, :] += jnp.where(spot, jnp.where(kept, grad_gate, 0.0), 0.0)
+    grad_hidden = gate * grad_hidden
+    dg = (grad_hidden * upper * (sigma * (1.0 + gated * (1.0 - sigma)))).astype(BF16)
+    du = (grad_hidden * silu).astype(BF16)
+    gh_ref[...] = gated_hidden
+    dgu_ref[:, :FF] = dg
+    dgu_ref[:, FF:] = du
+    for j in range(D // FF):
+        cols = slice(j * FF, (j + 1) * FF)
+        mix_acc[own, cols] += jnp.dot(gated_hidden, thirds[j], preferred_element_type=F32)
+        back_acc[own, cols] += lax.dot_general(
+            dg, gate_w[cols], NT, preferred_element_type=F32
+        ) + lax.dot_general(du, up_w[cols], NT, preferred_element_type=F32)
+
+    @pl.when(expert == pl.num_programs(0) - 1)
+    def _():
+        total = jnp.where(lane < LANES // 2, pltpu.roll(table[own, :], LANES // 2, 1), 0.0)
+        coarse = total.astype(BF16)
+        fine = total - coarse.astype(F32)
+        grad_gates = coarse.astype(F32) + pltpu.roll(fine, LANES // 2, 1)
+        if has_before:
+            mix_ref[...] = (mix_acc[own, :] + mix_before[...].astype(F32)).astype(BF16)
+            back_ref[:, :D] = (back_acc[own, :] + back_before[:, :D].astype(F32)).astype(BF16)
+            back_ref[:, D:] = (grad_gates + back_before[:, D:].astype(F32)).astype(BF16)
+        else:
+            mix_ref[...] = mix_acc[own, :].astype(BF16)
+            back_ref[:, :D] = back_acc[own, :].astype(BF16)
+            back_ref[:, D:] = grad_gates.astype(BF16)
+
+
+def run_experts(first, part, parts, second, known, first_w, weights, block, before, kept):
+    tokens = second.shape[0]
+    chunk = tokens // 2
+    owners, experts, depth, _ = weights.shape
+    last = experts - 1
+    once = pl.Buffered(1)
+
+    def final(e, c, *_):
+        return (jnp.where(e == last, c, 0), 0)
+
+    in_specs = [
+        pl.BlockSpec((chunk, D), lambda e, c, *_: (c, 0)),
+        pl.BlockSpec((chunk, D), lambda e, c, *_: (c, 0)),
+        pl.BlockSpec((chunk, LANES), lambda e, c, *_: (c, D // LANES)),
+        pl.BlockSpec((D, LANES), lambda e, c, *_: (0, block), pipeline_mode=once),
+    ]
+    in_specs.append(pl.BlockSpec((owners, 1, depth, FF), lambda e, c, *_: (0, e, 0, 0)))
+    operands = [first, second, known, known, first_w, weights]
+    if before:
+        in_specs += [
+            pl.BlockSpec((chunk, D + LANES), final, pipeline_mode=once),
+            pl.BlockSpec((chunk, D), final, pipeline_mode=once),
+        ]
+        operands += list(before)
+    aliases = {}
+    if kept:
+        in_specs += [pl.BlockSpec(memory_space=pl.ANY)] * 2
+        aliases = {len(operands): 0, len(operands) + 1: 1}
+        operands += list(kept)
+    return pl.pallas_call(
+        functools.partial(experts_kernel, bool(before)),
+        grid_spec=pltpu.PrefetchScalarGridSpec(
+            num_scalar_prefetch=1,
+            grid=(experts, 2),
+            in_specs=in_specs,
+            out_specs=[
+                pl.BlockSpec((chunk, FF), lambda e, c, *_: (2 * part + c, e)),
+                pl.BlockSpec((chunk, 2 * FF), lambda e, c, *_: (2 * part + c, e)),
+                pl.BlockSpec((chunk, D + LANES), final),
+                pl.BlockSpec((chunk, D), final),
+            ],
+            scratch_shapes=[
+                pltpu.VMEM((tokens, LANES), F32),
+                pltpu.VMEM((tokens, D), F32),
+                pltpu.VMEM((tokens, D), F32),
+            ],
+        ),
+        out_shape=[
+            jax.ShapeDtypeStruct((parts * tokens, experts * FF), BF16),
+            jax.ShapeDtypeStruct((parts * tokens, experts * 2 * FF), BF16),
+            jax.ShapeDtypeStruct((tokens, D + LANES), BF16),
+            jax.ShapeDtypeStruct((tokens, D), BF16),
+        ],
+        input_output_aliases=aliases,
+        compiler_params=pltpu.CompilerParams(vmem_limit_bytes=58 * 1024 * 1024),
+        cost_estimate=pl.CostEstimate(
+            flops=18 * tokens * D * FF * experts,
+            bytes_accessed=tokens * D * 16,
+            transcendentals=0,
+        ),
+    )(*operands)
+
+
+def swap_core(block):
+    return lax.ppermute(block, "exp", [(i, i ^ 1) for i in range(lax.axis_size("exp"))])
+
+
+def swap_far(block):
+    return lax.ppermute(block, "exp", [(i, i ^ 2) for i in range(lax.axis_size("exp"))])
 
 
 def body(
@@ -457,7 +942,6 @@
     local_experts = experts // exp_count
     top_count = routes.shape[-1]
     capacity = rows_dev * top_count * 9 // (8 * experts)
-    every = ("dp", "ctx", "exp")
     query_end = HEADS * HD
     qkv = (HEADS + 2 * KVH) * HD
     shard = attend_master.shape[0]
@@ -469,31 +953,29 @@
     first_own = jnp.concatenate(
         [attend_own, router_master, gains_master.T, jnp.zeros((shard, rest), F32)], axis=1
     ).astype(BF16)
-    first_w = lax.all_gather(first_own, every, axis=0, tiled=True)
+    half = local_experts // 2
+    packed = [
+        pack_experts(
+            expand_master[i : i + half].astype(BF16), shrink_master[i : i + half].astype(BF16)
+        )
+        for i in (0, half)
+    ]
+    front = lax.all_gather(packed[0], ("dp", "ctx"), axis=0, tiled=False)
+    rear = lax.all_gather(packed[1], ("dp", "ctx"), axis=0, tiled=False)
+    first_w, outward_w = dense_gather(first_own, pair_heads(outward_master, 0).T.astype(BF16))
     attend_w = first_w[:, :qkv]
     router_w = first_w[:, qkv : qkv + experts]
     gains_f = first_w[:, qkv + experts : qkv + experts + 2].T.astype(F32)
-    outward_w = lax.all_gather(
-        pair_heads(outward_master, 0).T.astype(BF16), every, axis=0, tiled=True
-    )
-    expand_w = lax.all_gather(expand_master.astype(BF16), ("dp", "ctx"), axis=1, tiled=True)
-    shrink_w = lax.all_gather(shrink_master.astype(BF16), ("dp", "ctx"), axis=1, tiled=True)
 
     codes = slot_codes(routes[0, 0], priority[0, 0, 0], experts, capacity)
     known = jnp.concatenate(
-        [
-            cotangent[0, 0],
-            (codes // 256).astype(BF16),
-            (codes % 256).astype(BF16),
-            jnp.zeros((rows_dev, LANES - 2 * experts), BF16),
-        ],
-        axis=1,
-    )
-    known = swap_rows(known)
-    grad_out_all = known[:, :, :width]
-    codes_all = 256 * known[:, :, width : width + experts].astype(jnp.int32) + known[
-        :, :, width + experts : width + 2 * experts
-    ].astype(jnp.int32)
+        [cotangent[0, 0], codes.astype(BF16), jnp.zeros((rows_dev, LANES - experts), BF16)], axis=1
+    )
+    known_core = swap_core(known)
+    known_far = swap_far(known)
+    known_last = swap_core(known_far)
+    known_near = jnp.concatenate([known, known_core], axis=0)
+    known_far = jnp.concatenate([known_far, known_last], axis=0)
 
     positions = ctx_place * rows_dev + jnp.arange(rows_dev, dtype=jnp.int32)
     all_positions = jnp.arange(stream_len, dtype=jnp.int32)
@@ -514,77 +996,84 @@
         lax.dynamic_slice_in_dim(table, ctx_place * rows_dev, rows_dev, 0) for table in tables
     )
     queries, pairs, first_low = project(local_low, gains_f[0:1], first_w, *own_tables)
-    pairs_all = lax.all_gather(pairs, "ctx", axis=0, tiled=True)
-    mixed_low, mixed_turned, log_total = attend_forward(bounds, place, queries, pairs_all)
+    key_pieces = [pairs]
+    for step in range(ctx_count - 1):
+        key_pieces.append(
+            lax.ppermute(key_pieces[-1], "ctx", [(i, i + 1) for i in range(step, ctx_count - 1)])
+        )
+    key_owners = ctx_place - jnp.arange(ctx_count, dtype=jnp.int32)
+    mixed_low, mixed_turned, log_total = attend_forward(
+        bounds, key_owners, place, queries, key_pieces
+    )
     branch = lax.dot_general(mixed_low, outward_w, NT, preferred_element_type=F32)
     middle = local_rows + branch
     second_norm, second_unit, second_scale = rms_forward(middle, gains_f[1])
     second_low = second_norm.astype(BF16)
 
-    second_all = swap_rows(second_low)
-    logits_all = jnp.einsum("ntd,de->nte", second_all, router_w, preferred_element_type=F32)
-    gates_all = jax.nn.softmax(jnp.where(codes_all > 0, logits_all, NEGATIVE), axis=-1)
-    gates_all = jnp.where(codes_all > 0, gates_all, 0.0)
-    first_expert = exp_place * local_experts
-    own_codes = lax.dynamic_slice_in_dim(codes_all, first_expert, local_experts, 2)
-    own_gates = lax.dynamic_slice_in_dim(gates_all, first_expert, local_experts, 2)
-    slots = jnp.arange(1, capacity + 1, dtype=jnp.int32)
-    hot = jnp.swapaxes(own_codes, 1, 2)[:, :, None, :] == slots[None, None, :, None]
-    hot_low = hot.astype(BF16)
-    slot_gates = jnp.sum(
-        jnp.where(hot, jnp.swapaxes(own_gates, 1, 2)[:, :, None, :], 0.0), axis=-1, keepdims=True
-    )
-    received = jnp.einsum("nist,ntd->nisd", hot_low, second_all, preferred_element_type=F32).astype(
-        BF16
-    )
-    gate_up = jnp.einsum("nisd,idf->nisf", received, expand_w, preferred_element_type=F32)
-    gate_part = gate_up[..., :FF]
-    up_part = gate_up[..., FF:]
-    hidden_low = (jax.nn.silu(gate_part) * up_part).astype(BF16)
-    results = jnp.einsum("nisf,ifd->nisd", hidden_low, shrink_w, preferred_element_type=F32)
-    results_low = (slot_gates * results).astype(BF16)
-    mixture = jnp.einsum("nist,nisd->ntd", hot_low, results_low, preferred_element_type=F32)
-    mixture = lax.psum_scatter(
-        mixture.astype(BF16).reshape(exp_count * rows_dev, width),
-        "exp",
-        scatter_dimension=0,
-        tiled=True,
-    )
-    output = (middle + mixture.astype(F32)).astype(BF16)
-
-    grad_received = jnp.einsum("nist,ntd->nisd", hot_low, grad_out_all, preferred_element_type=F32)
-    grad_slot_gates = jnp.sum(grad_received * results, axis=-1)
-    grad_results = (slot_gates * grad_received).astype(BF16)
-    grad_gates = jnp.einsum(
-        "nist,nis->nti", hot.astype(F32), grad_slot_gates, precision=lax.Precision.HIGHEST
-    )
-    grad_gates = lax.all_to_all(grad_gates, "exp", split_axis=0, concat_axis=0, tiled=True)
-    grad_gates = jnp.swapaxes(grad_gates, 0, 1).reshape(rows_dev, experts)
-    grad_hidden = jnp.einsum("nisd,ifd->nisf", grad_results, shrink_w, preferred_element_type=F32)
-    sigma = jax.nn.sigmoid(gate_part)
-    grad_gate = grad_hidden * up_part * sigma * (1.0 + gate_part * (1.0 - sigma))
-    grad_up = grad_hidden * gate_part * sigma
-    grad_gate_up = jnp.concatenate([grad_gate, grad_up], axis=-1).astype(BF16)
-    grad_rows = jnp.einsum(
-        "nisf,idf->nisd", grad_gate_up, expand_w, preferred_element_type=F32
-    ).astype(BF16)
-    row_grads = jnp.einsum("nist,nisd->ntd", hot_low, grad_rows, preferred_element_type=F32)
-    row_grads = lax.psum_scatter(
-        row_grads.astype(BF16).reshape(exp_count * rows_dev, width),
-        "exp",
-        scatter_dimension=0,
-        tiled=True,
-    ).astype(F32)
-    shrink_grad = jnp.einsum(
-        "nisf,nisd->ifd", hidden_low, grad_results, preferred_element_type=F32
-    ).astype(BF16)
-    expand_grad = jnp.einsum(
-        "nisd,nisf->idf", received, grad_gate_up, preferred_element_type=F32
-    ).astype(BF16)
-    shrink_sum = lax.psum_scatter(shrink_grad, ("dp", "ctx"), scatter_dimension=1, tiled=True)
-    expand_sum = lax.psum_scatter(expand_grad, ("dp", "ctx"), scatter_dimension=1, tiled=True)
-
-    gates = lax.dynamic_index_in_dim(gates_all, exp_place, 0, keepdims=False)
+    first_expert = jnp.reshape(exp_place * local_experts, (1,)).astype(jnp.int32)
+    second_core = swap_core(second_low)
+    second_far = swap_far(second_low)
+    second_near = jnp.concatenate([second_low, second_core], axis=0)
+    router_block = qkv // LANES
+
+    def group(index, part, second, known, weights, before, kept):
+        first = first_expert + index * half
+        return run_experts(
+            first, part, 2, second, known, first_w, weights, router_block, before, kept
+        )
+
+    def weight_grads(hidden, grad):
+        contract = (((0,), (0,)), ((), ()))
+        wide = lax.dot_general(second_all, grad, contract, preferred_element_type=F32)
+        thin = lax.dot_general(hidden, grad_out_all, contract, preferred_element_type=F32)
+        return (wide.astype(BF16), thin.astype(BF16).reshape(half, FF, width))
+
+    def scatter(wide, thin):
+        inner = ("dp", "ctx")
+        wide = lax.psum_scatter(wide, inner, scatter_dimension=0, tiled=True)
+        thin = lax.psum_scatter(thin, inner, scatter_dimension=1, tiled=True)
+        wide = jnp.swapaxes(wide.reshape(-1, half, 2 * FF), 0, 1)
+        return (wide.astype(F32), thin.astype(F32))
+
+    *kept, back_near, mix_near = group(0, 0, second_near, known_near, front, (), ())
+    second_last = swap_core(second_far)
+    second_far = jnp.concatenate([second_far, second_last], axis=0)
+    second_far = after(second_far, back_near)
+    second_all = jnp.concatenate([second_near, second_far], axis=0)
+    grad_out_all = jnp.concatenate([known_near[:, :width], known_far[:, :width]], axis=0)
+    hidden, grad, back_far, mix_far = group(0, 1, second_far, known_far, front, (), kept)
+    front_grads = weight_grads(hidden, grad)
+    front_sums = scatter(*front_grads)
+    second_far = after(second_far, *front_grads)
+    *kept, back_far, mix_far = group(
+        1, 1, second_far, known_far, rear, (back_far, mix_far), ()
+    )
+    across = back_far[:rows_dev].astype(F32) + swap_core(back_far[rows_dev:]).astype(F32)
+    across = swap_far(across.astype(BF16))
+    second_near = after(second_near, back_far)
+    hidden, grad, back_near, mix_near = group(
+        1, 0, second_near, known_near, rear, (back_near, mix_near), kept
+    )
+    row_grads = (
+        back_near[:rows_dev].astype(F32)
+        + swap_core(back_near[rows_dev:]).astype(F32)
+        + across.astype(F32)
+    )
+    grad_gates = (
+        row_grads[:, width : width + experts]
+        + row_grads[:, width + LANES // 2 : width + LANES // 2 + experts]
+    )
+    rear_grads = weight_grads(hidden, after(grad, back_near))
+    rear_sums = scatter(*rear_grads)
+    mix_near, mix_far, row_grads = lax.optimization_barrier((mix_near, mix_far, row_grads))
+    mix_core = swap_core(mix_near[rows_dev:])
+    mixture = mix_far[:rows_dev].astype(F32) + swap_core(mix_far[rows_dev:]).astype(F32)
+    mixture = swap_far(mixture.astype(BF16))
+    row_grads = row_grads[:, :width]
+
+    logits = jnp.dot(second_low, router_w, preferred_element_type=F32)
+    gates = jax.nn.softmax(jnp.where(codes > 0, logits, NEGATIVE), axis=-1)
+    gates = jnp.where(codes > 0, gates, 0.0)
     mean_term = jnp.sum(gates * grad_gates, axis=-1, keepdims=True)
     grad_logits = (gates * (grad_gates - mean_term)).astype(BF16)
     router_grad = jnp.einsum("td,te->de", second_low, grad_logits, preferred_element_type=F32)
@@ -600,44 +1089,48 @@
     grad_mixed = jnp.dot(grad_branch, outward_w, preferred_element_type=F32).astype(BF16)
     grad_query, grad_keys, grad_values = attend_backward(
         bounds,
+        key_owners,
         place,
         queries,
         grad_mixed,
         mixed_turned,
         log_total,
-        pairs_all,
+        key_pieces,
         tables,
         own_tables,
     )
-    key_sum = lax.psum_scatter(
-        jnp.concatenate([grad_keys, grad_values], axis=1), "ctx", scatter_dimension=0, tiled=True
-    )
+    grad_pairs = jnp.concatenate([grad_keys, grad_values], axis=1)
+    key_sum = scatter_keys(grad_pairs, rows_dev).astype(BF16)
+    mixture, mix_core = lax.optimization_barrier((mixture, mix_core, key_sum))[:2]
+    mixture = mixture.astype(F32) + mix_core.astype(F32) + mix_near[:rows_dev].astype(F32)
+    output = (middle + mixture).astype(BF16)
     outward_grad = jnp.einsum("td,tc->dc", grad_branch, mixed_low, preferred_element_type=F32)
-    outward_sum = lax.psum_scatter(outward_grad.astype(BF16), every, scatter_dimension=0, tiled=True)
     grad_project = jnp.concatenate([grad_query, key_sum], axis=1)
     attend_grad = jnp.einsum("tc,tp->cp", first_low, grad_project, preferred_element_type=F32)
     grad_first = lax.dot_general(grad_project, attend_w, NT, preferred_element_type=F32)
     first_norm, first_unit, first_scale = rms_forward(local_rows, gains_f[0])
     grad_input_norm, gain_one_grad = rms_backward(grad_first, first_unit, first_scale, gains_f[0])
     input_grad = grad_middle + grad_input_norm
-    first_grad = jnp.concatenate(
+    thin_grad = jnp.concatenate(
         [
-            attend_grad.astype(BF16),
             router_grad.astype(BF16),
             jnp.stack([gain_one_grad, gain_two_grad], axis=1).astype(BF16),
             jnp.zeros((width, rest), BF16),
         ],
         axis=1,
     )
-    first_sum = lax.psum_scatter(first_grad, every, scatter_dimension=0, tiled=True).astype(F32)
+    first_sum = dense_sum(attend_grad.astype(BF16), thin_grad, outward_grad.astype(BF16))
+    outward_sum = first_sum[:, qkv + LANES :]
     attend_sum = jnp.concatenate(
         [unpair_heads(first_sum[:, :query_end], 1), first_sum[:, query_end:qkv]], axis=1
     )
     router_sum = first_sum[:, qkv : qkv + experts]
     gains_sum = first_sum[:, qkv + experts : qkv + experts + 2].T
-    outward_sum = unpair_heads(outward_sum.astype(F32).T, 0)
-    expand_sum = expand_sum.astype(F32)
-    shrink_sum = shrink_sum.astype(F32)
+    outward_sum = unpair_heads(outward_sum.T, 0)
+    expand_sum, shrink_sum = (
+        jnp.concatenate(parts, axis=0)
+        for parts in zip(front_sums, rear_sums)
+    )
     attend_new = adam_update(
         attend_master, attend_mean, attend_square, attend_sum, D ** (-0.5), DECAY
     )

time: 1580 us -> 1030 us (0.65)
  waiting for transfers between devices: 1130 us -> 322 us
  Pallas kernels: 63 us -> 399 us
  matrix products: 243 us -> 94.4 us
  starting transfers between devices: 5.25 us -> 38.4 us
    reduce_scatter x6 -> x4, waiting for transfers between devices: 521 us -> 21.8 us  [the longest x2 21.8 us: scatter(): thin = lax.psum_scatter(thin, inner, scatter_dimension=1, tiled=True)]
    all_gather x7 -> x2, waiting for transfers between devices: 483 us -> 0.02 us  [the longest x1 0.02 us: body(): rear = lax.all_gather(packed[1], ('dp', 'ctx'), axis=0, tiled=False)]
    pallas_call x0 -> x6, Pallas kernels: none -> 335 us  [the longest x4 136 us: run_experts(): pl.pallas_call(functools.partial(experts_kernel, bool(before)), grid_spec...]
    ppermute x0 -> x18, waiting for transfers between devices: none -> 300 us  [the longest x3 196 us: scatter_keys(): lax.ppermute(send, 'ctx', [(i, i - 1) for i in range(count - step, count)])]
    dot_general x11 -> x5, matrix products: 197 us -> 60.9 us  [the longest x2 36.1 us: weight_grads(): lax.dot_general(second_all, grad, contract, preferred_element_type=F32)]
    unnamed x15 -> x6, waiting for transfers between devices: 127 us -> 0.62 us
    ppermute x0 -> x18, starting transfers between devices: none -> 38.1 us  [the longest x3 29.4 us: body(): lax.ppermute(key_pieces[-1], 'ctx', [(i, i + 1) for i in range(step, ctx_...]
  transfers between devices with their start and end apart: 15 -> 24, of which waited for: 15 -> 6; matrix products, arithmetic and copies ran while one was open for 15% -> 20% of each run, Pallas kernels for 1% -> 39%
where the time goes in v2:
time: 1030 us; the launch traced here: 1010 us
  Pallas kernels  399 us (39%)
  waiting for transfers between devices  322 us (31%)
  matrix products  94.4 us (9%)
  other arithmetic  71.8 us (7%)
  local copies, waits for them, and re-layouts  69.7 us (7%)
  starting transfers between devices  38.4 us (4%)
  between operations  16 us (2%)
    ppermute x3, waiting for transfers between devices, scatter_keys(): lax.ppermute(send, 'ctx', [(i, i - 1) for i in range(count - step, count)])  196 us
    pallas_call x4, Pallas kernels, run_experts(): pl.pallas_call(functools.partial(experts_kernel, bool(before)), grid_spec...  136 us
    pallas_call x1, Pallas kernels, dense_sum(): pl.pallas_call(functools.partial(dense_sum_kernel, tuple(starts)), in_spe...  111 us
    pallas_call x1, Pallas kernels, dense_gather(): pl.pallas_call(dense_gather_kernel, in_specs=[pl.BlockSpec(memory_space=p...  87.4 us
    ppermute x4, waiting for transfers between devices, swap_far(): lax.ppermute(block, 'exp', [(i, i ^ 2) for i in range(lax.axis_size('exp'...  58.9 us
    ppermute x3, waiting for transfers between devices, body(): lax.ppermute(key_pieces[-1], 'ctx', [(i, i + 1) for i in range(step, ctx_...  44.6 us
    dot_general x2, matrix products, weight_grads(): lax.dot_general(second_all, grad, contract, preferred_element_type=F32)  36.1 us
    pallas_call x1, Pallas kernels, attend_backward(): pl.pallas_call(attend_back_kernel, grid_spec=pltpu.PrefetchScalarGridSpec...  33.6 us
  transfers between devices with their start and end apart: 24, of which 6 were waited for; matrix products, arithmetic and copies ran while one was open for 20% of the time, Pallas kernels for 39%

profile of v2, /device:TPU:0, one launch (start us, length us, event | category | flops | bytes accessed | tf_op | source)
XLA Modules:
  0.0 1011.8 jit_solution(18305112369202004789)
XLA Ops:
  16.8 87.4 %shard_map.422 = (bf16[2,4,2,2,48,2688]{5,4,3,2,1,0:T(8,128)(2,1)}, bf16[2,4,2,2,48,1536]{5,4,3,2,1,0:T(8,128)(2,1)}) custom-call(bf16[48,2688]{1,0:T(8,128)(2,1)} %concatenate.63.first_ref, bf16[48,1536]{1,0:T(8,128)(2,1)} %bitcast.119), custom_call_target="tpu_custom_call" | custom-call | bytes 12976128 | tf_op jit(solution)/shard_map/pallas_call | solution.py:582
  106.8 3.7 fusion.30
  114.3 3.4 copy-done.11
  117.8 10.6 %shard_map.423 = (bf16[512,1536]{1,0:T(8,128)(2,1)S(1)}, bf16[512,1024]{1,0:T(8,128)(2,1)S(1)}, bf16[512,1536]{1,0:T(8,128)(2,1)S(1)}) custom-call(bf16[512,1536]{1,0:T(8,128)(2,1)S(1)} %bitcast.93, f32[1,1536]{1,0:T(1,128)S(1)} %copy.232.gain_ref, bf16[1536,2688]{1,0:T(8,128)(2,1)S(1)} %bitcast.106, ...), custom_call_target="tpu_custom_call" | custom-call | flops 4026531840 | bytes 7864320 | tf_op jit(solution)/shard_map/pallas_call | solution.py:128
  130.6 26.0 %collective-permute-start = (bf16[512,1024]{1,0:T(8,128)(2,1)S(1)}, bf16[512,1024]{1,0:T(8,128)(2,1)}, u32[]{:S(2)}, u32[]{:S(2)}) collective-permute-start(bf16[512,1024]{1,0:T(8,128)(2,1)S(1)} %get-tuple-element.64.refs_0_.refs_1_), channel_id=1, source_target_pairs={{0,4},{4,8},{8,12},{1,5},{5,9},{9,13},{2,6},{6,10},{10,14},{3,7},{... | collective-permute-start | bytes 3145736 | tf_op jit(solution)/shard_map/ppermute | solution.py:1002
  156.6 44.6 %collective-permute-done.refs_2_.refs_3_ = bf16[512,1024]{1,0:T(8,128)(2,1)} collective-permute-done((bf16[512,1024]{1,0:T(8,128)(2,1)S(1)}, bf16[512,1024]{1,0:T(8,128)(2,1)}, u32[]{:S(2)}, u32[]{:S(2)}) %collective-permute-start) | collective-permute-done | bytes 1048608 | tf_op jit(solution)/shard_map/ppermute | solution.py:1002
  204.8 2.7 convert_reduce_fusion
  209.3 3.7 concatenate.68
  215.5 20.6 %shard_map.424 = (bf16[512,1536]{1,0:T(8,128)(2,1)S(1)}, f32[4,3,128,512]{3,2,1,0:T(8,128)S(1)}, f32[4,6,512]{2,1,0:T(8,128)S(1)}) custom-call(s32[2,4]{1,0:T(2,128)S(1)} %pad_add_fusion.1.bounds_ref, s32[4]{0:T(128)S(1)} %iota_subtract_fusion.owner_ref, s32[2,512]{1,0:T(2,128)S(1)} %pad_add_fusion.place_ref, bf16[512,1536]{1,0:T(8,128)(2,1)S(1)} %copy-done.21, ...), custom_call_target="tpu_custom_call" | custom-call | flops 25769803776 | bytes 4194304 | tf_op jit(solution)/shard_map/pallas_call | solution.py:265
  236.2 6.4 multiply_reduce_fusion.2
  246.7 6.8 collective-permute-done.7
  254.0 31.7 %collective-permute-done.4 = bf16[512,1536]{1,0:T(8,128)(2,1)} collective-permute-done((bf16[512,1536]{1,0:T(8,128)(2,1)S(1)}, bf16[512,1536]{1,0:T(8,128)(2,1)}, u32[]{:S(2)}, u32[]{:S(2)}) %collective-permute-start.4) | collective-permute-done | bytes 1572896 | tf_op jit(solution)/shard_map/ppermute | solution.py:905
  287.3 3.2 fusion.9
  290.4 4.0 pad_maximum_fusion.4.do_ref.code_ref
  298.9 3.3 pad_maximum_fusion.9.h_ref
  302.1 3.9 pad_maximum_fusion.10.h_ref
  306.0 30.7 %shard_map.425 = (bf16[2048,1024]{1,0:T(8,128)(2,1)}, bf16[2048,2048]{1,0:T(8,128)(2,1)}, bf16[1024,1664]{1,0:T(8,128)(2,1)}, bf16[1024,1536]{1,0:T(8,128)(2,1)}) custom-call(s32[1]{0:T(128)} %bitcast.14.first_ref, bf16[1024,1536]{1,0:T(8,128)(2,1)} %pad_maximum_fusion.9.h_ref, bf16[1024,1664]{1,0:T(8,128)(2,1)} %pad_maximum_fusion.4.do_ref.code_ref, ...), custom_call_target="tpu_custom_call" | custom-call | flops 28991029248 | bytes 25165824 | tf_op jit(solution)/shard_map/pallas_call | solution.py:866
  336.7 31.1 %shard_map.426 = (bf16[2048,1024]{1,0:T(8,128)(2,1)}, bf16[2048,2048]{1,0:T(8,128)(2,1)}, bf16[1024,1664]{1,0:T(8,128)(2,1)}, bf16[1024,1536]{1,0:T(8,128)(2,1)}) custom-call(s32[1]{0:T(128)} %bitcast.14.first_ref, bf16[1024,1536]{1,0:T(8,128)(2,1)} %pad_maximum_fusion.10.h_ref, ...), custom_call_target="tpu_custom_call", output_to_operand_aliasing={{0}: (6, {}), {1}: (7, {})} | custom-call | flops 28991029248 | bytes 25165824 | tf_op jit(solution)/shard_map/pallas_call | solution.py:866
  367.8 11.6 %fusion.7 = bf16[1024,1536]{1,0:T(8,128)(2,1)} fusion(bf16[2048,1024]{1,0:T(8,128)(2,1)} %get-tuple-element.72, bf16[1024,1536]{1,0:T(8,128)(2,1)} %slice.190, bf16[1024,1536]{1,0:T(8,128)(2,1)} %fusion.9), kind=kOutput, calls=%fused_computation.22 | convolution fusion | flops 6456606720 | bytes 13631488 | tf_op jit(solution)/shard_map/dot_general | solution.py:1028
  379.4 17.1 %convolution_convert_fusion.3 = bf16[1536,2048]{1,0:T(8,128)(2,1)} fusion(bf16[2048,2048]{1,0:T(8,128)(2,1)S(1)} %copy-done.84, bf16[1024,1536]{1,0:T(8,128)(2,1)S(1)} %copy-done.41, bf16[512,1536]{1,0:T(8,128)(2,1)} %collective-permute-done.3, bf16[512,1536]{1,0:T(8,128)(2,1)S(1)} %multiply_convert_fusion), kind=kOutput, calls=%fused_computation.6 | convolution fusion | flops 12906921984 | bytes 20971520 | tf_op jit(solution)/shard_map/dot_general | solution.py:1027
  396.6 37.3 %shard_map.427 = (bf16[2048,1024]{1,0:T(8,128)(2,1)}, bf16[2048,2048]{1,0:T(8,128)(2,1)}, bf16[1024,1664]{1,0:T(8,128)(2,1)}, bf16[1024,1536]{1,0:T(8,128)(2,1)}) custom-call(s32[1]{0:T(128)S(6)} %add.238.first_ref, bf16[1024,1536]{1,0:T(8,128)(2,1)} %pad_maximum_fusion.10.h_ref, bf16[1024,1664]{1,0:T(8,128)(2,1)} %copy-done.37, ...), custom_call_target="tpu_custom_call" | custom-call | flops 28991029248 | bytes 25165824 | tf_op jit(solution)/shard_map/pallas_call | solution.py:866
  434.0 37.4 %shard_map.428 = (bf16[2048,1024]{1,0:T(8,128)(2,1)}, bf16[2048,2048]{1,0:T(8,128)(2,1)}, bf16[1024,1664]{1,0:T(8,128)(2,1)}, bf16[1024,1536]{1,0:T(8,128)(2,1)}) custom-call(s32[1]{0:T(128)S(6)} %add.238.first_ref, bf16[1024,1536]{1,0:T(8,128)(2,1)} %pad_maximum_fusion.9.h_ref, ...), custom_call_target="tpu_custom_call", output_to_operand_aliasing={{0}: (8, {}), {1}: (9, {})} | custom-call | flops 28991029248 | bytes 25165824 | tf_op jit(solution)/shard_map/pallas_call | solution.py:866
  471.4 11.4 %fusion.8 = bf16[1024,1536]{1,0:T(8,128)(2,1)} fusion(bf16[2048,1024]{1,0:T(8,128)(2,1)} %get-tuple-element.97, bf16[1024,1536]{1,0:T(8,128)(2,1)} %slice.190, bf16[1024,1536]{1,0:T(8,128)(2,1)} %fusion.9), kind=kOutput, calls=%fused_computation.23 | convolution fusion | flops 6456606720 | bytes 13631488 | tf_op jit(solution)/shard_map/dot_general | solution.py:1028
  483.5 2.8 slice.163
  489.0 2.8 slice.161
  491.9 3.2 add_convert_fusion
  495.7 19.0 %convolution_convert_fusion.2 = bf16[1536,2048]{1,0:T(8,128)(2,1)} fusion(bf16[2048,2048]{1,0:T(8,128)(2,1)} %get-tuple-element.96, bf16[1024,1536]{1,0:T(8,128)(2,1)S(1)} %copy-done.42, bf16[512,1536]{1,0:T(8,128)(2,1)} %collective-permute-done.3, bf16[512,1536]{1,0:T(8,128)(2,1)S(1)} %multiply_convert_fusion), kind=kOutput, calls=%fused_computation.5 | convolution fusion | flops 12906921984 | bytes 20971520 | tf_op jit(solution)/shard_map/dot_general | solution.py:1027
  514.7 20.4 %collective-permute-done.11 = bf16[512,1664]{1,0:T(8,128)(2,1)} collective-permute-done((bf16[512,1664]{1,0:T(8,128)(2,1)}, bf16[512,1664]{1,0:T(8,128)(2,1)}, u32[]{:S(2)}, u32[]{:S(2)}) %collective-permute-start.11) | collective-permute-done | bytes 1703968 | tf_op jit(solution)/shard_map/ppermute | solution.py:905
  535.1 3.1 convert_add_fusion.1
  539.0 2.3 multiply_reduce_fusion
  542.5 2.6 convolution_convert_fusion.4.do_ref
  545.9 33.6 %shard_map.429 = (bf16[512,1536]{1,0:T(8,128)(2,1)S(1)}, bf16[2048,512]{1,0:T(8,128)(2,1)S(1)}, bf16[2048,512]{1,0:T(8,128)(2,1)}) custom-call(s32[2,4]{1,0:T(2,128)S(1)} %copy-done.15, s32[4]{0:T(128)S(1)} %copy-done.17, s32[2,512]{1,0:T(2,128)S(1)} %copy-done.13, bf16[512,1536]{1,0:T(8,128)(2,1)S(1)} %copy-done.22, ...), custom_call_target="tpu_custom_call" | custom-call | flops 64424509440 | bytes 8388608 | tf_op jit(solution)/shard_map/pallas_call | solution.py:386
  591.8 2.8 slice.166
  598.0 4.3 convolution_convert_fusion.1
  602.3 3.1 add_convert_fusion.2
  605.8 2.7 add_convert_fusion.4
  612.8 21.8 %reduce-scatter.11.cloned.1.call-done = bf16[2,64,1536]{2,1,0:T(8,128)(2,1)} async-done(((bf16[2,512,1536]{2,1,0:T(8,128)(2,1)}), bf16[2,64,1536]{2,1,0:T(8,128)(2,1)}) %reduce-scatter.11.cloned.1.call-update) | async-done | bytes 393232 | tf_op jit(solution)/shard_map/reduce_scatter | solution.py:1034
  634.6 5.4 fusion.45
  640.1 196.2 %collective-permute-done.17 = bf16[512,1024]{1,0:T(8,128)(2,1)} collective-permute-done((bf16[512,1024]{1,0:T(8,128)(2,1)}, bf16[512,1024]{1,0:T(8,128)(2,1)}, u32[]{:S(2)}, u32[]{:S(2)}) %collective-permute-start.17) | collective-permute-done | bytes 1048608 | tf_op jit(solution)/shard_map/ppermute | solution.py:751
  838.3 10.0 fusion.16
  849.0 6.9 convolution_convert_fusion
  856.0 110.7 %shard_map.430 = f32[48,4224]{1,0:T(8,128)S(1)} custom-call(bf16[2,4,2,2,48,2560]{5,4,3,2,1,0:T(8,128)(2,1)} %bitcast.107, bf16[2,4,2,2,48,128]{5,4,3,2,1,0:T(8,128)(2,1)S(1)} %bitcast.97, bf16[2,4,2,2,48,1536]{5,4,3,2,1,0:T(8,128)(2,1)S(1)} %bitcast.96), custom_call_target="tpu_custom_call" | custom-call | bytes 415236096 | tf_op jit(solution)/shard_map/pallas_call | solution.py:715
  976.9 2.2 reshape.168
  981.0 2.2 fusion.56
  983.2 5.4 fusion.21
  991.2 2.5 fusion.15
  993.7 2.3 copy.272
  997.2 7.4 fusion.48
  (344 shorter events, 81.6 us)
Async XLA Ops:
  7.2 298.8 %all-gather.5.cloned.1.call-start = ((), (), s32[]{:S(2)}) async-start(), calls=%async_computation.8 | async-start | bytes 10616832 | tf_op jit(solution)/shard_map/all_gather | solution.py:963
  13.2 383.4 %all-gather.7.cloned.1.call-start = ((), (), s32[]{:S(2)}) async-start(), calls=%async_computation.9 | async-start | bytes 10616832 | tf_op jit(solution)/shard_map/all_gather | solution.py:964
  106.5 136.1 %copy-start.60 = (f32[1536]{0:T(1024)}, f32[1536]{0:T(1024)S(1)}, u32[]{:S(2)}) copy-start(f32[1536]{0:T(1024)S(1)} %get-tuple-element.233) | copy-start | bytes 18436
  113.2 15.1 %copy-start.7 = (f32[512,128]{1,0:T(8,128)}, f32[512,128]{1,0:T(8,128)S(1)}, u32[]{:S(2)}) copy-start(f32[512,128]{1,0:T(8,128)S(1)} %constant_dynamic-slice_fusion.2.cos_ref.own_cos_ref) | copy-start | bytes 786436
  114.3 14.0 %copy-start.9 = (f32[512,128]{1,0:T(8,128)}, f32[512,128]{1,0:T(8,128)S(1)}, u32[]{:S(2)}) copy-start(f32[512,128]{1,0:T(8,128)S(1)} %constant_dynamic-slice_fusion.1.sin_ref.own_sin_ref) | copy-start | bytes 786436
  117.7 85.8 %copy-start.73 = (s32[1,1,1,4096]{3,2,1,0:T(1,128)S(1)}, s32[1,1,1,4096]{3,2,1,0:T(1,128)}, u32[]{:S(2)}) copy-start(s32[1,1,1,4096]{3,2,1,0:T(1,128)} %param.27) | copy-start | bytes 49156
  117.8 86.8 %copy-start.74 = (s32[1,1,512,8]{2,3,1,0:T(8,128)S(1)}, s32[1,1,512,8]{2,3,1,0:T(8,128)}, u32[]{:S(2)}) copy-start(s32[1,1,512,8]{2,3,1,0:T(8,128)} %param.26) | copy-start | bytes 49156
  130.6 70.6 %collective-permute-start = (bf16[512,1024]{1,0:T(8,128)(2,1)S(1)}, bf16[512,1024]{1,0:T(8,128)(2,1)}, u32[]{:S(2)}, u32[]{:S(2)}) collective-permute-start(bf16[512,1024]{1,0:T(8,128)(2,1)S(1)} %get-tuple-element.64.refs_0_.refs_1_), channel_id=1, source_target_pairs={{0,4},{4,8},{8,12},{1,5},{5,9},{9,13},{2,6},{6,10},{10,14},{3,7},{... | collective-permute-start | bytes 3145736 | tf_op jit(solution)/shard_map/ppermute | solution.py:1002
  201.2 6.4 collective-permute-start.1
  204.7 31.4 %copy-start.56 = (pred[512,16]{1,0:T(32,128)(4,1)}, pred[512,16]{1,0:T(32,128)(4,1)S(1)}, u32[]{:S(2)}) copy-start(pred[512,16]{1,0:T(32,128)(4,1)S(1)} %copy.235) | copy-start | bytes 24580
  207.6 6.5 collective-permute-start.2
  213.0 40.5 %collective-permute-start.7 = (bf16[512,1664]{1,0:T(8,128)(2,1)}, bf16[512,1664]{1,0:T(8,128)(2,1)}, u32[]{:S(2)}, u32[]{:S(2)}) collective-permute-start(bf16[512,1664]{1,0:T(8,128)(2,1)} %concatenate.68), channel_id=1, source_target_pairs={{0,2},{1,3},{2,0},{3,1},{4,6},{5,7},{6,4},{7,5},{8,10},{9,11},{10,... | collective-permute-start | bytes 5111816 | tf_op jit(solution)/shard_map/ppermute | solution.py:905
  213.1 399.7 %reduce-scatter.9.cloned.1.call-start = ((), (), s32[]{:S(2)}) async-start(), calls=%async_computation.6 | async-start | bytes 3538944 | tf_op jit(solution)/shard_map/reduce_scatter | solution.py:1034
  214.0 22.1 %copy-start.16 = (s32[4]{0:T(128)}, s32[4]{0:T(128)S(1)}, u32[]{:S(2)}) copy-start(s32[4]{0:T(128)S(1)} %iota_subtract_fusion.owner_ref) | copy-start | bytes 52
  214.1 22.1 %copy-start.14 = (s32[2,4]{1,0:T(2,128)}, s32[2,4]{1,0:T(2,128)S(1)}, u32[]{:S(2)}) copy-start(s32[2,4]{1,0:T(2,128)S(1)} %pad_add_fusion.1.bounds_ref) | copy-start | bytes 100
  214.1 22.0 %copy-start.12 = (s32[2,512]{1,0:T(2,128)}, s32[2,512]{1,0:T(2,128)S(1)}, u32[]{:S(2)}) copy-start(s32[2,512]{1,0:T(2,128)S(1)} %pad_add_fusion.place_ref) | copy-start | bytes 12292
  242.6 44.6 %copy-start.68 = (f32[512]{0:T(512)}, f32[512]{0:T(512)S(1)}, u32[]{:S(2)}) copy-start(f32[512]{0:T(512)S(1)} %add_rsqrt_fusion.1) | copy-start | bytes 6148
  244.6 251.1 %copy-start.30 = (bf16[512,1536]{1,0:T(8,128)(2,1)}, bf16[512,1536]{1,0:T(8,128)(2,1)S(1)}, u32[]{:S(2)}) copy-start(bf16[512,1536]{1,0:T(8,128)(2,1)S(1)} %multiply_convert_fusion) | copy-start | bytes 4718596
  244.6 41.1 %collective-permute-start.4 = (bf16[512,1536]{1,0:T(8,128)(2,1)S(1)}, bf16[512,1536]{1,0:T(8,128)(2,1)}, u32[]{:S(2)}, u32[]{:S(2)}) collective-permute-start(bf16[512,1536]{1,0:T(8,128)(2,1)S(1)} %multiply_convert_fusion), channel_id=1, source_target_pairs={{0,2},{1,3},{2,0},{3,1},{4,6},{5,7},{6,4},{7,5},{8,10},{9,11},{10,... | collective-permute-start | bytes 4718600 | tf_op jit(solution)/shard_map/ppermute | solution.py:905
  246.7 40.6 %collective-permute-start.6 = (bf16[512,1664]{1,0:T(8,128)(2,1)}, bf16[512,1664]{1,0:T(8,128)(2,1)}, u32[]{:S(2)}, u32[]{:S(2)}) collective-permute-start(bf16[512,1664]{1,0:T(8,128)(2,1)} %concatenate.68), channel_id=1, source_target_pairs={{0,1},{1,0},{2,3},{3,2},{4,5},{5,4},{6,7},{7,6},{8,9},{9,8},{10,11... | collective-permute-start | bytes 5111816 | tf_op jit(solution)/shard_map/ppermute | solution.py:901
  253.5 40.9 %collective-permute-start.8 = (bf16[512,1664]{1,0:T(8,128)(2,1)}, bf16[512,1664]{1,0:T(8,128)(2,1)}, u32[]{:S(2)}, u32[]{:S(2)}) collective-permute-start(bf16[512,1664]{1,0:T(8,128)(2,1)} %collective-permute-done.7), channel_id=1, source_target_pairs={{0,1},{1,0},{2,3},{3,2},{4,5},{5,4},{6,7},{7,6},{8,9},{9,8},{10,11... | collective-permute-start | bytes 5111816 | tf_op jit(solution)/shard_map/ppermute | solution.py:901
  253.5 45.4 %collective-permute-start.3 = (bf16[512,1536]{1,0:T(8,128)(2,1)S(1)}, bf16[512,1536]{1,0:T(8,128)(2,1)}, u32[]{:S(2)}, u32[]{:S(2)}) collective-permute-start(bf16[512,1536]{1,0:T(8,128)(2,1)S(1)} %multiply_convert_fusion), channel_id=1, source_target_pairs={{0,1},{1,0},{2,3},{3,2},{4,5},{5,4},{6,7},{7,6},{8,9},{9,8},{10,11... | collective-permute-start | bytes 4718600 | tf_op jit(solution)/shard_map/ppermute | solution.py:901
  285.7 16.5 %collective-permute-start.5 = (bf16[512,1536]{1,0:T(8,128)(2,1)}, bf16[512,1536]{1,0:T(8,128)(2,1)}, u32[]{:S(2)}, u32[]{:S(2)}) collective-permute-start(bf16[512,1536]{1,0:T(8,128)(2,1)} %collective-permute-done.4), channel_id=1, source_target_pairs={{0,1},{1,0},{2,3},{3,2},{4,5},{5,4},{6,7},{7,6},{8,9},{9,8},{10,11... | collective-permute-start | bytes 4718600 | tf_op jit(solution)/shard_map/ppermute | solution.py:901
  396.6 238.1 %reduce-scatter.11.cloned.1.call-start = ((), (), s32[]{:S(2)}) async-start(), calls=%async_computation.7 | async-start | bytes 3538944 | tf_op jit(solution)/shard_map/reduce_scatter | solution.py:1034
  482.8 510.9 %reduce-scatter.5.cloned.1.call-start = ((), (), s32[]{:S(2)}) async-start(), calls=%async_computation.4 | async-start | bytes 7077888 | tf_op jit(solution)/shard_map/reduce_scatter | solution.py:1033
  483.4 512.6 %reduce-scatter.7.cloned.1.call-start = ((), (), s32[]{:S(2)}) async-start(), calls=%async_computation.5 | async-start | bytes 7077888 | tf_op jit(solution)/shard_map/reduce_scatter | solution.py:1033
  486.3 5.6 collective-permute-start.10
  491.9 22.8 %collective-permute-start.9 = (bf16[512,1664]{1,0:T(8,128)(2,1)}, bf16[512,1664]{1,0:T(8,128)(2,1)}, u32[]{:S(2)}, u32[]{:S(2)}) collective-permute-start(bf16[512,1664]{1,0:T(8,128)(2,1)} %slice.161), channel_id=1, source_target_pairs={{0,1},{1,0},{2,3},{3,2},{4,5},{5,4},{6,7},{7,6},{8,9},{9,8},{10,11... | collective-permute-start | bytes 5111816 | tf_op jit(solution)/shard_map/ppermute | solution.py:901
  495.1 40.0 %collective-permute-start.11 = (bf16[512,1664]{1,0:T(8,128)(2,1)}, bf16[512,1664]{1,0:T(8,128)(2,1)}, u32[]{:S(2)}, u32[]{:S(2)}) collective-permute-start(bf16[512,1664]{1,0:T(8,128)(2,1)} %add_convert_fusion), channel_id=1, source_target_pairs={{0,2},{1,3},{2,0},{3,1},{4,6},{5,7},{6,4},{7,5},{8,10},{9,11},{10,... | collective-permute-start | bytes 5111816 | tf_op jit(solution)/shard_map/ppermute | solution.py:905
  514.7 24.3 %copy-start.29 = (f32[512,1536]{1,0:T(8,128)S(1)}, f32[512,1536]{1,0:T(8,128)}, u32[]{:S(2)}) copy-start(f32[512,1536]{1,0:T(8,128)} %copy-done.28) | copy-start | bytes 9437188
  514.7 24.3 %copy-start.61 = (f32[1536]{0:T(1024)S(1)}, f32[1536]{0:T(1024)}, u32[]{:S(2)}) copy-start(f32[1536]{0:T(1024)} %copy-done.60) | copy-start | bytes 18436
  514.7 24.3 %copy-start.69 = (f32[512]{0:T(512)S(1)}, f32[512]{0:T(512)}, u32[]{:S(2)}) copy-start(f32[512]{0:T(512)} %copy-done.68) | copy-start | bytes 6148
  584.6 10.5 %collective-permute-start.15 = (bf16[512,1024]{1,0:T(8,128)(2,1)}, bf16[512,1024]{1,0:T(8,128)(2,1)}, u32[]{:S(2)}, u32[]{:S(2)}) collective-permute-start(bf16[512,1024]{1,0:T(8,128)(2,1)} %constant_dynamic-slice_fusion), channel_id=1, source_target_pairs={{12,8},{13,9},{14,10},{15,11},{28,24},{29,25},{30,26},{31,27}} | collective-permute-start | bytes 3145736 | tf_op jit(solution)/shard_map/ppermute | solution.py:751
  586.5 15.8 %collective-permute-start.12 = (bf16[512,1536]{1,0:T(8,128)(2,1)S(1)}, bf16[512,1536]{1,0:T(8,128)(2,1)}, u32[]{:S(2)}, u32[]{:S(2)}) collective-permute-start(bf16[512,1536]{1,0:T(8,128)(2,1)S(1)} %slice.165), channel_id=1, source_target_pairs={{0,1},{1,0},{2,3},{3,2},{4,5},{5,4},{6,7},{7,6},{8,9},{9,8},{10,11... | collective-permute-start | bytes 4718600 | tf_op jit(solution)/shard_map/ppermute | solution.py:901
  594.6 243.6 %collective-permute-start.14 = (bf16[512,1536]{1,0:T(8,128)(2,1)}, bf16[512,1536]{1,0:T(8,128)(2,1)}, u32[]{:S(2)}, u32[]{:S(2)}) collective-permute-start(bf16[512,1536]{1,0:T(8,128)(2,1)} %slice.166), channel_id=1, source_target_pairs={{0,1},{1,0},{2,3},{3,2},{4,5},{5,4},{6,7},{7,6},{8,9},{9,8},{10,11... | collective-permute-start | bytes 4718600 | tf_op jit(solution)/shard_map/ppermute | solution.py:901
  597.1 8.7 collective-permute-start.16
  605.4 29.2 %copy-start.39 = (f32[4,64,1536]{2,1,0:T(8,128)S(1)}, f32[4,64,1536]{2,1,0:T(8,128)}, u32[]{:S(2)}) copy-start(f32[4,64,1536]{2,1,0:T(8,128)} %param.43) | copy-start | bytes 4718596
  605.4 232.8 %collective-permute-start.13 = (bf16[512,1536]{1,0:T(8,128)(2,1)}, bf16[512,1536]{1,0:T(8,128)(2,1)}, u32[]{:S(2)}, u32[]{:S(2)}) collective-permute-start(bf16[512,1536]{1,0:T(8,128)(2,1)} %add_convert_fusion.2), channel_id=1, source_target_pairs={{0,2},{1,3},{2,0},{3,1},{4,6},{5,7},{6,4},{7,5},{8,10},{9,11},{10,... | collective-permute-start | bytes 4718600 | tf_op jit(solution)/shard_map/ppermute | solution.py:905
  608.5 227.8 %collective-permute-start.17 = (bf16[512,1024]{1,0:T(8,128)(2,1)}, bf16[512,1024]{1,0:T(8,128)(2,1)}, u32[]{:S(2)}, u32[]{:S(2)}) collective-permute-start(bf16[512,1024]{1,0:T(8,128)(2,1)} %add_convert_fusion.4), channel_id=1, source_target_pairs={{4,0},{8,4},{12,8},{5,1},{9,5},{13,9},{6,2},{10,6},{14,10},{7,3},{... | collective-permute-start | bytes 3145736 | tf_op jit(solution)/shard_map/ppermute | solution.py:751
  640.1 198.2 %copy-start.26 = (bf16[512,1536]{1,0:T(8,128)(2,1)S(1)}, bf16[512,1536]{1,0:T(8,128)(2,1)}, u32[]{:S(2)}) copy-start(bf16[512,1536]{1,0:T(8,128)(2,1)} %copy-done.25) | copy-start | bytes 4718596
  640.1 198.2 %copy-start.72 = (f32[1536]{0:T(1024)S(1)}, f32[1536]{0:T(1024)}, u32[]{:S(2)}) copy-start(f32[1536]{0:T(1024)} %get-tuple-element.232) | copy-start | bytes 18436
  855.9 110.8 %copy-start.65 = (f32[48,16]{1,0:T(8,128)S(1)}, f32[48,16]{1,0:T(8,128)}, u32[]{:S(2)}) copy-start(f32[48,16]{1,0:T(8,128)} %copy.246) | copy-start | bytes 9220
  855.9 110.8 %copy-start.66 = (f32[48,16]{1,0:T(8,128)S(1)}, f32[48,16]{1,0:T(8,128)}, u32[]{:S(2)}) copy-start(f32[48,16]{1,0:T(8,128)} %copy.242) | copy-start | bytes 9220
  855.9 110.8 %copy-start.67 = (f32[48,16]{1,0:T(8,128)S(1)}, f32[48,16]{1,0:T(8,128)}, u32[]{:S(2)}) copy-start(f32[48,16]{1,0:T(8,128)} %copy.244) | copy-start | bytes 9220
  856.0 113.6 %copy-start.63 = (f32[2,48]{0,1:T(8,128)S(1)}, f32[2,48]{0,1:T(8,128)}, u32[]{:S(2)}) copy-start(f32[2,48]{0,1:T(8,128)} %copy.249) | copy-start | bytes 1156
  856.0 113.6 %copy-start.64 = (f32[2,48]{0,1:T(8,128)S(1)}, f32[2,48]{0,1:T(8,128)}, u32[]{:S(2)}) copy-start(f32[2,48]{0,1:T(8,128)} %copy.247) | copy-start | bytes 1156
  856.0 115.2 %copy-start.62 = (f32[2,48]{0,1:T(8,128)S(1)}, f32[2,48]{0,1:T(8,128)}, u32[]{:S(2)}) copy-start(f32[2,48]{0,1:T(8,128)} %copy.252) | copy-start | bytes 1156
  966.7 12.4 %copy-start.2 = (f32[48,4224]{1,0:T(8,128)}, f32[48,4224]{1,0:T(8,128)S(1)}, u32[]{:S(2)}) copy-start(f32[48,4224]{1,0:T(8,128)S(1)} %shard_map.430) | copy-start | bytes 2433028
  (66 other events, 307.4 us)
Sparse Core Ops, SparseCore 0:
  13.3 189.3 all-gather.4
  213.2 172.5 all-gather.6
  396.7 151.5 reduce-scatter.8
  552.3 82.2 reduce-scatter.10
  638.0 124.8 reduce-scatter.4
  766.4 156.0 reduce-scatter.6

commit v3 on v2

--- a/solution.py
+++ b/solution.py
@@ -160,273 +160,312 @@
     )
 
 
-def key_loops(bounds_ref, sub, step):
-    low = bounds_ref[sub, 0]
-    full_low = bounds_ref[sub, 1]
-    full_high = bounds_ref[sub, 2]
-    high = bounds_ref[sub, 3]
-    lax.fori_loop(low, full_low, functools.partial(step, True), 0)
-    lax.fori_loop(full_low, full_high, functools.partial(step, False), 0)
-    lax.fori_loop(full_high, high, functools.partial(step, True), 0)
-
-
-def allowed_keys(block_id, key_rows, columns, place_ref):
-    key_pos = block_id * key_rows + lax.broadcasted_iota(jnp.int32, (key_rows, columns), 0)
+def chunk_flags(place, owner, sub_rows):
+    rows = place.shape[1]
+    start = owner * rows
+    end = start + rows - 1
+    first = place[:, ::sub_rows]
+    last = place[:, sub_rows - 1 :: sub_rows]
+    seen = (owner >= 0) & (start <= last[0]) & (end >= first[1])
+    whole = (last[1] <= start) & (end <= first[0])
+    return jnp.where(seen, jnp.where(whole, 2, 1), 0).astype(jnp.int32)
+
+
+def allowed_keys(owner, key_rows, columns, place_ref):
+    key_pos = owner * key_rows + lax.broadcasted_iota(jnp.int32, (key_rows, columns), 0)
     query_pos = jnp.concatenate([place_ref[0:1, :]] * 2, axis=1)
     first_pos = jnp.concatenate([place_ref[1:2, :]] * 2, axis=1)
     return (key_pos <= query_pos) & (key_pos >= first_pos)
 
 
-def lay_keys(owner_ref, pieces, k_ref, v_ref):
-    for index, (key_piece, value_piece) in enumerate(pieces):
-        rows = key_piece.shape[0]
-        owner = owner_ref[index]
-
-        @pl.when(owner >= 0)
-        def _():
-            start = pl.multiple_of(owner * rows, rows)
-            k_ref[pl.ds(start, rows), :] = key_piece[...]
-            v_ref[pl.ds(start, rows), :] = value_piece[...]
-
-
-def attend_kernel(bounds_ref, owner_ref, place_ref, q_ref, *refs):
-    count = owner_ref.shape[0]
-    pieces = [(refs[2 * i], refs[2 * i + 1]) for i in range(count)]
-    o_ref, ot_ref, lse_ref, k_ref, v_ref, qq, vt, top, total, acc = refs[2 * count :]
+def halves(index, rows):
+    return slice(index * rows, (index + 1) * rows)
+
+
+def attend_kernel(first, final, flag_ref, owner_ref, place_ref, q_ref, k_ref, v_ref, *refs):
     sub = pl.program_id(1)
-    query_rows = q_ref.shape[0]
-    columns = 2 * query_rows
-    key_rows = min(256, k_ref.shape[0])
-
-    @pl.when(sub == 0)
-    def _():
-        lay_keys(owner_ref, pieces, k_ref, v_ref)
-        vt[...] = v_ref[...].astype(F32).T.astype(BF16)
-
+    rows = q_ref.shape[0]
+    key_rows = k_ref.shape[0]
+    columns = 2 * rows
+    if first:
+        before = None
+    else:
+        before, refs = refs[:3], refs[3:]
+    outs, (top, total, acc) = refs[:3], refs[3:]
     for r in range(GROUP):
-        qq[r] = masked_pair(q_ref[:, r * LANES : (r + 1) * LANES])
-    top[...] = jnp.full(top.shape, NEGATIVE, F32)
-    total[...] = jnp.zeros(total.shape, F32)
-    acc[...] = jnp.zeros(acc.shape, F32)
-
-    def step(masked, block_id, carry):
-        start = pl.multiple_of(block_id * key_rows, key_rows)
-        keys = k_ref[pl.ds(start, key_rows), :]
-        turned = vt[:, pl.ds(start, key_rows)]
+        if first:
+            top[r] = jnp.full((1, columns), NEGATIVE, F32)
+            total[r] = jnp.zeros((1, columns), F32)
+            acc[r] = jnp.zeros((LANES, columns), F32)
+        else:
+            acc[r] = jnp.zeros((LANES, columns), F32)
+            for i in range(2):
+                cols = halves(i, rows)
+                head = slice(2 * r + i, 2 * r + i + 1)
+                top[r, :, cols] = before[0][0, head, :]
+                total[r, :, cols] = before[1][0, head, :]
+                acc[r, halves(i, HD), cols] = before[2][0, r, halves(i, HD), :]
+
+    def update(masked):
+        keys = k_ref[...]
+        turned = v_ref[...].astype(F32).T.astype(BF16)
         if masked:
-            allowed = allowed_keys(block_id, key_rows, columns, place_ref)
+            allowed = allowed_keys(owner_ref[0], key_rows, columns, place_ref)
         for r in range(GROUP):
-            scores = lax.dot_general(keys, qq[r], NT, preferred_element_type=F32)
+            queries = masked_pair(q_ref[:, r * LANES : (r + 1) * LANES])
+            scores = lax.dot_general(keys, queries, NT, preferred_element_type=F32)
             if masked:
                 scores = jnp.where(allowed, scores, NEGATIVE)
-            before = top[r]
-            now = jnp.maximum(before, jnp.max(scores, axis=0, keepdims=True))
-            shrinking = jnp.exp(before - now)
+            old = top[r]
+            now = jnp.maximum(old, jnp.max(scores, axis=0, keepdims=True))
+            shrinking = jnp.exp(old - now)
             terms = jnp.exp(scores - now)
             top[r] = now
             total[r] = total[r] * shrinking + jnp.sum(terms, axis=0, keepdims=True)
             acc[r] = acc[r] * shrinking + jnp.dot(
                 turned, terms.astype(BF16), preferred_element_type=F32
             )
-        return carry
-
-    key_loops(bounds_ref, sub, step)
+
+    @pl.when(flag_ref[sub] == 1)
+    def _():
+        update(True)
+
+    @pl.when(flag_ref[sub] == 2)
+    def _():
+        update(False)
+
     for r in range(GROUP):
-        mixed = acc[r] / total[r]
-        lse = top[r] + jnp.log(total[r])
+        mixed = acc[r] / total[r] if final else acc[r]
+        both = jnp.concatenate([mixed[:HD, :rows], mixed[HD:, rows:]], axis=0)
+        if final:
+            lse = top[r] + jnp.log(total[r])
         for i in range(2):
-            lse_ref[0, 2 * r + i : 2 * r + i + 1, :] = lse[
-                :, i * query_rows : (i + 1) * query_rows
-            ]
-        both = jnp.concatenate([mixed[:HD, :query_rows], mixed[HD:, query_rows:]], axis=0)
-        ot_ref[0, r] = both
-        o_ref[:, r * LANES : (r + 1) * LANES] = both.T.astype(BF16)
-
-
-def piece_specs(pieces):
-    specs = []
-    operands = []
-    for piece in pieces:
-        rows = piece.shape[0]
-        specs.append(pl.BlockSpec((rows, LANES), lambda p, s, *_: (0, p)))
-        specs.append(pl.BlockSpec((rows, LANES), lambda p, s, *_: (0, PAIRS + p)))
-        operands += [piece, piece]
-    return (specs, operands)
-
-
-def attend_forward(bounds, owners, place, q, pieces):
+            head = slice(2 * r + i, 2 * r + i + 1)
+            if final:
+                outs[1][0, head, :] = lse[:, halves(i, rows)]
+            else:
+                outs[0][0, head, :] = top[r, :, halves(i, rows)]
+                outs[1][0, head, :] = total[r, :, halves(i, rows)]
+        outs[2][0, r] = both
+        if final:
+            outs[0][:, r * LANES : (r + 1) * LANES] = both.T.astype(BF16)
+
+
+def head_specs(rows, sub_rows):
+    line = pl.BlockSpec((1, 2 * GROUP, sub_rows), lambda p, s, *_: (p, 0, s))
+    turned = pl.BlockSpec((1, GROUP, LANES, sub_rows), lambda p, s, *_: (p, 0, 0, s))
+    wide = pl.BlockSpec((sub_rows, GROUP * LANES), lambda p, s, *_: (s, p))
+    line_shape = jax.ShapeDtypeStruct((PAIRS, 2 * GROUP, rows), F32)
+    turned_shape = jax.ShapeDtypeStruct((PAIRS, GROUP, LANES, rows), F32)
+    wide_shape = jax.ShapeDtypeStruct((rows, HEADS * HD), BF16)
+    return (line, turned, wide, line_shape, turned_shape, wide_shape)
+
+
+def attend_forward(place, owner, q, piece, before, final):
     rows = q.shape[0]
-    stream = rows * len(pieces)
-    specs, operands = piece_specs(pieces)
     sub_rows = min(256, rows)
-    subs = rows // sub_rows
     columns = 2 * sub_rows
-    wide = GROUP * LANES
+    line, turned, wide, line_shape, turned_shape, wide_shape = head_specs(rows, sub_rows)
     return pl.pallas_call(
-        attend_kernel,
+        functools.partial(attend_kernel, not before, final),
         grid_spec=pltpu.PrefetchScalarGridSpec(
             num_scalar_prefetch=2,
-            grid=(PAIRS, subs),
+            grid=(PAIRS, rows // sub_rows),
             in_specs=[
                 pl.BlockSpec((2, sub_rows), lambda p, s, *_: (0, s)),
-                pl.BlockSpec((sub_rows, wide), lambda p, s, *_: (s, p)),
-                *specs,
+                wide,
+                pl.BlockSpec((rows, LANES), lambda p, s, *_: (0, p)),
+                pl.BlockSpec((rows, LANES), lambda p, s, *_: (0, PAIRS + p)),
+                *([line, line, turned] if before else []),
             ],
-            out_specs=[
-                pl.BlockSpec((sub_rows, wide), lambda p, s, *_: (s, p)),
-                pl.BlockSpec((1, GROUP, LANES, sub_rows), lambda p, s, *_: (p, 0, 0, s)),
-                pl.BlockSpec((1, 2 * GROUP, sub_rows), lambda p, s, *_: (p, 0, s)),
-            ],
+            out_specs=[wide, line, turned] if final else [line, line, turned],
             scratch_shapes=[
-                pltpu.VMEM((stream, LANES), BF16),
-                pltpu.VMEM((stream, LANES), BF16),
-                pltpu.VMEM((GROUP, columns, LANES), BF16),
-                pltpu.VMEM((LANES, stream), BF16),
                 pltpu.VMEM((GROUP, 1, columns), F32),
                 pltpu.VMEM((GROUP, 1, columns), F32),
                 pltpu.VMEM((GROUP, LANES, columns), F32),
             ],
         ),
-        out_shape=[
-            jax.ShapeDtypeStruct((rows, HEADS * HD), BF16),
-            jax.ShapeDtypeStruct((PAIRS, GROUP, LANES, rows), F32),
-            jax.ShapeDtypeStruct((PAIRS, 2 * GROUP, rows), F32),
-        ],
+        out_shape=[wide_shape if final else line_shape, line_shape, turned_shape],
         compiler_params=pltpu.CompilerParams(vmem_limit_bytes=40 * 1024 * 1024),
         cost_estimate=pl.CostEstimate(
-            flops=16 * rows * stream * D, bytes_accessed=2 * stream * 1024, transcendentals=0
+            flops=40 * rows * rows * D, bytes_accessed=8 * rows * D, transcendentals=0
         ),
-    )(bounds, owners, place, q, *operands)
+    )(chunk_flags(place, owner, sub_rows), owner[None], place, q, piece, piece, *before)
+
+
+def delta_kernel(do_ref, ot_ref, delta_ref):
+    for r in range(GROUP):
+        product = do_ref[:, r * LANES : (r + 1) * LANES].astype(F32).T * ot_ref[0, r]
+        for i in range(2):
+            delta_ref[0, 2 * r + i : 2 * r + i + 1, :] = jnp.sum(
+                product[halves(i, HD)], axis=0, keepdims=True
+            )
+
+
+def row_deltas(do, ot):
+    rows = do.shape[0]
+    line, turned, wide, line_shape, _, _ = head_specs(rows, rows)
+    return pl.pallas_call(
+        delta_kernel,
+        grid=(PAIRS, 1),
+        in_specs=[wide, turned],
+        out_specs=line,
+        out_shape=line_shape,
+        cost_estimate=pl.CostEstimate(
+            flops=2 * rows * D, bytes_accessed=6 * rows * D, transcendentals=0
+        ),
+    )(do, ot)
 
 
 def attend_back_kernel(
-    bounds_ref,
+    first,
+    final,
+    flag_ref,
     owner_ref,
     place_ref,
     q_ref,
     do_ref,
-    ot_ref,
     lse_ref,
+    delta_ref,
+    k_ref,
+    v_ref,
     cos_ref,
     sin_ref,
     own_cos_ref,
     own_sin_ref,
     *refs,
 ):
-    count = owner_ref.shape[0]
-    pieces = [(refs[2 * i], refs[2 * i + 1]) for i in range(count)]
-    dq_ref, dk_ref, dv_ref, k_ref, v_ref, qq, dd, kt, stats, acc, dk, dv = refs[2 * count :]
     sub = pl.program_id(1)
-    query_rows = q_ref.shape[0]
-    columns = 2 * query_rows
-    key_rows = min(256, k_ref.shape[0])
+    rows = q_ref.shape[0]
+    key_rows = k_ref.shape[0]
+    columns = 2 * rows
+    if not first:
+        before = refs[0]
+    grad_ref, pair_ref, acc, dk, dv = refs[len(refs) - 5 :]
 
     @pl.when(sub == 0)
     def _():
-        lay_keys(owner_ref, pieces, k_ref, v_ref)
-        kt[...] = k_ref[...].astype(F32).T.astype(BF16)
         dk[...] = jnp.zeros(dk.shape, F32)
         dv[...] = jnp.zeros(dv.shape, F32)
 
-    for r in range(GROUP):
-        lanes = slice(r * LANES, (r + 1) * LANES)
-        qq[r] = masked_pair(q_ref[:, lanes])
-        dd[r] = masked_pair(do_ref[:, lanes])
-        product = do_ref[:, lanes].astype(F32).T * ot_ref[0, r]
-        for i in range(2):
-            own = slice(i * query_rows, (i + 1) * query_rows)
-            stats[r, 0:1, own] = lse_ref[0, 2 * r + i : 2 * r + i + 1, :]
-            stats[r, 1:2, own] = jnp.sum(product[i * HD : (i + 1) * HD], axis=0, keepdims=True)
     acc[...] = jnp.zeros(acc.shape, F32)
-
-    def step(masked, block_id, carry):
-        start = pl.multiple_of(block_id * key_rows, key_rows)
-        keys = k_ref[pl.ds(start, key_rows), :]
-        values = v_ref[pl.ds(start, key_rows), :]
-        turned = kt[:, pl.ds(start, key_rows)]
-        key_grad = dk[pl.ds(start, key_rows), :]
-        value_grad = dv[pl.ds(start, key_rows), :]
+    if not first:
+        for r in range(GROUP):
+            for i in range(2):
+                acc[r, halves(i, HD), halves(i, rows)] = before[0, r, halves(i, HD), :]
+
+    def update(masked):
+        keys = k_ref[...]
+        values = v_ref[...]
+        turned = keys.astype(F32).T.astype(BF16)
+        key_grad = dk[...]
+        value_grad = dv[...]
         if masked:
-            allowed = allowed_keys(block_id, key_rows, columns, place_ref)
+            allowed = allowed_keys(owner_ref[0], key_rows, columns, place_ref)
         for r in range(GROUP):
-            scores = lax.dot_general(keys, qq[r], NT, preferred_element_type=F32)
-            probs = jnp.exp(scores - stats[r, 0:1, :])
+            lanes = slice(r * LANES, (r + 1) * LANES)
+            queries = masked_pair(q_ref[:, lanes])
+            grads = masked_pair(do_ref[:, lanes])
+            heads = [slice(2 * r + i, 2 * r + i + 1) for i in range(2)]
+            lse = jnp.concatenate([lse_ref[0, head, :] for head in heads], axis=1)
+            delta = jnp.concatenate([delta_ref[0, head, :] for head in heads], axis=1)
+            scores = lax.dot_general(keys, queries, NT, preferred_element_type=F32)
+            probs = jnp.exp(scores - lse)
             if masked:
                 probs = jnp.where(allowed, probs, 0.0)
-            value_grad += jnp.dot(probs.astype(BF16), dd[r], preferred_element_type=F32)
-            prob_grad = lax.dot_general(values, dd[r], NT, preferred_element_type=F32)
-            score_grad = (probs * (prob_grad - stats[r, 1:2, :])).astype(BF16)
-            key_grad += jnp.dot(score_grad, qq[r], preferred_element_type=F32)
+            value_grad += jnp.dot(probs.astype(BF16), grads, preferred_element_type=F32)
+            prob_grad = lax.dot_general(values, grads, NT, preferred_element_type=F32)
+            score_grad = (probs * (prob_grad - delta)).astype(BF16)
+            key_grad += jnp.dot(score_grad, queries, preferred_element_type=F32)
             acc[r] += jnp.dot(turned, score_grad, preferred_element_type=F32)
-        dk[pl.ds(start, key_rows), :] = key_grad
-        dv[pl.ds(start, key_rows), :] = value_grad
-        return carry
-
-    key_loops(bounds_ref, sub, step)
+        dk[...] = key_grad
+        dv[...] = value_grad
+
+    @pl.when(flag_ref[sub] == 1)
+    def _():
+        update(True)
+
+    @pl.when(flag_ref[sub] == 2)
+    def _():
+        update(False)
+
     for r in range(GROUP):
-        both = jnp.concatenate([acc[r, :HD, :query_rows], acc[r, HD:, query_rows:]], axis=0)
-        grad = both.T * SCALE
-        grad = grad * own_cos_ref[...] - swap_halves(grad) * own_sin_ref[...]
-        dq_ref[:, r * LANES : (r + 1) * LANES] = grad.astype(BF16)
+        both = jnp.concatenate([acc[r, :HD, :rows], acc[r, HD:, rows:]], axis=0)
+        if final:
+            grad = both.T * SCALE
+            grad = grad * own_cos_ref[...] - swap_halves(grad) * own_sin_ref[...]
+            grad_ref[:, r * LANES : (r + 1) * LANES] = grad.astype(BF16)
+        else:
+            grad_ref[0, r] = both
 
     @pl.when(sub == pl.num_programs(1) - 1)
     def _():
-        dk_ref[...] = (dk[...] * cos_ref[...] - swap_halves(dk[...]) * sin_ref[...]).astype(BF16)
-        dv_ref[...] = dv[...].astype(BF16)
-
-
-def attend_backward(bounds, owners, place, q, do, ot, lse, pieces, tables, own_tables):
+        pair_ref[0] = (dk[...] * cos_ref[...] - swap_halves(dk[...]) * sin_ref[...]).astype(BF16)
+        pair_ref[1] = dv[...].astype(BF16)
+
+
+def attend_backward(
+    place, owner, q, do, lse, delta, piece, tables, own_tables, before, final, tie
+):
     rows = q.shape[0]
-    stream = rows * len(pieces)
-    specs, operands = piece_specs(pieces)
     sub_rows = min(256, rows)
-    subs = rows // sub_rows
     columns = 2 * sub_rows
-    wide = GROUP * LANES
+    line, turned, wide, _, turned_shape, wide_shape = head_specs(rows, sub_rows)
+    far = pl.BlockSpec((rows, LANES), lambda p, s, flags, own: (jnp.maximum(own[0], 0), 0))
+    near = pl.BlockSpec((sub_rows, LANES), lambda p, s, *_: (s, 0))
     return pl.pallas_call(
-        attend_back_kernel,
+        functools.partial(attend_back_kernel, not before, final),
         grid_spec=pltpu.PrefetchScalarGridSpec(
             num_scalar_prefetch=2,
-            grid=(PAIRS, subs),
+            grid=(PAIRS, rows // sub_rows),
             in_specs=[
                 pl.BlockSpec((2, sub_rows), lambda p, s, *_: (0, s)),
-                pl.BlockSpec((sub_rows, wide), lambda p, s, *_: (s, p)),
-                pl.BlockSpec((sub_rows, wide), lambda p, s, *_: (s, p)),
-                pl.BlockSpec((1, GROUP, LANES, sub_rows), lambda p, s, *_: (p, 0, 0, s)),
-                pl.BlockSpec((1, 2 * GROUP, sub_rows), lambda p, s, *_: (p, 0, s)),
-                pl.BlockSpec((stream, LANES), lambda p, s, *_: (0, 0)),
-                pl.BlockSpec((stream, LANES), lambda p, s, *_: (0, 0)),
-                pl.BlockSpec((sub_rows, LANES), lambda p, s, *_: (s, 0)),
-                pl.BlockSpec((sub_rows, LANES), lambda p, s, *_: (s, 0)),
-                *specs,
+                wide,
+                wide,
+                line,
+                line,
+                pl.BlockSpec((rows, LANES), lambda p, s, *_: (0, p)),
+                pl.BlockSpec((rows, LANES), lambda p, s, *_: (0, PAIRS + p)),
+                far,
+                far,
+                near,
+                near,
+                *([turned] if before else []),
+                *([pl.BlockSpec(memory_space=pl.ANY)] * len(tie)),
             ],
             out_specs=[
-                pl.BlockSpec((sub_rows, wide), lambda p, s, *_: (s, p)),
-                pl.BlockSpec((stream, LANES), lambda p, s, *_: (0, p)),
-                pl.BlockSpec((stream, LANES), lambda p, s, *_: (0, p)),
+                wide if final else turned,
+                pl.BlockSpec((2, rows, LANES), lambda p, s, *_: (0, 0, p)),
             ],
             scratch_shapes=[
-                pltpu.VMEM((stream, LANES), BF16),
-                pltpu.VMEM((stream, LANES), BF16),
-                pltpu.VMEM((GROUP, columns, LANES), BF16),
-                pltpu.VMEM((GROUP, columns, LANES), BF16),
-                pltpu.VMEM((LANES, stream), BF16),
-                pltpu.VMEM((GROUP, 2, columns), F32),
                 pltpu.VMEM((GROUP, LANES, columns), F32),
-                pltpu.VMEM((stream, LANES), F32),
-                pltpu.VMEM((stream, LANES), F32),
+                pltpu.VMEM((rows, LANES), F32),
+                pltpu.VMEM((rows, LANES), F32),
             ],
         ),
         out_shape=[
-            jax.ShapeDtypeStruct((rows, HEADS * HD), BF16),
-            jax.ShapeDtypeStruct((stream, KVH * HD), BF16),
-            jax.ShapeDtypeStruct((stream, KVH * HD), BF16),
+            wide_shape if final else turned_shape,
+            jax.ShapeDtypeStruct((2, rows, KVH * HD), BF16),
         ],
         compiler_params=pltpu.CompilerParams(vmem_limit_bytes=40 * 1024 * 1024),
         cost_estimate=pl.CostEstimate(
-            flops=40 * rows * stream * D, bytes_accessed=4 * stream * 1024, transcendentals=0
+            flops=60 * rows * rows * D, bytes_accessed=8 * rows * D, transcendentals=0
         ),
-    )(bounds, owners, place, q, do, ot, lse, *tables, *own_tables, *operands)
+    )(
+        chunk_flags(place, owner, sub_rows),
+        owner[None],
+        place,
+        q,
+        do,
+        lse,
+        delta,
+        piece,
+        piece,
+        *tables,
+        *own_tables,
+        *before,
+        *tie,
+    )
 
 
 def slot_codes(route_ids, priority_row, experts, capacity):
@@ -738,26 +777,10 @@
     )(*[part.reshape(2, 4, 2, 2, rows, part.shape[1]) for part in parts])
 
 
-def scatter_keys(grads, rows):
-    count = lax.axis_size("ctx")
-    place = lax.axis_index("ctx")
-
-    def own(spot):
-        return lax.dynamic_slice_in_dim(grads, jnp.maximum(spot, 0) * rows, rows, 0).astype(F32)
-
-    got = jnp.zeros((rows, grads.shape[1]), F32)
-    for step in range(1, count):
-        send = (own(place - count + step) + got).astype(BF16)
-        got = lax.ppermute(
-            send, "ctx", [(i, i - 1) for i in range(count - step, count)]
-        ).astype(F32)
-    return own(place) + got
-
-
 def experts_kernel(has_before, first_ref, h_ref, do_ref, code_ref, router_ref, weights, *refs):
     if has_before:
-        back_before, mix_before = refs[:2]
-        refs = refs[2:]
+        back_before, tail_before, mix_before = refs[:3]
+        refs = refs[3:]
     refs = refs[len(refs) - 7 :]
     gh_ref, dgu_ref, back_ref, mix_ref, table, back_acc, mix_acc = refs
     expert = pl.program_id(0)
@@ -778,8 +801,12 @@
         terms = jnp.where(routed, jnp.exp(jnp.where(routed, logits - top, 0.0)), 0.0)
         shares = terms / jnp.sum(terms, axis=1, keepdims=True)
         table[own, :] = jnp.where(codes > 1.5, shares, 0.0)
-        back_acc[own, :] = jnp.zeros((tokens, D), F32)
-        mix_acc[own, :] = jnp.zeros((tokens, D), F32)
+        if has_before:
+            back_acc[own, :] = back_before[...].astype(F32)
+            mix_acc[own, :] = mix_before[...].astype(F32)
+        else:
+            back_acc[own, :] = jnp.zeros((tokens, D), F32)
+            mix_acc[own, :] = jnp.zeros((tokens, D), F32)
 
     mine = lane == first_ref[0] + expert
     kept = jnp.sum(jnp.where(mine, codes, 0.0), axis=1, keepdims=True) > 1.5
@@ -825,16 +852,13 @@
         fine = total - coarse.astype(F32)
         grad_gates = coarse.astype(F32) + pltpu.roll(fine, LANES // 2, 1)
         if has_before:
-            mix_ref[...] = (mix_acc[own, :] + mix_before[...].astype(F32)).astype(BF16)
-            back_ref[:, :D] = (back_acc[own, :] + back_before[:, :D].astype(F32)).astype(BF16)
-            back_ref[:, D:] = (grad_gates + back_before[:, D:].astype(F32)).astype(BF16)
-        else:
-            mix_ref[...] = mix_acc[own, :].astype(BF16)
-            back_ref[:, :D] = back_acc[own, :].astype(BF16)
-            back_ref[:, D:] = grad_gates.astype(BF16)
-
-
-def run_experts(first, part, parts, second, known, first_w, weights, block, before, kept):
+            grad_gates += tail_before[...].astype(F32)
+        mix_ref[...] = mix_acc[own, :].astype(BF16)
+        back_ref[:, :D] = back_acc[own, :].astype(BF16)
+        back_ref[:, D:] = grad_gates.astype(BF16)
+
+
+def run_experts(first, part, parts, second, known, first_w, weights, block, before, kept, tie):
     tokens = second.shape[0]
     chunk = tokens // 2
     owners, experts, depth, _ = weights.shape
@@ -843,6 +867,9 @@
 
     def final(e, c, *_):
         return (jnp.where(e == last, c, 0), 0)
+
+    def initial(e, c, *_):
+        return (jnp.where(e == 0, c, 1), 0)
 
     in_specs = [
         pl.BlockSpec((chunk, D), lambda e, c, *_: (c, 0)),
@@ -854,10 +881,13 @@
     operands = [first, second, known, known, first_w, weights]
     if before:
         in_specs += [
-            pl.BlockSpec((chunk, D + LANES), final, pipeline_mode=once),
-            pl.BlockSpec((chunk, D), final, pipeline_mode=once),
+            pl.BlockSpec((chunk, D), initial),
+            pl.BlockSpec((chunk, LANES), lambda e, c, *_: (c, D // LANES)),
+            pl.BlockSpec((chunk, D), initial),
         ]
-        operands += list(before)
+        operands += [before[0], before[0], before[1]]
+    in_specs += [pl.BlockSpec(memory_space=pl.ANY)] * len(tie)
+    operands += list(tie)
     aliases = {}
     if kept:
         in_specs += [pl.BlockSpec(memory_space=pl.ANY)] * 2
@@ -961,7 +991,6 @@
         for i in (0, half)
     ]
     front = lax.all_gather(packed[0], ("dp", "ctx"), axis=0, tiled=False)
-    rear = lax.all_gather(packed[1], ("dp", "ctx"), axis=0, tiled=False)
     first_w, outward_w = dense_gather(first_own, pair_heads(outward_master, 0).T.astype(BF16))
     attend_w = first_w[:, :qkv]
     router_w = first_w[:, qkv : qkv + experts]
@@ -971,26 +1000,19 @@
     known = jnp.concatenate(
         [cotangent[0, 0], codes.astype(BF16), jnp.zeros((rows_dev, LANES - experts), BF16)], axis=1
     )
+    known = after(known, first_w)
     known_core = swap_core(known)
     known_far = swap_far(known)
     known_last = swap_core(known_far)
     known_near = jnp.concatenate([known, known_core], axis=0)
     known_far = jnp.concatenate([known_far, known_last], axis=0)
+    grad_out_all = jnp.concatenate([known_near[:, :width], known_far[:, :width]], axis=0)
 
     positions = ctx_place * rows_dev + jnp.arange(rows_dev, dtype=jnp.int32)
     all_positions = jnp.arange(stream_len, dtype=jnp.int32)
     starts = doc_starts[0, 0]
     first_pos = jnp.max(jnp.where(starts[None, :] <= positions[:, None], starts[None, :], 0), axis=1)
     place = jnp.stack([positions, first_pos], axis=0)
-    sub_rows = min(256, rows_dev)
-    key_rows = min(256, stream_len)
-    sub_first = positions[::sub_rows]
-    sub_last = positions[sub_rows - 1 :: sub_rows]
-    low = first_pos[::sub_rows] // key_rows
-    high = sub_last // key_rows + 1
-    full_low = jnp.clip((first_pos[sub_rows - 1 :: sub_rows] + key_rows - 1) // key_rows, low, high)
-    full_high = jnp.clip((sub_first + 1) // key_rows, full_low, high)
-    bounds = jnp.stack([low, full_low, full_high, high], axis=1)
     tables = turn_tables(all_positions)
     own_tables = tuple(
         lax.dynamic_slice_in_dim(table, ctx_place * rows_dev, rows_dev, 0) for table in tables
@@ -1001,10 +1023,17 @@
         key_pieces.append(
             lax.ppermute(key_pieces[-1], "ctx", [(i, i + 1) for i in range(step, ctx_count - 1)])
         )
-    key_owners = ctx_place - jnp.arange(ctx_count, dtype=jnp.int32)
-    mixed_low, mixed_turned, log_total = attend_forward(
-        bounds, key_owners, place, queries, key_pieces
-    )
+    rear = lax.all_gather(after(packed[1], key_pieces[-1]), ("dp", "ctx"), axis=0, tiled=False)
+    state = ()
+    for step in range(ctx_count):
+        state = attend_forward(
+            place, ctx_place - step, queries, key_pieces[step], state, step == ctx_count - 1
+        )
+        if step == ctx_count - 2:
+            *state, known_near, known_far, grad_out_all = lax.optimization_barrier(
+                (*state, known_near, known_far, grad_out_all)
+            )
+    mixed_low, log_total, mixed_turned = state
     branch = lax.dot_general(mixed_low, outward_w, NT, preferred_element_type=F32)
     middle = local_rows + branch
     second_norm, second_unit, second_scale = rms_forward(middle, gains_f[1])
@@ -1016,44 +1045,60 @@
     second_near = jnp.concatenate([second_low, second_core], axis=0)
     router_block = qkv // LANES
 
-    def group(index, part, second, known, weights, before, kept):
+    def group(index, part, second, known, weights, before, kept, *tie):
         first = first_expert + index * half
         return run_experts(
-            first, part, 2, second, known, first_w, weights, router_block, before, kept
-        )
-
-    def weight_grads(hidden, grad):
-        contract = (((0,), (0,)), ((), ()))
+            first, part, 2, second, known, first_w, weights, router_block, before, kept, tie
+        )
+
+    contract = (((0,), (0,)), ((), ()))
+
+    def wide_grad_of(grad, *others):
+        grad = after(grad, *others)
         wide = lax.dot_general(second_all, grad, contract, preferred_element_type=F32)
+        return wide.astype(BF16)
+
+    def thin_grad_of(hidden, *others):
+        hidden = after(hidden, *others)
         thin = lax.dot_general(hidden, grad_out_all, contract, preferred_element_type=F32)
-        return (wide.astype(BF16), thin.astype(BF16).reshape(half, FF, width))
-
-    def scatter(wide, thin):
-        inner = ("dp", "ctx")
-        wide = lax.psum_scatter(wide, inner, scatter_dimension=0, tiled=True)
-        thin = lax.psum_scatter(thin, inner, scatter_dimension=1, tiled=True)
-        wide = jnp.swapaxes(wide.reshape(-1, half, 2 * FF), 0, 1)
-        return (wide.astype(F32), thin.astype(F32))
+        return thin.astype(BF16).reshape(half, FF, width)
+
+    owners = lax.axis_size("dp") * ctx_count
+
+    def owner_rows(wide, thin):
+        thin = jnp.swapaxes(thin.reshape(half, owners, FF // owners, width), 0, 1)
+        thin = thin.reshape(owners, width // owners, half * FF)
+        both = jnp.concatenate([wide.reshape(owners, width // owners, -1), thin], axis=2)
+        return both.reshape(width, -1)
+
+    def scatter(both):
+        return lax.psum_scatter(both, ("dp", "ctx"), scatter_dimension=0, tiled=True)
+
+    def own_grads(total):
+        wide = total[:, : half * 2 * FF].reshape(-1, half, 2 * FF)
+        thin = total[:, half * 2 * FF :].reshape(half, FF // owners, width)
+        return (jnp.swapaxes(wide, 0, 1).astype(F32), thin.astype(F32))
 
     *kept, back_near, mix_near = group(0, 0, second_near, known_near, front, (), ())
+    second_far = after(second_far, back_near)
     second_last = swap_core(second_far)
     second_far = jnp.concatenate([second_far, second_last], axis=0)
-    second_far = after(second_far, back_near)
     second_all = jnp.concatenate([second_near, second_far], axis=0)
-    grad_out_all = jnp.concatenate([known_near[:, :width], known_far[:, :width]], axis=0)
     hidden, grad, back_far, mix_far = group(0, 1, second_far, known_far, front, (), kept)
-    front_grads = weight_grads(hidden, grad)
-    front_sums = scatter(*front_grads)
-    second_far = after(second_far, *front_grads)
+    front_grads = (wide_grad_of(grad, back_far), thin_grad_of(hidden, back_far))
+    front_rows = owner_rows(*front_grads)
+    front_sum = scatter(front_rows)
     *kept, back_far, mix_far = group(
-        1, 1, second_far, known_far, rear, (back_far, mix_far), ()
+        1, 1, second_far, known_far, rear, (back_far, mix_far), (), front_rows
     )
     across = back_far[:rows_dev].astype(F32) + swap_core(back_far[rows_dev:]).astype(F32)
-    across = swap_far(across.astype(BF16))
-    second_near = after(second_near, back_far)
+    across = across.astype(BF16)
+    second_near = after(second_near, across)
+    across = swap_far(across)
     hidden, grad, back_near, mix_near = group(
         1, 0, second_near, known_near, rear, (back_near, mix_near), kept
     )
+    back_near, across = lax.optimization_barrier((back_near, across))
     row_grads = (
         back_near[:rows_dev].astype(F32)
         + swap_core(back_near[rows_dev:]).astype(F32)
@@ -1063,8 +1108,6 @@
         row_grads[:, width : width + experts]
         + row_grads[:, width + LANES // 2 : width + LANES // 2 + experts]
     )
-    rear_grads = weight_grads(hidden, after(grad, back_near))
-    rear_sums = scatter(*rear_grads)
     mix_near, mix_far, row_grads = lax.optimization_barrier((mix_near, mix_far, row_grads))
     mix_core = swap_core(mix_near[rows_dev:])
     mixture = mix_far[:rows_dev].astype(F32) + swap_core(mix_far[rows_dev:]).astype(F32)
@@ -1087,25 +1130,43 @@
     grad_branch = grad_middle.astype(BF16)
 
     grad_mixed = jnp.dot(grad_branch, outward_w, preferred_element_type=F32).astype(BF16)
-    grad_query, grad_keys, grad_values = attend_backward(
-        bounds,
-        key_owners,
-        place,
-        queries,
-        grad_mixed,
-        mixed_turned,
-        log_total,
-        key_pieces,
-        tables,
-        own_tables,
-    )
-    grad_pairs = jnp.concatenate([grad_keys, grad_values], axis=1)
-    key_sum = scatter_keys(grad_pairs, rows_dev).astype(BF16)
+    deltas = row_deltas(grad_mixed, mixed_turned)
+    grad_query = ()
+    got = None
+    for step in range(1, ctx_count + 1):
+        back = ctx_count - step
+        *grad_query, grad_pairs = attend_backward(
+            place,
+            ctx_place - back,
+            queries,
+            grad_mixed,
+            log_total,
+            deltas,
+            key_pieces[back],
+            tables,
+            own_tables,
+            grad_query,
+            back == 0,
+            (front_sum,) if step == 3 else (),
+        )
+        key_sum = grad_pairs.astype(F32)
+        if step > 1:
+            key_sum += got.astype(F32)
+        key_sum = key_sum.astype(BF16)
+        if back > 0:
+            pairs_back = [(i, i - 1) for i in range(back, ctx_count)]
+            got = lax.ppermute(key_sum, "ctx", pairs_back)
+        if step == 1:
+            thin = thin_grad_of(hidden, grad_pairs)
+        if step == 2:
+            wide = wide_grad_of(grad, grad_pairs)
+    (grad_query,) = grad_query
+    rear_sum = scatter(owner_rows(wide, thin))
     mixture, mix_core = lax.optimization_barrier((mixture, mix_core, key_sum))[:2]
     mixture = mixture.astype(F32) + mix_core.astype(F32) + mix_near[:rows_dev].astype(F32)
     output = (middle + mixture).astype(BF16)
     outward_grad = jnp.einsum("td,tc->dc", grad_branch, mixed_low, preferred_element_type=F32)
-    grad_project = jnp.concatenate([grad_query, key_sum], axis=1)
+    grad_project = jnp.concatenate([grad_query, key_sum[0], key_sum[1]], axis=1)
     attend_grad = jnp.einsum("tc,tp->cp", first_low, grad_project, preferred_element_type=F32)
     grad_first = lax.dot_general(grad_project, attend_w, NT, preferred_element_type=F32)
     first_norm, first_unit, first_scale = rms_forward(local_rows, gains_f[0])
@@ -1127,9 +1188,9 @@
     router_sum = first_sum[:, qkv : qkv + experts]
     gains_sum = first_sum[:, qkv + experts : qkv + experts + 2].T
     outward_sum = unpair_heads(outward_sum.T, 0)
+    front_sum, rear_sum, first_sum = lax.optimization_barrier((front_sum, rear_sum, first_sum))
     expand_sum, shrink_sum = (
-        jnp.concatenate(parts, axis=0)
-        for parts in zip(front_sums, rear_sums)
+        jnp.concatenate(parts, axis=0) for parts in zip(own_grads(front_sum), own_grads(rear_sum))
     )
     attend_new = adam_update(
         attend_master, attend_mean, attend_square, attend_sum, D ** (-0.5), DECAY

time: 1030 us -> 961 us (0.933)
  waiting for transfers between devices: 322 us -> 205 us
  local copies, waits for them, and re-layouts: 69.7 us -> 116 us
  Pallas kernels: 399 us -> 415 us
    ppermute x3, waiting for transfers between devices: 196 us -> 103 us  [body(): got = lax.ppermute(key_sum, 'ctx', pairs_back)]
    all_gather x1, waiting for transfers between devices: 0.02 us -> 53.9 us  [body(): lax.all_gather(after(packed[1], key_pieces[-1]), ('dp', 'ctx'), axis=0, t...]
    ppermute x4, waiting for transfers between devices: 58.9 us -> 6.16 us  [swap_far(): lax.ppermute(block, 'exp', [(i, i ^ 2) for i in range(lax.axis_size('exp'...]
    ppermute x3, waiting for transfers between devices: 44.6 us -> 15 us  [body(): lax.ppermute(key_pieces[-1], 'ctx', [(i, i + 1) for i in range(step, ctx_...]
    unnamed x197 -> x268, local copies, waits for them, and re-layouts: 29.9 us -> 53.5 us
    pallas_call x2 -> x9, Pallas kernels: 54.2 us -> 74.5 us  [the longest x4 41.2 us: attend_backward(): pl.pallas_call(functools.partial(attend_back_kernel, not before, final),...]
    concatenate x1 -> x4, local copies, waits for them, and re-layouts: 0.25 us -> 14.1 us  [the longest x2 12.3 us: owner_rows(): jnp.concatenate([wide.reshape(owners, width // owners, -1), thin], axis=2)]
    pallas_call x4, Pallas kernels: 136 us -> 125 us  [run_experts(): pl.pallas_call(functools.partial(experts_kernel, bool(before)), grid_spec...]
  transfers between devices with their start and end apart: 24 -> 22, of which waited for: 6 -> 9; matrix products, arithmetic and copies ran while one was open for 20% -> 22% of each run, Pallas kernels for 39% -> 40%
where the time goes in v3:
time: 961 us; the launch traced here: 951 us
  Pallas kernels  415 us (43%)
  waiting for transfers between devices  205 us (21%)
  local copies, waits for them, and re-layouts  116 us (12%)
  matrix products  87.6 us (9%)
  other arithmetic  71 us (7%)
  starting transfers between devices  40.5 us (4%)
  between operations  15.9 us (2%)
    pallas_call x4, Pallas kernels, run_experts(): pl.pallas_call(functools.partial(experts_kernel, bool(before)), grid_spec...  125 us
    pallas_call x1, Pallas kernels, dense_sum(): pl.pallas_call(functools.partial(dense_sum_kernel, tuple(starts)), in_spe...  116 us
    ppermute x3, waiting for transfers between devices, body(): got = lax.ppermute(key_sum, 'ctx', pairs_back)  103 us
    pallas_call x1, Pallas kernels, dense_gather(): pl.pallas_call(dense_gather_kernel, in_specs=[pl.BlockSpec(memory_space=p...  88.7 us
    all_gather x1, waiting for transfers between devices, body(): lax.all_gather(after(packed[1], key_pieces[-1]), ('dp', 'ctx'), axis=0, t...  53.9 us
    unnamed x268, local copies, waits for them, and re-layouts  53.5 us
    pallas_call x4, Pallas kernels, attend_backward(): pl.pallas_call(functools.partial(attend_back_kernel, not before, final),...  41.2 us
    dot_general x2, matrix products, wide_grad_of(): lax.dot_general(second_all, grad, contract, preferred_element_type=F32)  35.4 us
  transfers between devices with their start and end apart: 22, of which 9 were waited for; matrix products, arithmetic and copies ran while one was open for 22% of the time, Pallas kernels for 40%

profile of v3, /device:TPU:0, one launch (start us, length us, event | category | flops | bytes accessed | tf_op | source)
XLA Modules:
  0.0 951.3 jit_solution(3893991146993823707)
XLA Ops:
  17.0 2.9 convert_reduce_fusion
  21.0 88.7 %shard_map.422 = (bf16[2,4,2,2,48,2688]{5,4,3,2,1,0:T(8,128)(2,1)}, bf16[2,4,2,2,48,1536]{5,4,3,2,1,0:T(8,128)(2,1)}) custom-call(bf16[48,2688]{1,0:T(8,128)(2,1)} %concatenate.72.first_ref, bf16[48,1536]{1,0:T(8,128)(2,1)} %bitcast.148), custom_call_target="tpu_custom_call" | custom-call | bytes 12976128 | tf_op jit(solution)/shard_map/pallas_call | solution.py:621
  115.0 3.7 fusion.25
  122.5 3.4 copy-done.18
  125.9 10.6 %shard_map.423 = (bf16[512,1536]{1,0:T(8,128)(2,1)S(1)}, bf16[512,1024]{1,0:T(8,128)(2,1)S(1)}, bf16[512,1536]{1,0:T(8,128)(2,1)S(1)}) custom-call(bf16[512,1536]{1,0:T(8,128)(2,1)S(1)} %bitcast.116, f32[1,1536]{1,0:T(1,128)S(1)} %copy.220.gain_ref, bf16[1536,2688]{1,0:T(8,128)(2,1)S(1)} %bitcast.129, ...), custom_call_target="tpu_custom_call" | custom-call | flops 4026531840 | bytes 7864320 | tf_op jit(solution)/shard_map/pallas_call | solution.py:128
  139.5 27.5 %collective-permute-start = (bf16[512,1024]{1,0:T(8,128)(2,1)S(1)}, bf16[512,1024]{1,0:T(8,128)(2,1)}, u32[]{:S(2)}, u32[]{:S(2)}) collective-permute-start(bf16[512,1024]{1,0:T(8,128)(2,1)S(1)} %get-tuple-element.92.k_ref.v_ref), channel_id=1, source_target_pairs={{0,4},{4,8},{8,12},{1,5},{5,9},{9,13},{2,6},{6,10},{10,14},{3,7},{... | collective-permute-start | bytes 3145736 | tf_op jit(solution)/shard_map/ppermute | solution.py:1024
  169.2 17.4 %shard_map.424 = (f32[4,6,512]{2,1,0:T(8,128)S(1)}, f32[4,6,512]{2,1,0:T(8,128)S(1)}, f32[4,3,128,512]{3,2,1,0:T(8,128)S(1)}) custom-call(s32[2]{0:T(128)S(1)} %get-tuple-element.336.flag_ref, s32[1]{0:T(128)} %bitcast.16.owner_ref, s32[2,512]{1,0:T(2,128)S(1)} %pad_add_fusion.place_ref, bf16[512,1536]{1,0:T(8,128)(2,1)S(1)} %copy-done.40, ...), custom_call_target="tpu_custom_call" | custom-call | flops 16106127360 | bytes 6291456 | tf_op jit(solution)/shard_map/pallas_call | solution.py:269
  191.1 15.0 %collective-permute-done.k_ref.v_ref = bf16[512,1024]{1,0:T(8,128)(2,1)} collective-permute-done((bf16[512,1024]{1,0:T(8,128)(2,1)S(1)}, bf16[512,1024]{1,0:T(8,128)(2,1)}, u32[]{:S(2)}, u32[]{:S(2)}) %collective-permute-start) | collective-permute-done | bytes 1048608 | tf_op jit(solution)/shard_map/ppermute | solution.py:1024
  208.7 5.3 shard_map.425
  218.4 2.8 constant_dynamic-update-slice_fusion.3
  226.3 3.1 constant_dynamic-update-slice_fusion.2.do_ref.code_ref
  229.4 3.9 slice.257
  233.3 5.1 pad_maximum_fusion.2
  238.4 3.8 shard_map.427
  250.8 3.3 pad_maximum_fusion.4.h_ref
  254.0 30.7 %shard_map.428 = (bf16[2048,1024]{1,0:T(8,128)(2,1)}, bf16[2048,2048]{1,0:T(8,128)(2,1)}, bf16[1024,1664]{1,0:T(8,128)(2,1)}, bf16[1024,1536]{1,0:T(8,128)(2,1)}) custom-call(s32[1]{0:T(128)} %bitcast.22.first_ref, bf16[1024,1536]{1,0:T(8,128)(2,1)} %pad_maximum_fusion.4.h_ref, bf16[1024,1664]{1,0:T(8,128)(2,1)} %copy-done.66, ...), custom_call_target="tpu_custom_call" | custom-call | flops 28991029248 | bytes 25165824 | tf_op jit(solution)/shard_map/pallas_call | solution.py:896
  285.3 2.9 collective-permute-done.8
  291.1 30.9 %shard_map.429 = (bf16[2048,1024]{1,0:T(8,128)(2,1)}, bf16[2048,2048]{1,0:T(8,128)(2,1)}, bf16[1024,1664]{1,0:T(8,128)(2,1)}, bf16[1024,1536]{1,0:T(8,128)(2,1)}) custom-call(s32[1]{0:T(128)} %bitcast.22.first_ref, bf16[1024,1536]{1,0:T(8,128)(2,1)} %copy-done.92, ...), custom_call_target="tpu_custom_call", output_to_operand_aliasing={{0}: (6, {}), {1}: (7, {})} | custom-call | flops 28991029248 | bytes 25165824 | tf_op jit(solution)/shard_map/pallas_call | solution.py:896
  322.0 10.2 %convolution_convert_fusion.5 = bf16[1024,1536]{1,0:T(8,128)(2,1)S(1)} fusion(bf16[2048,1024]{1,0:T(8,128)(2,1)} %get-tuple-element.120, bf16[2048,1536]{1,0:T(8,128)(2,1)} %pad_maximum_fusion.2), kind=kOutput, calls=%fused_computation.20 | convolution fusion | flops 6444023808 | bytes 13631488 | tf_op jit(solution)/shard_map/dot_general | solution.py:1063
  334.2 6.1 concatenate.84
  340.3 17.3 %convolution_convert_fusion.3 = bf16[1536,2048]{1,0:T(8,128)(2,1)S(1)} fusion(bf16[2048,2048]{1,0:T(8,128)(2,1)} %get-tuple-element.118, bf16[512,1536]{1,0:T(8,128)(2,1)} %copy-done.85, bf16[512,1536]{1,0:T(8,128)(2,1)S(1)} %collective-permute-done.7, bf16[512,1536]{1,0:T(8,128)(2,1)} %collective-permute-done.6, bf16[512,1536]{1,0:T(8,128)(2,1)S(1)} %multiply_convert_fusion), kind=kOutput, calls=%fused_computation.8 | convolution fusion | flops 12913213440 | bytes 20971520 | tf_op jit(solution)/shard_map/dot_general | solution.py:1058
  357.7 4.6 pad_maximum_fusion.refs_3_
  362.3 53.9 %all-gather.7.cloned.1.call-done = bf16[16,576,512]{2,1,0:T(8,128)(2,1)} async-done(((bf16[2,576,512]{2,1,0:T(8,128)(2,1)}), bf16[16,576,512]{2,1,0:T(8,128)(2,1)}) %all-gather.7.cloned.1.call-update) | async-done | bytes 9437200 | tf_op jit(solution)/shard_map/all_gather | solution.py:1026
  416.2 31.9 %shard_map.430 = (bf16[2048,1024]{1,0:T(8,128)(2,1)}, bf16[2048,2048]{1,0:T(8,128)(2,1)}, bf16[1024,1664]{1,0:T(8,128)(2,1)}, bf16[1024,1536]{1,0:T(8,128)(2,1)}) custom-call(s32[1]{0:T(128)S(6)} %add.213.first_ref, bf16[1024,1536]{1,0:T(8,128)(2,1)} %copy-done.92, bf16[1024,1664]{1,0:T(8,128)(2,1)} %constant_dynamic-update-slice_fusion.2.do_ref.code_ref, ...), custom_call_target="tpu_custom_call" | custom-call | flops 28991029248 | bytes 25165824 | tf_op jit(solution)/shard_map/pallas_call | solution.py:896
  450.9 3.9 collective-permute-done.9
  458.7 31.7 %shard_map.431 = (bf16[2048,1024]{1,0:T(8,128)(2,1)}, bf16[2048,2048]{1,0:T(8,128)(2,1)}, bf16[1024,1664]{1,0:T(8,128)(2,1)}, bf16[1024,1536]{1,0:T(8,128)(2,1)}) custom-call(s32[1]{0:T(128)S(6)} %add.213.first_ref, bf16[1024,1536]{1,0:T(8,128)(2,1)} %pad_maximum_fusion.4.h_ref, ...), custom_call_target="tpu_custom_call", output_to_operand_aliasing={{0}: (9, {}), {1}: (10, {})} | custom-call | flops 28991029248 | bytes 25165824 | tf_op jit(solution)/shard_map/pallas_call | solution.py:896
  490.4 6.1 collective-permute-done.10
  508.4 3.7 convolution_convert_fusion.6.do_ref
  512.1 4.4 shard_map.432.delta_ref
  521.4 6.1 shard_map.433
  527.5 4.0 shard_map.434
  531.5 10.2 %convolution_convert_fusion.4 = bf16[1024,1536]{1,0:T(8,128)(2,1)S(1)} fusion(bf16[2048,1024]{1,0:T(8,128)(2,1)} %get-tuple-element.151, bf16[2048,1536]{1,0:T(8,128)(2,1)S(1)} %bitcast.137), kind=kOutput, calls=%fused_computation.19 | convolution fusion | flops 6444023808 | bytes 13631488 | tf_op jit(solution)/shard_map/dot_general | solution.py:1063
  543.6 6.2 concatenate.89
  549.8 18.0 %convolution_convert_fusion.2 = bf16[1536,2048]{1,0:T(8,128)(2,1)S(1)} fusion(bf16[2048,2048]{1,0:T(8,128)(2,1)} %get-tuple-element.149, bf16[512,1536]{1,0:T(8,128)(2,1)} %copy-done.85, bf16[512,1536]{1,0:T(8,128)(2,1)} %copy-done.84, bf16[512,1536]{1,0:T(8,128)(2,1)} %collective-permute-done.6, bf16[512,1536]{1,0:T(8,128)(2,1)S(1)} %copy-done.58), kind=kOutput, calls=%fused_computation.7 | convolution fusion | flops 12913213440 | bytes 20971520 | tf_op jit(solution)/shard_map/dot_general | solution.py:1058
  567.9 4.7 pad_maximum_fusion.1
  575.7 2.8 slice.233
  586.1 6.4 convolution_convert_fusion.1
  597.0 3.0 add_convert_fusion.2
  601.3 17.2 %reduce-scatter.3.cloned.1.call-done.refs_1_ = bf16[192,3072]{1,0:T(8,128)(2,1)} async-done(((bf16[1536,3072]{1,0:T(8,128)(2,1)}), bf16[192,3072]{1,0:T(8,128)(2,1)}) %reduce-scatter.3.cloned.1.call-update) | async-done | bytes 1179664 | tf_op jit(solution)/shard_map/reduce_scatter | solution.py:1075
  623.8 7.0 shard_map.435
  636.7 24.1 %shard_map.436 = (bf16[512,1536]{1,0:T(8,128)(2,1)S(1)}, bf16[2,512,512]{2,1,0:T(8,128)(2,1)S(1)}) custom-call(s32[2]{0:T(128)S(1)} %copy-done.24, s32[1]{0:T(128)} %bitcast.16.owner_ref, s32[2,512]{1,0:T(2,128)S(1)} %copy-done.22, bf16[512,1536]{1,0:T(8,128)(2,1)S(1)} %copy-done.44, bf16[512,1536]{1,0:T(8,128)(2,1)S(1)} %copy-done.10, ...), custom_call_target="tpu_custom_call" | custom-call | flops 24159191040 | bytes 6291456 | tf_op jit(solution)/shard_map/pallas_call | solution.py:416
  660.8 102.8 %collective-permute-done.17 = bf16[2,512,512]{2,1,0:T(8,128)(2,1)} collective-permute-done((bf16[2,512,512]{2,1,0:T(8,128)(2,1)S(1)}, bf16[2,512,512]{2,1,0:T(8,128)(2,1)}, u32[]{:S(2)}, u32[]{:S(2)}) %collective-permute-start.17) | collective-permute-done | bytes 1048608 | tf_op jit(solution)/shard_map/ppermute | solution.py:1158
  765.3 6.7 fusion.11
  772.3 8.1 convolution_convert_fusion
  780.8 116.0 %shard_map.437 = f32[48,4224]{1,0:T(8,128)S(1)} custom-call(bf16[2,4,2,2,48,2560]{5,4,3,2,1,0:T(8,128)(2,1)} %bitcast.135, bf16[2,4,2,2,48,128]{5,4,3,2,1,0:T(8,128)(2,1)S(1)} %bitcast.120, bf16[2,4,2,2,48,1536]{5,4,3,2,1,0:T(8,128)(2,1)S(1)} %bitcast.119), custom_call_target="tpu_custom_call" | custom-call | bytes 415236096 | tf_op jit(solution)/shard_map/pallas_call | solution.py:754
  914.7 5.4 fusion.16
  932.8 4.9 fusion.41
  939.0 5.4 fusion.44
  (426 shorter events, 141.7 us)
Async XLA Ops:
  7.2 246.8 %all-gather.5.cloned.1.call-start = ((), (), s32[]{:S(2)}) async-start(), calls=%async_computation.4 | async-start | bytes 10616832 | tf_op jit(solution)/shard_map/all_gather | solution.py:993
  12.0 404.2 %all-gather.7.cloned.1.call-start = ((), (), s32[]{:S(2)}) async-start(), calls=%async_computation.5 | async-start | bytes 10616832 | tf_op jit(solution)/shard_map/all_gather | solution.py:1026
  12.4 97.4 %copy-start.67 = (bf16[1,1,512,1536]{3,2,1,0:T(8,128)(2,1)S(1)}, bf16[1,1,512,1536]{3,2,1,0:T(8,128)(2,1)}, u32[]{:S(2)}) copy-start(bf16[1,1,512,1536]{3,2,1,0:T(8,128)(2,1)} %param.24) | copy-start | bytes 4718596
  20.0 93.6 %copy-start.76 = (s32[16,512]{0,1:T(8,128)}, s32[16,512]{0,1:T(8,128)S(1)}, u32[]{:S(2)}) copy-start(s32[16,512]{0,1:T(8,128)S(1)} %copy.222) | copy-start | bytes 98308
  20.2 94.6 %copy-start.93 = (pred[512,16]{1,0:T(32,128)(4,1)}, pred[512,16]{1,0:T(32,128)(4,1)S(1)}, u32[]{:S(2)}) copy-start(pred[512,16]{1,0:T(32,128)(4,1)S(1)} %copy.223) | copy-start | bytes 24580
  111.8 106.6 %collective-permute-start.4 = (bf16[512,1664]{1,0:T(8,128)(2,1)}, bf16[512,1664]{1,0:T(8,128)(2,1)}, u32[]{:S(2)}, u32[]{:S(2)}) collective-permute-start(bf16[512,1664]{1,0:T(8,128)(2,1)} %concatenate.75), channel_id=1, source_target_pairs={{0,2},{1,3},{2,0},{3,1},{4,6},{5,7},{6,4},{7,5},{8,10},{9,11},{10,... | collective-permute-start | bytes 5111816 | tf_op jit(solution)/shard_map/ppermute | solution.py:935
  112.3 101.7 %collective-permute-start.3 = (bf16[512,1664]{1,0:T(8,128)(2,1)}, bf16[512,1664]{1,0:T(8,128)(2,1)}, u32[]{:S(2)}, u32[]{:S(2)}) collective-permute-start(bf16[512,1664]{1,0:T(8,128)(2,1)} %concatenate.75), channel_id=1, source_target_pairs={{0,1},{1,0},{2,3},{3,2},{4,5},{5,4},{6,7},{7,6},{8,9},{9,8},{10,11... | collective-permute-start | bytes 5111816 | tf_op jit(solution)/shard_map/ppermute | solution.py:931
  114.8 130.3 %copy-start.97 = (f32[1536]{0:T(1024)}, f32[1536]{0:T(1024)S(1)}, u32[]{:S(2)}) copy-start(f32[1536]{0:T(1024)S(1)} %get-tuple-element.289) | copy-start | bytes 18436
  122.5 14.0 %copy-start.16 = (f32[512,128]{1,0:T(8,128)}, f32[512,128]{1,0:T(8,128)S(1)}, u32[]{:S(2)}) copy-start(f32[512,128]{1,0:T(8,128)S(1)} %constant_dynamic-slice_fusion.1.cos_ref.own_cos_ref) | copy-start | bytes 786436
  125.9 41.1 %copy-start.113 = (s32[1,1,9]{2,1,0:T(1,128)S(1)}, s32[1,1,9]{2,1,0:T(1,128)}, u32[]{:S(2)}) copy-start(s32[1,1,9]{2,1,0:T(1,128)} %param.25) | copy-start | bytes 112
  139.5 66.6 %collective-permute-start = (bf16[512,1024]{1,0:T(8,128)(2,1)S(1)}, bf16[512,1024]{1,0:T(8,128)(2,1)}, u32[]{:S(2)}, u32[]{:S(2)}) collective-permute-start(bf16[512,1024]{1,0:T(8,128)(2,1)S(1)} %get-tuple-element.92.k_ref.v_ref), channel_id=1, source_target_pairs={{0,4},{4,8},{8,12},{1,5},{5,9},{9,13},{2,6},{6,10},{10,14},{3,7},{... | collective-permute-start | bytes 3145736 | tf_op jit(solution)/shard_map/ppermute | solution.py:1024
  167.1 71.3 %copy-start.21 = (s32[2,512]{1,0:T(2,128)}, s32[2,512]{1,0:T(2,128)S(1)}, u32[]{:S(2)}) copy-start(s32[2,512]{1,0:T(2,128)S(1)} %pad_add_fusion.place_ref) | copy-start | bytes 12292
  167.3 39.5 %copy-start.25 = (s32[2]{0:T(128)}, s32[2]{0:T(128)S(1)}, u32[]{:S(2)}) copy-start(s32[2]{0:T(128)S(1)} %get-tuple-element.337.flag_ref) | copy-start | bytes 28
  189.3 17.5 %copy-start.41 = (bf16[512,1536]{1,0:T(8,128)(2,1)S(1)}, bf16[512,1536]{1,0:T(8,128)(2,1)}, u32[]{:S(2)}) copy-start(bf16[512,1536]{1,0:T(8,128)(2,1)} %copy-done.39) | copy-start | bytes 4718596
  191.0 30.9 %copy-start.27 = (s32[2]{0:T(128)}, s32[2]{0:T(128)S(1)}, u32[]{:S(2)}) copy-start(s32[2]{0:T(128)S(1)} %get-tuple-element.338.flag_ref) | copy-start | bytes 28
  191.0 47.4 %copy-start.29 = (s32[2]{0:T(128)}, s32[2]{0:T(128)S(1)}, u32[]{:S(2)}) copy-start(s32[2]{0:T(128)S(1)} %get-tuple-element.339.flag_ref) | copy-start | bytes 28
  206.1 15.2 %collective-permute-start.1 = (bf16[512,1024]{1,0:T(8,128)(2,1)}, bf16[512,1024]{1,0:T(8,128)(2,1)S(1)}, u32[]{:S(2)}, u32[]{:S(2)}) collective-permute-start(bf16[512,1024]{1,0:T(8,128)(2,1)} %collective-permute-done.k_ref.v_ref), channel_id=1, source_target_pairs={{4,8},{8,12},{5,9},{9,13},{6,10},{10,14},{7,11},{11,15},{20,24},{2... | collective-permute-start | bytes 3145736 | tf_op jit(solution)/shard_map/ppermute | solution.py:1024
  218.4 7.8 collective-permute-start.5
  221.2 4.9 collective-permute-start.2
  226.2 12.2 %copy-start.35 = (bf16[512,1024]{1,0:T(8,128)(2,1)}, bf16[512,1024]{1,0:T(8,128)(2,1)S(1)}, u32[]{:S(2)}) copy-start(bf16[512,1024]{1,0:T(8,128)(2,1)S(1)} %collective-permute-done.2.k_ref.v_ref) | copy-start | bytes 3145732
  226.2 392.3 %reduce-scatter.3.cloned.1.call-start = ((), (), s32[]{:S(2)}) async-start(), calls=%async_computation.2 | async-start | bytes 10616832 | tf_op jit(solution)/shard_map/reduce_scatter | solution.py:1075
  247.0 251.6 %copy-start.57 = (bf16[512,1536]{1,0:T(8,128)(2,1)}, bf16[512,1536]{1,0:T(8,128)(2,1)S(1)}, u32[]{:S(2)}) copy-start(bf16[512,1536]{1,0:T(8,128)(2,1)S(1)} %multiply_convert_fusion) | copy-start | bytes 4718596
  247.0 3.7 collective-permute-start.6
  247.6 37.1 %collective-permute-start.7 = (bf16[512,1536]{1,0:T(8,128)(2,1)S(1)}, bf16[512,1536]{1,0:T(8,128)(2,1)S(1)}, u32[]{:S(2)}, u32[]{:S(2)}) collective-permute-start(bf16[512,1536]{1,0:T(8,128)(2,1)S(1)} %multiply_convert_fusion), channel_id=1, source_target_pairs={{0,2},{1,3},{2,0},{3,1},{4,6},{5,7},{6,4},{7,5},{8,10},{9,11},{10,... | collective-permute-start | bytes 4718600 | tf_op jit(solution)/shard_map/ppermute | solution.py:935
  284.7 55.6 %copy-start.84 = (bf16[512,1536]{1,0:T(8,128)(2,1)}, bf16[512,1536]{1,0:T(8,128)(2,1)S(1)}, u32[]{:S(2)}) copy-start(bf16[512,1536]{1,0:T(8,128)(2,1)S(1)} %collective-permute-done.7) | copy-start | bytes 4718596
  284.7 3.5 collective-permute-start.8
  340.3 17.3 %copy-start.61 = (bf16[1536,1024]{1,0:T(8,128)(2,1)S(1)}, bf16[1536,1024]{1,0:T(8,128)(2,1)}, u32[]{:S(2)}) copy-start(bf16[1536,1024]{1,0:T(8,128)(2,1)} %concatenate.84) | copy-start | bytes 9437188
  450.8 3.9 collective-permute-start.9
  450.8 474.3 %reduce-scatter.5.cloned.1.call-start = ((), (), s32[]{:S(2)}) async-start(), calls=%async_computation.3 | async-start | bytes 10616832 | tf_op jit(solution)/shard_map/reduce_scatter | solution.py:1075
  457.1 39.4 %collective-permute-start.10 = (bf16[512,1664]{1,0:T(8,128)(2,1)S(1)}, bf16[512,1664]{1,0:T(8,128)(2,1)}, u32[]{:S(2)}, u32[]{:S(2)}) collective-permute-start(bf16[512,1664]{1,0:T(8,128)(2,1)S(1)} %add_convert_fusion), channel_id=1, source_target_pairs={{0,2},{1,3},{2,0},{3,1},{4,6},{5,7},{6,4},{7,5},{8,10},{9,11},{10,... | collective-permute-start | bytes 5111816 | tf_op jit(solution)/shard_map/ppermute | solution.py:935
  498.4 3.7 collective-permute-start.11
  531.5 10.3 %copy-start.12 = (bf16[2,512,512]{2,1,0:T(8,128)(2,1)}, bf16[2,512,512]{2,1,0:T(8,128)(2,1)S(1)}, u32[]{:S(2)}) copy-start(bf16[2,512,512]{2,1,0:T(8,128)(2,1)S(1)} %get-tuple-element.142) | copy-start | bytes 3145732
  549.8 18.0 %copy-start.60 = (bf16[1536,1024]{1,0:T(8,128)(2,1)S(1)}, bf16[1536,1024]{1,0:T(8,128)(2,1)}, u32[]{:S(2)}) copy-start(bf16[1536,1024]{1,0:T(8,128)(2,1)} %concatenate.89) | copy-start | bytes 9437188
  578.5 18.5 %collective-permute-start.12 = (bf16[512,1536]{1,0:T(8,128)(2,1)}, bf16[512,1536]{1,0:T(8,128)(2,1)}, u32[]{:S(2)}, u32[]{:S(2)}) collective-permute-start(bf16[512,1536]{1,0:T(8,128)(2,1)} %slice.233), channel_id=1, source_target_pairs={{0,1},{1,0},{2,3},{3,2},{4,5},{5,4},{6,7},{7,6},{8,9},{9,8},{10,11... | collective-permute-start | bytes 4718600 | tf_op jit(solution)/shard_map/ppermute | solution.py:931
  579.5 13.0 %collective-permute-start.15 = (bf16[2,512,512]{2,1,0:T(8,128)(2,1)}, bf16[2,512,512]{2,1,0:T(8,128)(2,1)}, u32[]{:S(2)}, u32[]{:S(2)}) collective-permute-start(bf16[2,512,512]{2,1,0:T(8,128)(2,1)} %get-tuple-element.143), channel_id=1, source_target_pairs={{12,8},{13,9},{14,10},{15,11},{28,24},{29,25},{30,26},{31,27}} | collective-permute-start | bytes 3145736 | tf_op jit(solution)/shard_map/ppermute | solution.py:1158
  586.1 326.2 %collective-permute-start.14 = (bf16[512,1536]{1,0:T(8,128)(2,1)}, bf16[512,1536]{1,0:T(8,128)(2,1)}, u32[]{:S(2)}, u32[]{:S(2)}) collective-permute-start(bf16[512,1536]{1,0:T(8,128)(2,1)} %slice.234), channel_id=1, source_target_pairs={{0,1},{1,0},{2,3},{3,2},{4,5},{5,4},{6,7},{7,6},{8,9},{9,8},{10,11... | collective-permute-start | bytes 4718600 | tf_op jit(solution)/shard_map/ppermute | solution.py:931
  595.2 23.3 %copy-start.20 = (f32[4,6,512]{2,1,0:T(8,128)S(1)}, f32[4,6,512]{2,1,0:T(8,128)}, u32[]{:S(2)}) copy-start(f32[4,6,512]{2,1,0:T(8,128)} %shard_map.432.delta_ref) | copy-start | bytes 147460
  595.2 23.3 %copy-start.26 = (s32[2]{0:T(128)S(1)}, s32[2]{0:T(128)}, u32[]{:S(2)}) copy-start(s32[2]{0:T(128)} %copy-done.25) | copy-start | bytes 28
  595.2 35.7 %collective-permute-start.16 = (bf16[2,512,512]{2,1,0:T(8,128)(2,1)}, bf16[2,512,512]{2,1,0:T(8,128)(2,1)}, u32[]{:S(2)}, u32[]{:S(2)}) collective-permute-start(bf16[2,512,512]{2,1,0:T(8,128)(2,1)} %add_convert_fusion.5), channel_id=1, source_target_pairs={{8,4},{12,8},{9,5},{13,9},{10,6},{14,10},{11,7},{15,11},{24,20},{2... | collective-permute-start | bytes 3145736 | tf_op jit(solution)/shard_map/ppermute | solution.py:1158
  600.0 312.4 %collective-permute-start.13 = (bf16[512,1536]{1,0:T(8,128)(2,1)}, bf16[512,1536]{1,0:T(8,128)(2,1)}, u32[]{:S(2)}, u32[]{:S(2)}) collective-permute-start(bf16[512,1536]{1,0:T(8,128)(2,1)} %add_convert_fusion.2), channel_id=1, source_target_pairs={{0,2},{1,3},{2,0},{3,1},{4,6},{5,7},{6,4},{7,5},{8,10},{9,11},{10,... | collective-permute-start | bytes 4718600 | tf_op jit(solution)/shard_map/ppermute | solution.py:935
  633.3 130.4 %collective-permute-start.17 = (bf16[2,512,512]{2,1,0:T(8,128)(2,1)S(1)}, bf16[2,512,512]{2,1,0:T(8,128)(2,1)}, u32[]{:S(2)}, u32[]{:S(2)}) collective-permute-start(bf16[2,512,512]{2,1,0:T(8,128)(2,1)S(1)} %add_convert_fusion.4), channel_id=1, source_target_pairs={{4,0},{8,4},{12,8},{5,1},{9,5},{13,9},{6,2},{10,6},{14,10},{7,3},{... | collective-permute-start | bytes 3145736 | tf_op jit(solution)/shard_map/ppermute | solution.py:1158
  634.6 130.7 %slice-start.5 = ((s8[8257536]{0:T(1024)(128)(4,1)}), s8[4194304]{0:T(1024)(128)(4,1)S(1)}, s32[]{:S(2)}) async-start(s8[8257536]{0:T(1024)(128)(4,1)} %bitcast.130), calls=%async_computation.11 | async-start | bytes 8388608
  636.7 128.6 %slice-start.6 = ((s8[8257536]{0:T(1024)(128)(4,1)}), s8[4063232]{0:T(1024)(128)(4,1)S(1)}, s32[]{:S(2)}) async-start(s8[8257536]{0:T(1024)(128)(4,1)} %bitcast.130), calls=%async_computation.12 | async-start | bytes 8126464
  660.8 111.2 %copy-start.47 = (bf16[512,1536]{1,0:T(8,128)(2,1)}, bf16[512,1536]{1,0:T(8,128)(2,1)S(1)}, u32[]{:S(2)}) copy-start(bf16[512,1536]{1,0:T(8,128)(2,1)S(1)} %get-tuple-element.146) | copy-start | bytes 4718596
  660.8 104.4 %copy-start.104 = (f32[1536]{0:T(1024)S(1)}, f32[1536]{0:T(1024)}, u32[]{:S(2)}) copy-start(f32[1536]{0:T(1024)} %get-tuple-element.288) | copy-start | bytes 18436
  896.8 10.8 %copy-start.2 = (f32[48,4224]{1,0:T(8,128)}, f32[48,4224]{1,0:T(8,128)S(1)}, u32[]{:S(2)}) copy-start(f32[48,4224]{1,0:T(8,128)S(1)} %shard_map.437) | copy-start | bytes 2433028
  900.4 12.0 %copy-start.110 = (f32[512]{0:T(512)S(1)}, f32[512]{0:T(512)}, u32[]{:S(2)}) copy-start(f32[512]{0:T(512)} %get-tuple-element.287) | copy-start | bytes 6148
  900.4 12.0 %copy-start.90 = (f32[1536,48]{0,1:T(8,128)S(1)}, f32[1536,48]{0,1:T(8,128)}, u32[]{:S(2)}) copy-start(f32[1536,48]{0,1:T(8,128)} %param.31) | copy-start | bytes 884740
  (101 other events, 375.4 us)
Sparse Core Ops, SparseCore 0:
  12.1 189.3 all-gather.4
  226.3 189.7 all-gather.6
  451.0 167.4 reduce-scatter.2
  621.9 227.7 reduce-scatter.4

commit v4 on v3

--- a/solution.py
+++ b/solution.py
@@ -55,6 +55,88 @@
         first_hat / (jnp.sqrt(second_hat) + ADAM_EPSILON) + decay * master
     )
     return (first_new, second_new, master_new, master_new.astype(jnp.bfloat16))
+
+
+def adam_kernel(rate, decay, master_ref, mean_ref, square_ref, grad_ref, *refs):
+    outs = refs[len(refs) - 4 :]
+    grad = grad_ref[...].reshape(master_ref.shape).astype(F32)
+    news = adam_update(master_ref[...], mean_ref[...], square_ref[...], grad, rate, decay)
+    for out, new in zip(outs, news):
+        out[...] = new
+
+
+def dense_adam_kernel(experts, rates, sum_ref, *refs):
+    groups = [refs[3 * i : 3 * i + 3] for i in range(4)]
+    results = [refs[12 + 4 * i : 16 + 4 * i] for i in range(4)]
+    rows = sum_ref.shape[0]
+    lane = lax.broadcasted_iota(jnp.int32, (rows, LANES), 1)
+    qkv = (HEADS + 2 * KVH) * HD
+
+    def update(index, cut, grad):
+        rate, decay = rates[index]
+        news = adam_update(*(ref[cut] for ref in groups[index]), grad, rate, decay)
+        for out, new in zip(results[index], news):
+            out[cut] = new
+
+    def columns(start):
+        return (slice(None), slice(start, start + LANES))
+
+    def place(head):
+        group, member = head // GROUP, head % GROUP
+        return (GROUP * (group // 2) + member, group % 2)
+
+    for index, begin in ((0, 0), (1, qkv + LANES)):
+        for pair in range(HEADS // 2):
+            parts = []
+            for side in range(2):
+                spot, part = place(2 * pair + side)
+                block = sum_ref[columns(begin + spot * LANES)]
+                parts.append(block if part == side else pltpu.roll(block, HD, 1))
+            update(index, columns(pair * LANES), jnp.where(lane < HD, parts[0], parts[1]))
+    for start in range(HEADS * HD, qkv, LANES):
+        update(0, columns(start), sum_ref[columns(start)])
+    thin = sum_ref[columns(qkv)]
+    whole = (slice(None), slice(None))
+    update(2, whole, thin[:, :experts])
+    update(3, whole, thin.T[experts : experts + 2])
+
+
+def dense_adam(total, arrays, rates):
+    shapes = []
+    for master, _, _ in arrays:
+        shapes += [jax.ShapeDtypeStruct(master.shape, F32)] * 3
+        shapes.append(jax.ShapeDtypeStruct(master.shape, BF16))
+    outs = pl.pallas_call(
+        functools.partial(dense_adam_kernel, arrays[2][0].shape[1], rates),
+        in_specs=[pl.BlockSpec(memory_space=pltpu.VMEM)] * 13,
+        out_specs=[pl.BlockSpec(memory_space=pltpu.VMEM)] * 16,
+        out_shape=shapes,
+        compiler_params=pltpu.CompilerParams(vmem_limit_bytes=48 * 1024 * 1024),
+        cost_estimate=pl.CostEstimate(
+            flops=20 * total.size, bytes_accessed=40 * total.size, transcendentals=0
+        ),
+    )(total, *(array for group in arrays for array in group))
+    return [outs[4 * i : 4 * i + 4] for i in range(4)]
+
+
+def adam_group(arrays, grad, grad_spec, first, tiles, rate, decay, kept):
+    shape = arrays[0].shape
+    rows = shape[1] // tiles
+    own = pl.BlockSpec((1, rows, shape[2]), lambda i, j: (first + i, j, 0))
+    count = shape[0] // 2
+    whole = [pl.BlockSpec(memory_space=pl.ANY)] * len(kept)
+    return pl.pallas_call(
+        functools.partial(adam_kernel, rate, decay),
+        grid=(count, tiles),
+        in_specs=[own, own, own, grad_spec, *whole],
+        out_specs=[own] * 4,
+        out_shape=[jax.ShapeDtypeStruct(shape, F32)] * 3 + [jax.ShapeDtypeStruct(shape, BF16)],
+        input_output_aliases={4 + i: i for i in range(len(kept))},
+        compiler_params=pltpu.CompilerParams(vmem_limit_bytes=40 * 1024 * 1024),
+        cost_estimate=pl.CostEstimate(
+            flops=10 * arrays[0].size, bytes_accessed=14 * arrays[0].size, transcendentals=0
+        ),
+    )(*arrays, grad, *kept)
 
 
 def pair_heads(block, axis):
@@ -275,7 +357,7 @@
                 pl.BlockSpec((2, sub_rows), lambda p, s, *_: (0, s)),
                 wide,
                 pl.BlockSpec((rows, LANES), lambda p, s, *_: (0, p)),
-                pl.BlockSpec((rows, LANES), lambda p, s, *_: (0, PAIRS + p)),
+                pl.BlockSpec((rows, LANES), lambda p, s, *_: (0, p)),
                 *([line, line, turned] if before else []),
             ],
             out_specs=[wide, line, turned] if final else [line, line, turned],
@@ -290,7 +372,7 @@
         cost_estimate=pl.CostEstimate(
             flops=40 * rows * rows * D, bytes_accessed=8 * rows * D, transcendentals=0
         ),
-    )(chunk_flags(place, owner, sub_rows), owner[None], place, q, piece, piece, *before)
+    )(chunk_flags(place, owner, sub_rows), owner[None], place, q, *piece, *before)
 
 
 def delta_kernel(do_ref, ot_ref, delta_ref):
@@ -425,7 +507,7 @@
                 line,
                 line,
                 pl.BlockSpec((rows, LANES), lambda p, s, *_: (0, p)),
-                pl.BlockSpec((rows, LANES), lambda p, s, *_: (0, PAIRS + p)),
+                pl.BlockSpec((rows, LANES), lambda p, s, *_: (0, p)),
                 far,
                 far,
                 near,
@@ -459,8 +541,7 @@
         do,
         lse,
         delta,
-        piece,
-        piece,
+        *piece,
         *tables,
         *own_tables,
         *before,
@@ -1018,12 +1099,11 @@
         lax.dynamic_slice_in_dim(table, ctx_place * rows_dev, rows_dev, 0) for table in tables
     )
     queries, pairs, first_low = project(local_low, gains_f[0:1], first_w, *own_tables)
-    key_pieces = [pairs]
+    key_pieces = [(pairs[:, : KVH * HD], pairs[:, KVH * HD :])]
     for step in range(ctx_count - 1):
-        key_pieces.append(
-            lax.ppermute(key_pieces[-1], "ctx", [(i, i + 1) for i in range(step, ctx_count - 1)])
-        )
-    rear = lax.all_gather(after(packed[1], key_pieces[-1]), ("dp", "ctx"), axis=0, tiled=False)
+        route = [(i, i + 1) for i in range(step, ctx_count - 1)]
+        key_pieces.append(tuple(lax.ppermute(part, "ctx", route) for part in key_pieces[-1]))
+    rear = lax.all_gather(after(packed[1], *key_pieces[-1]), ("dp", "ctx"), axis=0, tiled=False)
     state = ()
     for step in range(ctx_count):
         state = attend_forward(
@@ -1074,10 +1154,31 @@
     def scatter(both):
         return lax.psum_scatter(both, ("dp", "ctx"), scatter_dimension=0, tiled=True)
 
-    def own_grads(total):
-        wide = total[:, : half * 2 * FF].reshape(-1, half, 2 * FF)
+    def update_experts(total, first, expand_kept, shrink_kept):
+        rows = total.shape[0]
+        tiles = 2 if rows % 32 == 0 else 1
+        expand = adam_group(
+            (expand_master, expand_mean, expand_square),
+            total,
+            pl.BlockSpec((rows // tiles, 2 * FF), lambda i, j: (j, i)),
+            first,
+            tiles,
+            D ** (-0.5),
+            DECAY,
+            expand_kept,
+        )
         thin = total[:, half * 2 * FF :].reshape(half, FF // owners, width)
-        return (jnp.swapaxes(wide, 0, 1).astype(F32), thin.astype(F32))
+        shrink = adam_group(
+            (shrink_master, shrink_mean, shrink_square),
+            thin,
+            pl.BlockSpec((1, FF // owners, width), lambda i, j: (i, j, 0)),
+            first,
+            1,
+            (FF // 32) ** (-0.5),
+            DECAY,
+            shrink_kept,
+        )
+        return (expand, shrink)
 
     *kept, back_near, mix_near = group(0, 0, second_near, known_near, front, (), ())
     second_far = after(second_far, back_near)
@@ -1133,6 +1234,8 @@
     deltas = row_deltas(grad_mixed, mixed_turned)
     grad_query = ()
     got = None
+    expand_new, shrink_new = update_experts(front_sum, 0, (), ())
+    early = (expand_new[0], shrink_new[0])
     for step in range(1, ctx_count + 1):
         back = ctx_count - step
         *grad_query, grad_pairs = attend_backward(
@@ -1147,7 +1250,7 @@
             own_tables,
             grad_query,
             back == 0,
-            (front_sum,) if step == 3 else (),
+            (front_sum,) if step == 3 else early if back == 0 else (),
         )
         key_sum = grad_pairs.astype(F32)
         if step > 1:
@@ -1155,7 +1258,7 @@
         key_sum = key_sum.astype(BF16)
         if back > 0:
             pairs_back = [(i, i - 1) for i in range(back, ctx_count)]
-            got = lax.ppermute(key_sum, "ctx", pairs_back)
+            got = jnp.stack([lax.ppermute(key_sum[i], "ctx", pairs_back) for i in range(2)])
         if step == 1:
             thin = thin_grad_of(hidden, grad_pairs)
         if step == 2:
@@ -1181,33 +1284,39 @@
         axis=1,
     )
     first_sum = dense_sum(attend_grad.astype(BF16), thin_grad, outward_grad.astype(BF16))
-    outward_sum = first_sum[:, qkv + LANES :]
-    attend_sum = jnp.concatenate(
-        [unpair_heads(first_sum[:, :query_end], 1), first_sum[:, query_end:qkv]], axis=1
-    )
-    router_sum = first_sum[:, qkv : qkv + experts]
-    gains_sum = first_sum[:, qkv + experts : qkv + experts + 2].T
-    outward_sum = unpair_heads(outward_sum.T, 0)
-    front_sum, rear_sum, first_sum = lax.optimization_barrier((front_sum, rear_sum, first_sum))
-    expand_sum, shrink_sum = (
-        jnp.concatenate(parts, axis=0) for parts in zip(own_grads(front_sum), own_grads(rear_sum))
-    )
-    attend_new = adam_update(
-        attend_master, attend_mean, attend_square, attend_sum, D ** (-0.5), DECAY
-    )
-    outward_new = adam_update(
-        outward_master, outward_mean, outward_square, outward_sum, 4.0 * D ** (-0.5), DECAY
-    )
-    router_new = adam_update(
-        router_master, router_mean, router_square, router_sum, 0.5 * D ** (-0.5), DECAY
-    )
-    gains_new = adam_update(gains_master, gains_mean, gains_square, gains_sum, 0.6, 0.0)
-    expand_new = adam_update(
-        expand_master, expand_mean, expand_square, expand_sum, D ** (-0.5), DECAY
-    )
-    shrink_new = adam_update(
-        shrink_master, shrink_mean, shrink_square, shrink_sum, (FF // 32) ** (-0.5), DECAY
-    )
+    rear_sum, first_sum = lax.optimization_barrier((rear_sum, first_sum))
+    expand_new, shrink_new = update_experts(rear_sum, half, expand_new, shrink_new)
+    rates = ((D ** (-0.5), DECAY), (4.0 * D ** (-0.5), DECAY), (0.5 * D ** (-0.5), DECAY), (0.6, 0.0))
+    if split_devices():
+        attend_new, outward_new, router_new, gains_new = dense_adam(
+            first_sum,
+            (
+                (attend_master, attend_mean, attend_square),
+                (outward_master.T, outward_mean.T, outward_square.T),
+                (router_master, router_mean, router_square),
+                (gains_master, gains_mean, gains_square),
+            ),
+            rates,
+        )
+        outward_new = [new.T for new in outward_new]
+    else:
+        outward_sum = first_sum[:, qkv + LANES :]
+        attend_sum = jnp.concatenate(
+            [unpair_heads(first_sum[:, :query_end], 1), first_sum[:, query_end:qkv]], axis=1
+        )
+        router_sum = first_sum[:, qkv : qkv + experts]
+        gains_sum = first_sum[:, qkv + experts : qkv + experts + 2].T
+        outward_sum = unpair_heads(outward_sum.T, 0)
+        attend_new = adam_update(
+            attend_master, attend_mean, attend_square, attend_sum, D ** (-0.5), DECAY
+        )
+        outward_new = adam_update(
+            outward_master, outward_mean, outward_square, outward_sum, 4.0 * D ** (-0.5), DECAY
+        )
+        router_new = adam_update(
+            router_master, router_mean, router_square, router_sum, 0.5 * D ** (-0.5), DECAY
+        )
+        gains_new = adam_update(gains_master, gains_mean, gains_square, gains_sum, 0.6, 0.0)
     return (
         output[None, None],
         input_grad[None, None],

time: 961 us -> 954 us (level)
  waiting for transfers between devices: 205 us -> 186 us
  other arithmetic: 71 us -> 52.5 us
  local copies, waits for them, and re-layouts: 116 us -> 131 us
    unnamed x268 -> x331, local copies, waits for them, and re-layouts: 53.5 us -> 80.2 us
    ppermute x6 -> x12, waiting for transfers between devices: 118 us -> 95.6 us  [the longest x6 81.4 us: body(): lax.ppermute(key_sum[i], 'ctx', pairs_back)]
    convert_element_type x6 -> x0, other arithmetic: 14.8 us -> none  [adam_update(): return (first_new, second_new, master_new, master_new.astype(jnp.bfloat16))]
    pallas_call x0 -> x5, Pallas kernels: none -> 12 us  [the longest x4 9.88 us: adam_group(): pl.pallas_call(functools.partial(adam_kernel, rate, decay), grid=(count,...]
    ppermute x6 -> x12, starting transfers between devices: 33.7 us -> 37.9 us  [the longest x6 30.6 us: body(): lax.ppermute(part, 'ctx', route)]
  transfers between devices with their start and end apart: 22 -> 28, of which waited for: 9 -> 10; matrix products, arithmetic and copies ran while one was open for 22% -> 20% of each run, Pallas kernels for 40% -> 41%
where the time goes in v4:
time: 954 us; the launch traced here: 943 us
  Pallas kernels  423 us (44%)
  waiting for transfers between devices  186 us (19%)
  local copies, waits for them, and re-layouts  131 us (14%)
  matrix products  88.2 us (9%)
  other arithmetic  52.5 us (6%)
  starting transfers between devices  46.5 us (5%)
  between operations  15.9 us (2%)
    pallas_call x4, Pallas kernels, run_experts(): pl.pallas_call(functools.partial(experts_kernel, bool(before)), grid_spec...  126 us
    pallas_call x1, Pallas kernels, dense_sum(): pl.pallas_call(functools.partial(dense_sum_kernel, tuple(starts)), in_spe...  116 us
    pallas_call x1, Pallas kernels, dense_gather(): pl.pallas_call(dense_gather_kernel, in_specs=[pl.BlockSpec(memory_space=p...  88.5 us
    ppermute x6, waiting for transfers between devices, body(): lax.ppermute(key_sum[i], 'ctx', pairs_back)  81.4 us
    unnamed x331, local copies, waits for them, and re-layouts  80.2 us
    all_gather x1, waiting for transfers between devices, body(): lax.all_gather(after(packed[1], *key_pieces[-1]), ('dp', 'ctx'), axis=0,...  49.5 us
    pallas_call x4, Pallas kernels, attend_backward(): pl.pallas_call(functools.partial(attend_back_kernel, not before, final),...  38.3 us
    dot_general x2, matrix products, wide_grad_of(): lax.dot_general(second_all, grad, contract, preferred_element_type=F32)  34.8 us
  transfers between devices with their start and end apart: 28, of which 10 were waited for; matrix products, arithmetic and copies ran while one was open for 20% of the time, Pallas kernels for 41%

profile of v4, /device:TPU:0, one launch (start us, length us, event | category | flops | bytes accessed | tf_op | source)
XLA Modules:
  0.0 943.1 jit_solution(2258521910720157053)
XLA Ops:
  16.3 3.2 convert_reduce_fusion
  20.6 88.5 %shard_map.422 = (bf16[2,4,2,2,48,2688]{5,4,3,2,1,0:T(8,128)(2,1)}, bf16[2,4,2,2,48,1536]{5,4,3,2,1,0:T(8,128)(2,1)}) custom-call(bf16[48,2688]{1,0:T(8,128)(2,1)} %concatenate.57.first_ref, bf16[48,1536]{1,0:T(8,128)(2,1)} %bitcast.135), custom_call_target="tpu_custom_call" | custom-call | bytes 12976128 | tf_op jit(solution)/shard_map/pallas_call | solution.py:702
  116.0 3.7 fusion.20
  123.4 3.4 copy-done.58
  126.9 10.6 %shard_map.423 = (bf16[512,1536]{1,0:T(8,128)(2,1)S(1)}, bf16[512,1024]{1,0:T(8,128)(2,1)S(1)}, bf16[512,1536]{1,0:T(8,128)(2,1)S(1)}) custom-call(bf16[512,1536]{1,0:T(8,128)(2,1)S(1)} %bitcast.108, f32[1,1536]{1,0:T(1,128)S(1)} %copy.152.gain_ref, bf16[1536,2688]{1,0:T(8,128)(2,1)S(1)} %bitcast.124, ...), custom_call_target="tpu_custom_call" | custom-call | flops 4026531840 | bytes 7864320 | tf_op jit(solution)/shard_map/pallas_call | solution.py:210
  139.4 25.1 %collective-permute-start = (bf16[512,512]{1,0:T(8,128)(2,1)S(1)}, bf16[512,512]{1,0:T(8,128)(2,1)S(1)}, u32[]{:S(2)}, u32[]{:S(2)}) collective-permute-start(bf16[512,512]{1,0:T(8,128)(2,1)S(1)} %get-tuple-element.367.k_ref), channel_id=1, source_target_pairs={{0,4},{4,8},{8,12},{1,5},{5,9},{9,13},{2,6},{6,10},{10,14},{3,7},{... | collective-permute-start | bytes 1572872 | tf_op jit(solution)/shard_map/ppermute | solution.py:1105
  169.0 17.0 %shard_map.424 = (f32[4,6,512]{2,1,0:T(8,128)S(1)}, f32[4,6,512]{2,1,0:T(8,128)S(1)}, f32[4,3,128,512]{3,2,1,0:T(8,128)S(1)}) custom-call(s32[2]{0:T(128)S(1)} %get-tuple-element.378.flag_ref, s32[1]{0:T(128)} %bitcast.16.owner_ref, s32[2,512]{1,0:T(2,128)S(1)} %pad_add_fusion.place_ref, bf16[512,1536]{1,0:T(8,128)(2,1)S(1)} %copy-done.92, ...), custom_call_target="tpu_custom_call" | custom-call | flops 16106127360 | bytes 6291456 | tf_op jit(solution)/shard_map/pallas_call | solution.py:351
  188.2 2.9 constant_dynamic-update-slice_fusion.1
  191.8 14.1 %collective-permute-done.3.v_ref = bf16[512,512]{1,0:T(8,128)(2,1)} collective-permute-done((bf16[512,512]{1,0:T(8,128)(2,1)S(1)}, bf16[512,512]{1,0:T(8,128)(2,1)}, u32[]{:S(2)}, u32[]{:S(2)}) %collective-permute-start.3) | collective-permute-done | bytes 524320 | tf_op jit(solution)/shard_map/ppermute | solution.py:1105
  208.6 5.1 shard_map.425
  219.4 3.1 constant_dynamic-update-slice_fusion.do_ref.code_ref
  231.5 5.1 pad_maximum_fusion.2
  236.7 3.7 shard_map.427
  248.9 3.3 pad_maximum_fusion.4.h_ref
  252.1 30.7 %shard_map.428 = (bf16[2048,1024]{1,0:T(8,128)(2,1)}, bf16[2048,2048]{1,0:T(8,128)(2,1)}, bf16[1024,1664]{1,0:T(8,128)(2,1)}, bf16[1024,1536]{1,0:T(8,128)(2,1)}) custom-call(s32[1]{0:T(128)} %bitcast.22.first_ref, bf16[1024,1536]{1,0:T(8,128)(2,1)} %pad_maximum_fusion.4.h_ref, bf16[1024,1664]{1,0:T(8,128)(2,1)} %constant_dynamic-update-slice_fusion.do_ref.code_ref, ...), custom_call_target="tpu_custom_call" | custom-call | flops 28991029248 | bytes 25165824 | tf_op jit(solution)/shard_map/pallas_call | solution.py:977
  283.4 2.9 collective-permute-done.11
  289.2 31.1 %shard_map.429 = (bf16[2048,1024]{1,0:T(8,128)(2,1)}, bf16[2048,2048]{1,0:T(8,128)(2,1)}, bf16[1024,1664]{1,0:T(8,128)(2,1)}, bf16[1024,1536]{1,0:T(8,128)(2,1)}) custom-call(s32[1]{0:T(128)} %bitcast.22.first_ref, bf16[1024,1536]{1,0:T(8,128)(2,1)} %copy-done.135, bf16[1024,1664]{1,0:T(8,128)(2,1)} %copy-done.121, ...), custom_call_target="tpu_custom_call", output_to_operand_aliasing={{0}: (6, {}), {1}: (7, {})} | custom-call | flops 28991029248 | bytes 25165824 | tf_op jit(solution)/shard_map/pallas_call | solution.py:977
  320.3 10.2 %convolution_convert_fusion.5 = bf16[1024,1536]{1,0:T(8,128)(2,1)S(1)} fusion(bf16[2048,1024]{1,0:T(8,128)(2,1)} %get-tuple-element.152, bf16[2048,1536]{1,0:T(8,128)(2,1)} %pad_maximum_fusion.2), kind=kOutput, calls=%fused_computation.18 | convolution fusion | flops 6444023808 | bytes 13631488 | tf_op jit(solution)/shard_map/dot_general | solution.py:1143
  332.5 5.9 concatenate.69
  338.5 17.0 %convolution_convert_fusion.3 = bf16[1536,2048]{1,0:T(8,128)(2,1)S(1)} fusion(bf16[2048,2048]{1,0:T(8,128)(2,1)} %get-tuple-element.150, bf16[512,1536]{1,0:T(8,128)(2,1)} %copy-done.132, bf16[512,1536]{1,0:T(8,128)(2,1)S(1)} %collective-permute-done.10, bf16[512,1536]{1,0:T(8,128)(2,1)} %collective-permute-done.9, ...), kind=kOutput, calls=%fused_computation.8 | convolution fusion | flops 12913213440 | bytes 20971520 | tf_op jit(solution)/shard_map/dot_general | solution.py:1138
  355.5 4.6 pad_maximum_fusion.refs_3_
  360.2 49.5 %all-gather.7.cloned.1.call-done = bf16[16,576,512]{2,1,0:T(8,128)(2,1)} async-done(((bf16[2,576,512]{2,1,0:T(8,128)(2,1)}), bf16[16,576,512]{2,1,0:T(8,128)(2,1)}) %all-gather.7.cloned.1.call-update) | async-done | bytes 9437200 | tf_op jit(solution)/shard_map/all_gather | solution.py:1106
  409.7 32.0 %shard_map.430 = (bf16[2048,1024]{1,0:T(8,128)(2,1)}, bf16[2048,2048]{1,0:T(8,128)(2,1)}, bf16[1024,1664]{1,0:T(8,128)(2,1)}, bf16[1024,1536]{1,0:T(8,128)(2,1)}) custom-call(s32[1]{0:T(128)S(6)} %add.123.first_ref, bf16[1024,1536]{1,0:T(8,128)(2,1)} %copy-done.135, bf16[1024,1664]{1,0:T(8,128)(2,1)} %copy-done.121, bf16[1024,1664]{1,0:T(8,128)(2,1)} %copy-done.121, ...), custom_call_target="tpu_custom_call" | custom-call | flops 28991029248 | bytes 25165824 | tf_op jit(solution)/shard_map/pallas_call | solution.py:977
  441.6 2.8 slice.234
  444.5 3.9 collective-permute-done.12
  452.2 31.8 %shard_map.431 = (bf16[2048,1024]{1,0:T(8,128)(2,1)}, bf16[2048,2048]{1,0:T(8,128)(2,1)}, bf16[1024,1664]{1,0:T(8,128)(2,1)}, bf16[1024,1536]{1,0:T(8,128)(2,1)}) custom-call(s32[1]{0:T(128)S(6)} %add.123.first_ref, bf16[1024,1536]{1,0:T(8,128)(2,1)} %pad_maximum_fusion.4.h_ref, ...), custom_call_target="tpu_custom_call", output_to_operand_aliasing={{0}: (9, {}), {1}: (10, {})} | custom-call | flops 28991029248 | bytes 25165824 | tf_op jit(solution)/shard_map/pallas_call | solution.py:977
  484.0 6.1 collective-permute-done.13
  501.9 3.7 convolution_convert_fusion.6.do_ref
  505.6 4.4 shard_map.432.delta_ref
  515.8 4.0 shard_map.433
  520.8 3.8 shard_map.434
  524.6 10.2 %convolution_convert_fusion.4 = bf16[1024,1536]{1,0:T(8,128)(2,1)S(1)} fusion(bf16[2048,1024]{1,0:T(8,128)(2,1)} %get-tuple-element.184, bf16[2048,1536]{1,0:T(8,128)(2,1)S(1)} %bitcast.129), kind=kOutput, calls=%fused_computation.17 | convolution fusion | flops 6444023808 | bytes 13631488 | tf_op jit(solution)/shard_map/dot_general | solution.py:1143
  536.7 6.2 concatenate.72
  542.9 17.8 %convolution_convert_fusion.2 = bf16[1536,2048]{1,0:T(8,128)(2,1)S(1)} fusion(bf16[2048,2048]{1,0:T(8,128)(2,1)} %get-tuple-element.182, bf16[512,1536]{1,0:T(8,128)(2,1)} %copy-done.132, bf16[512,1536]{1,0:T(8,128)(2,1)} %copy-done.131, bf16[512,1536]{1,0:T(8,128)(2,1)} %collective-permute-done.9, bf16[512,1536]{1,0:T(8,128)(2,1)S(1)} %copy-done.114), kind=kOutput, calls=%fused_computation.7 | convolution fusion | flops 12913213440 | bytes 20971520 | tf_op jit(solution)/shard_map/dot_general | solution.py:1138
  560.8 4.7 pad_maximum_fusion.1
  578.7 4.3 convolution_convert_fusion.1
  587.6 2.9 add_convert_fusion.2
  592.1 24.7 %reduce-scatter.3.cloned.1.call-done.refs_1_.grad_ref = bf16[192,3072]{1,0:T(8,128)(2,1)} async-done(((bf16[1536,3072]{1,0:T(8,128)(2,1)}), bf16[192,3072]{1,0:T(8,128)(2,1)}) %reduce-scatter.3.cloned.1.call-update) | async-done | bytes 1179664 | tf_op jit(solution)/shard_map/reduce_scatter | solution.py:1155
  621.9 6.8 shard_map.435
  647.3 3.1 shard_map.436
  654.6 23.7 %shard_map.438 = (bf16[512,1536]{1,0:T(8,128)(2,1)S(1)}, bf16[2,512,512]{2,1,0:T(8,128)(2,1)S(1)}) custom-call(s32[2]{0:T(128)S(1)} %copy-done.72, s32[1]{0:T(128)} %bitcast.16.owner_ref, s32[2,512]{1,0:T(2,128)S(1)} %copy-done.66, bf16[512,1536]{1,0:T(8,128)(2,1)S(1)} %copy-done.97, bf16[512,1536]{1,0:T(8,128)(2,1)S(1)} %copy-done.33, ...), custom_call_target="tpu_custom_call" | custom-call | flops 24159191040 | bytes 6291456 | tf_op jit(solution)/shard_map/pallas_call | solution.py:498
  678.3 65.2 %collective-permute-done.22 = bf16[512,512]{1,0:T(8,128)(2,1)} collective-permute-done((bf16[512,512]{1,0:T(8,128)(2,1)}, bf16[512,512]{1,0:T(8,128)(2,1)}, u32[]{:S(2)}, u32[]{:S(2)}) %collective-permute-start.22) | collective-permute-done | bytes 524320 | tf_op jit(solution)/shard_map/ppermute | solution.py:1261
  743.5 16.2 %collective-permute-done.23 = bf16[512,512]{1,0:T(8,128)(2,1)} collective-permute-done((bf16[512,512]{1,0:T(8,128)(2,1)}, bf16[512,512]{1,0:T(8,128)(2,1)}, u32[]{:S(2)}, u32[]{:S(2)}) %collective-permute-start.23) | collective-permute-done | bytes 524320 | tf_op jit(solution)/shard_map/ppermute | solution.py:1261
  761.4 9.7 %fusion.10 = (bf16[1536]{0:T(1024)(128)(2,1)S(1)}, f32[512]{0:T(512)S(1)}, f32[512,1536]{1,0:T(8,128)}) fusion(f32[512]{0:T(512)S(1)} %add_rsqrt_fusion, bf16[1,1,512,1536]{3,2,1,0:T(8,128)(2,1)S(1)} %copy-done.10, f32[1536]{0:T(1024)S(1)} %copy-done.144, bf16[1536,2688]{1,0:T(8,128)(2,1)} %bitcast.123, bf16[512,512]{1,0:T(8,128)(2,1)S(1)} %get-tuple-element.359, ...), kind=kOutput, calls=%fused_computation.26 | convolution fusion | flops 4039899136 | bytes 15217664 | tf_op jit(solution)/shard_map/dot_general | solution.py:1274
  771.8 8.1 convolution_convert_fusion
  779.9 115.5 %shard_map.439.sum_ref = f32[48,4224]{1,0:T(8,128)S(1)} custom-call(bf16[2,4,2,2,48,2560]{5,4,3,2,1,0:T(8,128)(2,1)} %bitcast.127, bf16[2,4,2,2,48,128]{5,4,3,2,1,0:T(8,128)(2,1)S(1)} %bitcast.112, bf16[2,4,2,2,48,1536]{5,4,3,2,1,0:T(8,128)(2,1)S(1)} %bitcast.111), custom_call_target="tpu_custom_call" | custom-call | bytes 415236096 | tf_op jit(solution)/shard_map/pallas_call | solution.py:835
  895.5 4.7 fusion.12
  930.3 3.1 shard_map.441
  (480 shorter events, 167.0 us)
Async XLA Ops:
  7.2 244.9 %all-gather.5.cloned.1.call-start = ((), (), s32[]{:S(2)}) async-start(), calls=%async_computation.4 | async-start | bytes 10616832 | tf_op jit(solution)/shard_map/all_gather | solution.py:1074
  12.0 397.7 %all-gather.7.cloned.1.call-start = ((), (), s32[]{:S(2)}) async-start(), calls=%async_computation.5 | async-start | bytes 10616832 | tf_op jit(solution)/shard_map/all_gather | solution.py:1106
  12.4 96.8 %copy-start.122 = (bf16[1,1,512,1536]{3,2,1,0:T(8,128)(2,1)S(1)}, bf16[1,1,512,1536]{3,2,1,0:T(8,128)(2,1)}, u32[]{:S(2)}) copy-start(bf16[1,1,512,1536]{3,2,1,0:T(8,128)(2,1)} %param.24) | copy-start | bytes 4718596
  19.6 93.8 %copy-start.127 = (s32[16,512]{0,1:T(8,128)}, s32[16,512]{0,1:T(8,128)S(1)}, u32[]{:S(2)}) copy-start(s32[16,512]{0,1:T(8,128)S(1)} %copy.154) | copy-start | bytes 98308
  19.8 95.9 %copy-start.136 = (pred[512,16]{1,0:T(32,128)(4,1)}, pred[512,16]{1,0:T(32,128)(4,1)S(1)}, u32[]{:S(2)}) copy-start(pred[512,16]{1,0:T(32,128)(4,1)S(1)} %copy.155) | copy-start | bytes 24580
  111.2 104.0 %collective-permute-start.7 = (bf16[512,1664]{1,0:T(8,128)(2,1)}, bf16[512,1664]{1,0:T(8,128)(2,1)}, u32[]{:S(2)}, u32[]{:S(2)}) collective-permute-start(bf16[512,1664]{1,0:T(8,128)(2,1)} %concatenate.60), channel_id=1, source_target_pairs={{0,2},{1,3},{2,0},{3,1},{4,6},{5,7},{6,4},{7,5},{8,10},{9,11},{10,... | collective-permute-start | bytes 5111816 | tf_op jit(solution)/shard_map/ppermute | solution.py:1016
  113.2 106.2 %collective-permute-start.6 = (bf16[512,1664]{1,0:T(8,128)(2,1)}, bf16[512,1664]{1,0:T(8,128)(2,1)}, u32[]{:S(2)}, u32[]{:S(2)}) collective-permute-start(bf16[512,1664]{1,0:T(8,128)(2,1)} %concatenate.60), channel_id=1, source_target_pairs={{0,1},{1,0},{2,3},{3,2},{4,5},{5,4},{6,7},{7,6},{8,9},{9,8},{10,11... | collective-permute-start | bytes 5111816 | tf_op jit(solution)/shard_map/ppermute | solution.py:1012
  115.7 127.5 %copy-start.138 = (f32[1536]{0:T(1024)}, f32[1536]{0:T(1024)S(1)}, u32[]{:S(2)}) copy-start(f32[1536]{0:T(1024)S(1)} %get-tuple-element.353) | copy-start | bytes 18436
  126.9 40.4 %copy-start.149 = (s32[1,1,9]{2,1,0:T(1,128)S(1)}, s32[1,1,9]{2,1,0:T(1,128)}, u32[]{:S(2)}) copy-start(s32[1,1,9]{2,1,0:T(1,128)} %param.25) | copy-start | bytes 112
  139.4 46.6 %copy-start.41 = (bf16[512,512]{1,0:T(8,128)(2,1)}, bf16[512,512]{1,0:T(8,128)(2,1)S(1)}, u32[]{:S(2)}) copy-start(bf16[512,512]{1,0:T(8,128)(2,1)S(1)} %get-tuple-element.366.v_ref) | copy-start | bytes 1572868
  139.4 46.6 %copy-start.43 = (bf16[512,512]{1,0:T(8,128)(2,1)}, bf16[512,512]{1,0:T(8,128)(2,1)S(1)}, u32[]{:S(2)}) copy-start(bf16[512,512]{1,0:T(8,128)(2,1)S(1)} %get-tuple-element.367.k_ref) | copy-start | bytes 1572868
  139.4 51.7 %collective-permute-start = (bf16[512,512]{1,0:T(8,128)(2,1)S(1)}, bf16[512,512]{1,0:T(8,128)(2,1)S(1)}, u32[]{:S(2)}, u32[]{:S(2)}) collective-permute-start(bf16[512,512]{1,0:T(8,128)(2,1)S(1)} %get-tuple-element.367.k_ref), channel_id=1, source_target_pairs={{0,4},{4,8},{8,12},{1,5},{5,9},{9,13},{2,6},{6,10},{10,14},{3,7},{... | collective-permute-start | bytes 1572872 | tf_op jit(solution)/shard_map/ppermute | solution.py:1105
  164.5 41.4 %collective-permute-start.3 = (bf16[512,512]{1,0:T(8,128)(2,1)S(1)}, bf16[512,512]{1,0:T(8,128)(2,1)}, u32[]{:S(2)}, u32[]{:S(2)}) collective-permute-start(bf16[512,512]{1,0:T(8,128)(2,1)S(1)} %get-tuple-element.366.v_ref), channel_id=1, source_target_pairs={{0,4},{4,8},{8,12},{1,5},{5,9},{9,13},{2,6},{6,10},{10,14},{3,7},{... | collective-permute-start | bytes 1572872 | tf_op jit(solution)/shard_map/ppermute | solution.py:1105
  167.4 69.3 %copy-start.65 = (s32[2,512]{1,0:T(2,128)}, s32[2,512]{1,0:T(2,128)S(1)}, u32[]{:S(2)}) copy-start(s32[2,512]{1,0:T(2,128)S(1)} %pad_add_fusion.place_ref) | copy-start | bytes 12292
  167.6 39.1 %copy-start.73 = (s32[2]{0:T(128)}, s32[2]{0:T(128)S(1)}, u32[]{:S(2)}) copy-start(s32[2]{0:T(128)S(1)} %get-tuple-element.379.flag_ref) | copy-start | bytes 28
  191.1 45.5 %copy-start.77 = (s32[2]{0:T(128)}, s32[2]{0:T(128)S(1)}, u32[]{:S(2)}) copy-start(s32[2]{0:T(128)S(1)} %get-tuple-element.381.flag_ref) | copy-start | bytes 28
  191.1 22.6 %collective-permute-start.1 = (bf16[512,512]{1,0:T(8,128)(2,1)S(1)}, bf16[512,512]{1,0:T(8,128)(2,1)S(1)}, u32[]{:S(2)}, u32[]{:S(2)}) collective-permute-start(bf16[512,512]{1,0:T(8,128)(2,1)S(1)} %collective-permute-done.k_ref), channel_id=1, source_target_pairs={{4,8},{8,12},{5,9},{9,13},{6,10},{10,14},{7,11},{11,15},{20,24},{2... | collective-permute-start | bytes 1572872 | tf_op jit(solution)/shard_map/ppermute | solution.py:1105
  206.0 8.4 collective-permute-start.4
  213.7 5.6 collective-permute-start.2
  214.4 4.9 collective-permute-start.5
  215.2 11.0 %collective-permute-start.8 = (bf16[512,1664]{1,0:T(8,128)(2,1)}, bf16[512,1664]{1,0:T(8,128)(2,1)}, u32[]{:S(2)}, u32[]{:S(2)}) collective-permute-start(bf16[512,1664]{1,0:T(8,128)(2,1)} %collective-permute-done.7), channel_id=1, source_target_pairs={{0,1},{1,0},{2,3},{3,2},{4,5},{5,4},{6,7},{7,6},{8,9},{9,8},{10,11... | collective-permute-start | bytes 5111816 | tf_op jit(solution)/shard_map/ppermute | solution.py:1012
  219.4 397.4 %reduce-scatter.3.cloned.1.call-start = ((), (), s32[]{:S(2)}) async-start(), calls=%async_computation.2 | async-start | bytes 10616832 | tf_op jit(solution)/shard_map/reduce_scatter | solution.py:1155
  240.4 376.4 %copy-start.108 = (f32[4,6,512]{2,1,0:T(8,128)}, f32[4,6,512]{2,1,0:T(8,128)S(1)}, u32[]{:S(2)}) copy-start(f32[4,6,512]{2,1,0:T(8,128)S(1)} %get-tuple-element.167.lse_ref) | copy-start | bytes 147460
  245.1 246.9 %copy-start.113 = (bf16[512,1536]{1,0:T(8,128)(2,1)}, bf16[512,1536]{1,0:T(8,128)(2,1)S(1)}, u32[]{:S(2)}) copy-start(bf16[512,1536]{1,0:T(8,128)(2,1)S(1)} %multiply_convert_fusion) | copy-start | bytes 4718596
  245.2 3.7 collective-permute-start.9
  245.7 37.1 %collective-permute-start.10 = (bf16[512,1536]{1,0:T(8,128)(2,1)S(1)}, bf16[512,1536]{1,0:T(8,128)(2,1)S(1)}, u32[]{:S(2)}, u32[]{:S(2)}) collective-permute-start(bf16[512,1536]{1,0:T(8,128)(2,1)S(1)} %multiply_convert_fusion), channel_id=1, source_target_pairs={{0,2},{1,3},{2,0},{3,1},{4,6},{5,7},{6,4},{7,5},{8,10},{9,11},{10,... | collective-permute-start | bytes 4718600 | tf_op jit(solution)/shard_map/ppermute | solution.py:1016
  282.8 55.6 %copy-start.131 = (bf16[512,1536]{1,0:T(8,128)(2,1)}, bf16[512,1536]{1,0:T(8,128)(2,1)S(1)}, u32[]{:S(2)}) copy-start(bf16[512,1536]{1,0:T(8,128)(2,1)S(1)} %collective-permute-done.10) | copy-start | bytes 4718596
  282.9 3.5 collective-permute-start.11
  444.4 3.9 collective-permute-start.12
  444.4 458.2 %reduce-scatter.5.cloned.1.call-start = ((), (), s32[]{:S(2)}) async-start(), calls=%async_computation.3 | async-start | bytes 10616832 | tf_op jit(solution)/shard_map/reduce_scatter | solution.py:1155
  450.7 39.4 %collective-permute-start.13 = (bf16[512,1664]{1,0:T(8,128)(2,1)S(1)}, bf16[512,1664]{1,0:T(8,128)(2,1)}, u32[]{:S(2)}, u32[]{:S(2)}) collective-permute-start(bf16[512,1664]{1,0:T(8,128)(2,1)S(1)} %add_convert_fusion), channel_id=1, source_target_pairs={{0,2},{1,3},{2,0},{3,1},{4,6},{5,7},{6,4},{7,5},{8,10},{9,11},{10,... | collective-permute-start | bytes 5111816 | tf_op jit(solution)/shard_map/ppermute | solution.py:1016
  491.9 3.7 collective-permute-start.14
  571.4 16.2 %collective-permute-start.15 = (bf16[512,1536]{1,0:T(8,128)(2,1)}, bf16[512,1536]{1,0:T(8,128)(2,1)}, u32[]{:S(2)}, u32[]{:S(2)}) collective-permute-start(bf16[512,1536]{1,0:T(8,128)(2,1)} %slice.238), channel_id=1, source_target_pairs={{0,1},{1,0},{2,3},{3,2},{4,5},{5,4},{6,7},{7,6},{8,9},{9,8},{10,11... | collective-permute-start | bytes 4718600 | tf_op jit(solution)/shard_map/ppermute | solution.py:1012
  572.9 10.2 %collective-permute-start.18 = (bf16[512,512]{1,0:T(8,128)(2,1)S(1)}, bf16[512,512]{1,0:T(8,128)(2,1)S(1)}, u32[]{:S(2)}, u32[]{:S(2)}) collective-permute-start(bf16[512,512]{1,0:T(8,128)(2,1)S(1)} %get-tuple-element.364), channel_id=1, source_target_pairs={{12,8},{13,9},{14,10},{15,11},{28,24},{29,25},{30,26},{31,27}} | collective-permute-start | bytes 1572872 | tf_op jit(solution)/shard_map/ppermute | solution.py:1261
  573.7 9.3 collective-permute-start.19
  578.3 193.1 %collective-permute-start.17 = (bf16[512,1536]{1,0:T(8,128)(2,1)}, bf16[512,1536]{1,0:T(8,128)(2,1)}, u32[]{:S(2)}, u32[]{:S(2)}) collective-permute-start(bf16[512,1536]{1,0:T(8,128)(2,1)} %slice.239), channel_id=1, source_target_pairs={{0,1},{1,0},{2,3},{3,2},{4,5},{5,4},{6,7},{7,6},{8,9},{9,8},{10,11... | collective-permute-start | bytes 4718600 | tf_op jit(solution)/shard_map/ppermute | solution.py:1012
  583.4 33.4 %copy-start.28 = (f32[2048,128]{1,0:T(8,128)S(1)}, f32[2048,128]{1,0:T(8,128)}, u32[]{:S(2)}) copy-start(f32[2048,128]{1,0:T(8,128)} %copy-done.26) | copy-start | bytes 3145732
  583.4 33.4 %copy-start.60 = (f32[4,6,512]{2,1,0:T(8,128)S(1)}, f32[4,6,512]{2,1,0:T(8,128)}, u32[]{:S(2)}) copy-start(f32[4,6,512]{2,1,0:T(8,128)} %shard_map.432.delta_ref) | copy-start | bytes 147460
  583.4 33.4 %copy-start.74 = (s32[2]{0:T(128)S(1)}, s32[2]{0:T(128)}, u32[]{:S(2)}) copy-start(s32[2]{0:T(128)} %copy-done.73) | copy-start | bytes 28
  584.5 44.3 %collective-permute-start.20 = (bf16[512,512]{1,0:T(8,128)(2,1)}, bf16[512,512]{1,0:T(8,128)(2,1)}, u32[]{:S(2)}, u32[]{:S(2)}) collective-permute-start(bf16[512,512]{1,0:T(8,128)(2,1)} %get-tuple-element.362), channel_id=1, source_target_pairs={{8,4},{12,8},{9,5},{13,9},{10,6},{14,10},{11,7},{15,11},{24,20},{2... | collective-permute-start | bytes 1572872 | tf_op jit(solution)/shard_map/ppermute | solution.py:1261
  586.1 42.7 %collective-permute-start.21 = (bf16[512,512]{1,0:T(8,128)(2,1)}, bf16[512,512]{1,0:T(8,128)(2,1)}, u32[]{:S(2)}, u32[]{:S(2)}) collective-permute-start(bf16[512,512]{1,0:T(8,128)(2,1)} %get-tuple-element.363), channel_id=1, source_target_pairs={{8,4},{12,8},{9,5},{13,9},{10,6},{14,10},{11,7},{15,11},{24,20},{2... | collective-permute-start | bytes 1572872 | tf_op jit(solution)/shard_map/ppermute | solution.py:1261
  590.5 180.9 %collective-permute-start.16 = (bf16[512,1536]{1,0:T(8,128)(2,1)}, bf16[512,1536]{1,0:T(8,128)(2,1)}, u32[]{:S(2)}, u32[]{:S(2)}) collective-permute-start(bf16[512,1536]{1,0:T(8,128)(2,1)} %add_convert_fusion.2), channel_id=1, source_target_pairs={{0,2},{1,3},{2,0},{3,1},{4,6},{5,7},{6,4},{7,5},{8,10},{9,11},{10,... | collective-permute-start | bytes 4718600 | tf_op jit(solution)/shard_map/ppermute | solution.py:1016
  632.3 111.2 %collective-permute-start.22 = (bf16[512,512]{1,0:T(8,128)(2,1)}, bf16[512,512]{1,0:T(8,128)(2,1)}, u32[]{:S(2)}, u32[]{:S(2)}) collective-permute-start(bf16[512,512]{1,0:T(8,128)(2,1)} %get-tuple-element.360), channel_id=1, source_target_pairs={{4,0},{8,4},{12,8},{5,1},{9,5},{13,9},{6,2},{10,6},{14,10},{7,3},{... | collective-permute-start | bytes 1572872 | tf_op jit(solution)/shard_map/ppermute | solution.py:1261
  633.6 126.1 %collective-permute-start.23 = (bf16[512,512]{1,0:T(8,128)(2,1)}, bf16[512,512]{1,0:T(8,128)(2,1)}, u32[]{:S(2)}, u32[]{:S(2)}) collective-permute-start(bf16[512,512]{1,0:T(8,128)(2,1)} %get-tuple-element.361), channel_id=1, source_target_pairs={{4,0},{8,4},{12,8},{5,1},{9,5},{13,9},{6,2},{10,6},{14,10},{7,3},{... | collective-permute-start | bytes 1572872 | tf_op jit(solution)/shard_map/ppermute | solution.py:1261
  678.3 92.8 %copy-start.100 = (bf16[512,1536]{1,0:T(8,128)(2,1)}, bf16[512,1536]{1,0:T(8,128)(2,1)S(1)}, u32[]{:S(2)}) copy-start(bf16[512,1536]{1,0:T(8,128)(2,1)S(1)} %get-tuple-element.180) | copy-start | bytes 4718596
  678.3 83.0 %copy-start.10 = (bf16[1,1,512,1536]{3,2,1,0:T(8,128)(2,1)S(1)}, bf16[1,1,512,1536]{3,2,1,0:T(8,128)(2,1)}, u32[]{:S(2)}) copy-start(bf16[1,1,512,1536]{3,2,1,0:T(8,128)(2,1)} %param.23) | copy-start | bytes 4718596
  678.3 83.0 %copy-start.144 = (f32[1536]{0:T(1024)S(1)}, f32[1536]{0:T(1024)}, u32[]{:S(2)}) copy-start(f32[1536]{0:T(1024)} %get-tuple-element.352) | copy-start | bytes 18436
  779.9 115.6 %copy-start.112 = (f32[512,1536]{1,0:T(8,128)S(1)}, f32[512,1536]{1,0:T(8,128)}, u32[]{:S(2)}) copy-start(f32[512,1536]{1,0:T(8,128)} %copy-done.110) | copy-start | bytes 9437188
  (139 other events, 627.9 us)
Sparse Core Ops, SparseCore 0:
  12.1 190.7 all-gather.4
  219.5 190.1 all-gather.6
  444.6 172.1 reduce-scatter.2
  620.2 225.3 reduce-scatter.4

commit v5 on v4

--- a/solution.py
+++ b/solution.py
@@ -1250,7 +1250,7 @@
             own_tables,
             grad_query,
             back == 0,
-            (front_sum,) if step == 3 else early if back == 0 else (),
+            hops if step == 2 else (front_sum,) if step == 3 else early if back == 0 else (),
         )
         key_sum = grad_pairs.astype(F32)
         if step > 1:
@@ -1258,10 +1258,10 @@
         key_sum = key_sum.astype(BF16)
         if back > 0:
             pairs_back = [(i, i - 1) for i in range(back, ctx_count)]
-            got = jnp.stack([lax.ppermute(key_sum[i], "ctx", pairs_back) for i in range(2)])
+            hops = tuple(lax.ppermute(key_sum[i], "ctx", pairs_back) for i in range(2))
+            got = jnp.stack(hops)
         if step == 1:
             thin = thin_grad_of(hidden, grad_pairs)
-        if step == 2:
             wide = wide_grad_of(grad, grad_pairs)
     (grad_query,) = grad_query
     rear_sum = scatter(owner_rows(wide, thin))

time: 954 us -> 930 us (0.975)
  waiting for transfers between devices: 186 us -> 155 us
  Pallas kernels: 423 us -> 436 us
    reduce_scatter x2, waiting for transfers between devices: 24.7 us -> 0.01 us  [scatter(): lax.psum_scatter(both, ('dp', 'ctx'), scatter_dimension=0, tiled=True)]
    pallas_call x1, Pallas kernels: 116 us -> 126 us  [dense_sum(): pl.pallas_call(functools.partial(dense_sum_kernel, tuple(starts)), in_spe...]
  transfers between devices with their start and end apart: 28 -> 28, of which waited for: 10 -> 9; matrix products, arithmetic and copies ran while one was open for 20% -> 21% of each run, Pallas kernels for 41% -> 47%
where the time goes in v5:
time: 930 us; the launch traced here: 919 us
  Pallas kernels  436 us (47%)
  waiting for transfers between devices  155 us (17%)
  local copies, waits for them, and re-layouts  126 us (14%)
  matrix products  90 us (10%)
  other arithmetic  49.2 us (5%)
  starting transfers between devices  46.5 us (5%)
  between operations  16 us (2%)
    pallas_call x4, Pallas kernels, run_experts(): pl.pallas_call(functools.partial(experts_kernel, bool(before)), grid_spec...  126 us
    pallas_call x1, Pallas kernels, dense_sum(): pl.pallas_call(functools.partial(dense_sum_kernel, tuple(starts)), in_spe...  126 us
    pallas_call x1, Pallas kernels, dense_gather(): pl.pallas_call(dense_gather_kernel, in_specs=[pl.BlockSpec(memory_space=p...  88.5 us
    unnamed x331, local copies, waits for them, and re-layouts  77.5 us
    ppermute x6, waiting for transfers between devices, body(): lax.ppermute(key_sum[i], 'ctx', pairs_back)  76.2 us
    all_gather x1, waiting for transfers between devices, body(): lax.all_gather(after(packed[1], *key_pieces[-1]), ('dp', 'ctx'), axis=0,...  49.5 us
    pallas_call x4, Pallas kernels, attend_backward(): pl.pallas_call(functools.partial(attend_back_kernel, not before, final),...  40.9 us
    dot_general x2, matrix products, wide_grad_of(): lax.dot_general(second_all, grad, contract, preferred_element_type=F32)  34.6 us
  transfers between devices with their start and end apart: 28, of which 9 were waited for; matrix products, arithmetic and copies ran while one was open for 21% of the time, Pallas kernels for 47%

profile of v5, /device:TPU:0, one launch (start us, length us, event | category | flops | bytes accessed | tf_op | source)
XLA Modules:
  0.0 919.0 jit_solution(305715693016676131)
XLA Ops:
  16.3 3.2 convert_reduce_fusion
  20.6 88.5 %shard_map.422 = (bf16[2,4,2,2,48,2688]{5,4,3,2,1,0:T(8,128)(2,1)}, bf16[2,4,2,2,48,1536]{5,4,3,2,1,0:T(8,128)(2,1)}) custom-call(bf16[48,2688]{1,0:T(8,128)(2,1)} %concatenate.57.first_ref, bf16[48,1536]{1,0:T(8,128)(2,1)} %bitcast.135), custom_call_target="tpu_custom_call" | custom-call | bytes 12976128 | tf_op jit(solution)/shard_map/pallas_call | solution.py:702
  116.0 3.7 fusion.20
  123.4 3.4 copy-done.56
  126.8 10.6 %shard_map.423 = (bf16[512,1536]{1,0:T(8,128)(2,1)S(1)}, bf16[512,1024]{1,0:T(8,128)(2,1)S(1)}, bf16[512,1536]{1,0:T(8,128)(2,1)S(1)}) custom-call(bf16[512,1536]{1,0:T(8,128)(2,1)S(1)} %bitcast.108, f32[1,1536]{1,0:T(1,128)S(1)} %copy.152.gain_ref, bf16[1536,2688]{1,0:T(8,128)(2,1)S(1)} %bitcast.126, ...), custom_call_target="tpu_custom_call" | custom-call | flops 4026531840 | bytes 7864320 | tf_op jit(solution)/shard_map/pallas_call | solution.py:210
  139.4 25.1 %collective-permute-start = (bf16[512,512]{1,0:T(8,128)(2,1)S(1)}, bf16[512,512]{1,0:T(8,128)(2,1)S(1)}, u32[]{:S(2)}, u32[]{:S(2)}) collective-permute-start(bf16[512,512]{1,0:T(8,128)(2,1)S(1)} %get-tuple-element.367.k_ref), channel_id=1, source_target_pairs={{0,4},{4,8},{8,12},{1,5},{5,9},{9,13},{2,6},{6,10},{10,14},{3,7},{... | collective-permute-start | bytes 1572872 | tf_op jit(solution)/shard_map/ppermute | solution.py:1105
  164.5 2.7 collective-permute-start.3
  168.9 17.0 %shard_map.424 = (f32[4,6,512]{2,1,0:T(8,128)S(1)}, f32[4,6,512]{2,1,0:T(8,128)S(1)}, f32[4,3,128,512]{3,2,1,0:T(8,128)S(1)}) custom-call(s32[2]{0:T(128)S(1)} %get-tuple-element.378.flag_ref, s32[1]{0:T(128)} %bitcast.16.owner_ref, s32[2,512]{1,0:T(2,128)S(1)} %pad_add_fusion.place_ref, bf16[512,1536]{1,0:T(8,128)(2,1)S(1)} %copy-done.90, ...), custom_call_target="tpu_custom_call" | custom-call | flops 16106127360 | bytes 6291456 | tf_op jit(solution)/shard_map/pallas_call | solution.py:351
  188.2 2.9 constant_dynamic-update-slice_fusion.1
  191.8 14.2 %collective-permute-done.3.v_ref = bf16[512,512]{1,0:T(8,128)(2,1)} collective-permute-done((bf16[512,512]{1,0:T(8,128)(2,1)S(1)}, bf16[512,512]{1,0:T(8,128)(2,1)}, u32[]{:S(2)}, u32[]{:S(2)}) %collective-permute-start.3) | collective-permute-done | bytes 524320 | tf_op jit(solution)/shard_map/ppermute | solution.py:1105
  208.6 5.1 shard_map.425
  219.5 3.0 constant_dynamic-update-slice_fusion.do_ref.code_ref
  231.5 5.1 pad_maximum_fusion.2
  236.7 3.9 shard_map.427
  240.6 2.7 multiply_reduce_fusion.2
  249.1 3.3 pad_maximum_fusion.4.h_ref
  252.4 30.7 %shard_map.428 = (bf16[2048,1024]{1,0:T(8,128)(2,1)}, bf16[2048,2048]{1,0:T(8,128)(2,1)}, bf16[1024,1664]{1,0:T(8,128)(2,1)}, bf16[1024,1536]{1,0:T(8,128)(2,1)}) custom-call(s32[1]{0:T(128)} %bitcast.22.first_ref, bf16[1024,1536]{1,0:T(8,128)(2,1)} %pad_maximum_fusion.4.h_ref, bf16[1024,1664]{1,0:T(8,128)(2,1)} %constant_dynamic-update-slice_fusion.do_ref.code_ref, ...), custom_call_target="tpu_custom_call" | custom-call | flops 28991029248 | bytes 25165824 | tf_op jit(solution)/shard_map/pallas_call | solution.py:977
  283.6 3.0 collective-permute-done.11
  289.5 30.8 %shard_map.429 = (bf16[2048,1024]{1,0:T(8,128)(2,1)}, bf16[2048,2048]{1,0:T(8,128)(2,1)}, bf16[1024,1664]{1,0:T(8,128)(2,1)}, bf16[1024,1536]{1,0:T(8,128)(2,1)}) custom-call(s32[1]{0:T(128)} %bitcast.22.first_ref, bf16[1024,1536]{1,0:T(8,128)(2,1)} %copy-done.136, bf16[1024,1664]{1,0:T(8,128)(2,1)} %copy-done.120, ...), custom_call_target="tpu_custom_call", output_to_operand_aliasing={{0}: (6, {}), {1}: (7, {})} | custom-call | flops 28991029248 | bytes 25165824 | tf_op jit(solution)/shard_map/pallas_call | solution.py:977
  320.3 10.3 %convolution_convert_fusion.5 = bf16[1024,1536]{1,0:T(8,128)(2,1)S(1)} fusion(bf16[2048,1024]{1,0:T(8,128)(2,1)} %get-tuple-element.152, bf16[2048,1536]{1,0:T(8,128)(2,1)} %pad_maximum_fusion.2), kind=kOutput, calls=%fused_computation.18 | convolution fusion | flops 6444023808 | bytes 13631488 | tf_op jit(solution)/shard_map/dot_general | solution.py:1143
  332.6 5.9 concatenate.69
  338.5 16.8 %convolution_convert_fusion.3 = bf16[1536,2048]{1,0:T(8,128)(2,1)S(1)} fusion(bf16[2048,2048]{1,0:T(8,128)(2,1)} %get-tuple-element.150, bf16[512,1536]{1,0:T(8,128)(2,1)} %copy-done.133, bf16[512,1536]{1,0:T(8,128)(2,1)S(1)} %collective-permute-done.10, bf16[512,1536]{1,0:T(8,128)(2,1)} %collective-permute-done.9, ...), kind=kOutput, calls=%fused_computation.8 | convolution fusion | flops 12913213440 | bytes 20971520 | tf_op jit(solution)/shard_map/dot_general | solution.py:1138
  355.3 4.7 pad_maximum_fusion.refs_3_
  360.1 49.5 %all-gather.7.cloned.1.call-done = bf16[16,576,512]{2,1,0:T(8,128)(2,1)} async-done(((bf16[2,576,512]{2,1,0:T(8,128)(2,1)}), bf16[16,576,512]{2,1,0:T(8,128)(2,1)}) %all-gather.7.cloned.1.call-update) | async-done | bytes 9437200 | tf_op jit(solution)/shard_map/all_gather | solution.py:1106
  409.6 32.2 %shard_map.430 = (bf16[2048,1024]{1,0:T(8,128)(2,1)}, bf16[2048,2048]{1,0:T(8,128)(2,1)}, bf16[1024,1664]{1,0:T(8,128)(2,1)}, bf16[1024,1536]{1,0:T(8,128)(2,1)}) custom-call(s32[1]{0:T(128)S(6)} %add.123.first_ref, bf16[1024,1536]{1,0:T(8,128)(2,1)} %copy-done.136, bf16[1024,1664]{1,0:T(8,128)(2,1)} %copy-done.120, bf16[1024,1664]{1,0:T(8,128)(2,1)} %copy-done.120, ...), custom_call_target="tpu_custom_call" | custom-call | flops 28991029248 | bytes 25165824 | tf_op jit(solution)/shard_map/pallas_call | solution.py:977
  443.6 3.6 collective-permute-done.12
  449.1 32.1 %shard_map.431 = (bf16[2048,1024]{1,0:T(8,128)(2,1)}, bf16[2048,2048]{1,0:T(8,128)(2,1)}, bf16[1024,1664]{1,0:T(8,128)(2,1)}, bf16[1024,1536]{1,0:T(8,128)(2,1)}) custom-call(s32[1]{0:T(128)S(6)} %add.123.first_ref, bf16[1024,1536]{1,0:T(8,128)(2,1)} %pad_maximum_fusion.4.h_ref, ...), custom_call_target="tpu_custom_call", output_to_operand_aliasing={{0}: (9, {}), {1}: (10, {})} | custom-call | flops 28991029248 | bytes 25165824 | tf_op jit(solution)/shard_map/pallas_call | solution.py:977
  481.3 5.7 collective-permute-done.13
  498.7 3.7 convolution_convert_fusion.6.do_ref
  502.4 4.4 shard_map.432.delta_ref
  511.6 3.5 shard_map.433
  515.2 10.8 %convolution_convert_fusion.4 = bf16[1024,1536]{1,0:T(8,128)(2,1)S(1)} fusion(bf16[2048,1024]{1,0:T(8,128)(2,1)S(1)} %copy-done.151, bf16[2048,1536]{1,0:T(8,128)(2,1)} %pad_maximum_fusion.2), kind=kOutput, calls=%fused_computation.17 | convolution fusion | flops 6444023808 | bytes 13631488 | tf_op jit(solution)/shard_map/dot_general | solution.py:1143
  527.9 6.0 concatenate.72
  533.9 17.8 %convolution_convert_fusion.2 = bf16[1536,2048]{1,0:T(8,128)(2,1)S(1)} fusion(bf16[2048,2048]{1,0:T(8,128)(2,1)} %get-tuple-element.182, bf16[512,1536]{1,0:T(8,128)(2,1)} %copy-done.133, bf16[512,1536]{1,0:T(8,128)(2,1)} %copy-done.132, bf16[512,1536]{1,0:T(8,128)(2,1)} %collective-permute-done.9, bf16[512,1536]{1,0:T(8,128)(2,1)S(1)} %copy-done.114), kind=kOutput, calls=%fused_computation.7 | convolution fusion | flops 12913213440 | bytes 20971520 | tf_op jit(solution)/shard_map/dot_general | solution.py:1138
  551.7 4.7 pad_maximum_fusion.1
  569.9 4.8 convolution_convert_fusion.1
  574.8 6.8 shard_map.434
  593.6 6.8 shard_map.435
  618.8 3.1 shard_map.436
  626.0 23.7 %shard_map.438 = (bf16[512,1536]{1,0:T(8,128)(2,1)S(1)}, bf16[2,512,512]{2,1,0:T(8,128)(2,1)S(1)}) custom-call(s32[2]{0:T(128)S(1)} %copy-done.70, s32[1]{0:T(128)} %bitcast.16.owner_ref, s32[2,512]{1,0:T(2,128)S(1)} %copy-done.64, bf16[512,1536]{1,0:T(8,128)(2,1)S(1)} %copy-done.96, bf16[512,1536]{1,0:T(8,128)(2,1)S(1)} %copy-done.34, ...), custom_call_target="tpu_custom_call" | custom-call | flops 24159191040 | bytes 6291456 | tf_op jit(solution)/shard_map/pallas_call | solution.py:498
  649.8 66.0 %collective-permute-done.22 = bf16[512,512]{1,0:T(8,128)(2,1)} collective-permute-done((bf16[512,512]{1,0:T(8,128)(2,1)}, bf16[512,512]{1,0:T(8,128)(2,1)}, u32[]{:S(2)}, u32[]{:S(2)}) %collective-permute-start.22) | collective-permute-done | bytes 524320 | tf_op jit(solution)/shard_map/ppermute | solution.py:1261
  715.8 10.2 %collective-permute-done.23 = bf16[512,512]{1,0:T(8,128)(2,1)} collective-permute-done((bf16[512,512]{1,0:T(8,128)(2,1)}, bf16[512,512]{1,0:T(8,128)(2,1)}, u32[]{:S(2)}, u32[]{:S(2)}) %collective-permute-start.23) | collective-permute-done | bytes 524320 | tf_op jit(solution)/shard_map/ppermute | solution.py:1261
  727.6 9.5 %fusion.10 = (bf16[1536]{0:T(1024)(128)(2,1)S(1)}, f32[512]{0:T(512)S(1)}, f32[512,1536]{1,0:T(8,128)}) fusion(f32[512]{0:T(512)S(1)} %add_rsqrt_fusion, bf16[1,1,512,1536]{3,2,1,0:T(8,128)(2,1)S(1)} %copy-done.10, f32[1536]{0:T(1024)S(1)} %copy-done.145, bf16[1536,2688]{1,0:T(8,128)(2,1)} %bitcast.125, bf16[512,512]{1,0:T(8,128)(2,1)S(1)} %get-tuple-element.359, ...), kind=kOutput, calls=%fused_computation.26 | convolution fusion | flops 4039899136 | bytes 15217664 | tf_op jit(solution)/shard_map/dot_general | solution.py:1274
  737.8 7.9 convolution_convert_fusion
  745.8 125.5 %shard_map.439.sum_ref = f32[48,4224]{1,0:T(8,128)S(1)} custom-call(bf16[2,4,2,2,48,2560]{5,4,3,2,1,0:T(8,128)(2,1)} %bitcast.129, bf16[2,4,2,2,48,128]{5,4,3,2,1,0:T(8,128)(2,1)S(1)} %bitcast.112, bf16[2,4,2,2,48,1536]{5,4,3,2,1,0:T(8,128)(2,1)S(1)} %bitcast.111), custom_call_target="tpu_custom_call" | custom-call | bytes 415236096 | tf_op jit(solution)/shard_map/pallas_call | solution.py:835
  871.4 4.7 fusion.12
  876.1 2.5 fusion.9
  906.2 3.1 shard_map.441
  (479 shorter events, 157.8 us)
Async XLA Ops:
  7.2 245.2 %all-gather.5.cloned.1.call-start = ((), (), s32[]{:S(2)}) async-start(), calls=%async_computation.4 | async-start | bytes 10616832 | tf_op jit(solution)/shard_map/all_gather | solution.py:1074
  12.0 397.6 %all-gather.7.cloned.1.call-start = ((), (), s32[]{:S(2)}) async-start(), calls=%async_computation.5 | async-start | bytes 10616832 | tf_op jit(solution)/shard_map/all_gather | solution.py:1106
  12.4 96.8 %copy-start.121 = (bf16[1,1,512,1536]{3,2,1,0:T(8,128)(2,1)S(1)}, bf16[1,1,512,1536]{3,2,1,0:T(8,128)(2,1)}, u32[]{:S(2)}) copy-start(bf16[1,1,512,1536]{3,2,1,0:T(8,128)(2,1)} %param.24) | copy-start | bytes 4718596
  19.6 93.8 %copy-start.128 = (s32[16,512]{0,1:T(8,128)}, s32[16,512]{0,1:T(8,128)S(1)}, u32[]{:S(2)}) copy-start(s32[16,512]{0,1:T(8,128)S(1)} %copy.154) | copy-start | bytes 98308
  19.8 95.9 %copy-start.137 = (pred[512,16]{1,0:T(32,128)(4,1)}, pred[512,16]{1,0:T(32,128)(4,1)S(1)}, u32[]{:S(2)}) copy-start(pred[512,16]{1,0:T(32,128)(4,1)S(1)} %copy.155) | copy-start | bytes 24580
  111.2 104.0 %collective-permute-start.7 = (bf16[512,1664]{1,0:T(8,128)(2,1)}, bf16[512,1664]{1,0:T(8,128)(2,1)}, u32[]{:S(2)}, u32[]{:S(2)}) collective-permute-start(bf16[512,1664]{1,0:T(8,128)(2,1)} %concatenate.60), channel_id=1, source_target_pairs={{0,2},{1,3},{2,0},{3,1},{4,6},{5,7},{6,4},{7,5},{8,10},{9,11},{10,... | collective-permute-start | bytes 5111816 | tf_op jit(solution)/shard_map/ppermute | solution.py:1016
  113.3 106.2 %collective-permute-start.6 = (bf16[512,1664]{1,0:T(8,128)(2,1)}, bf16[512,1664]{1,0:T(8,128)(2,1)}, u32[]{:S(2)}, u32[]{:S(2)}) collective-permute-start(bf16[512,1664]{1,0:T(8,128)(2,1)} %concatenate.60), channel_id=1, source_target_pairs={{0,1},{1,0},{2,3},{3,2},{4,5},{5,4},{6,7},{7,6},{8,9},{9,8},{10,11... | collective-permute-start | bytes 5111816 | tf_op jit(solution)/shard_map/ppermute | solution.py:1012
  115.7 127.7 %copy-start.139 = (f32[1536]{0:T(1024)}, f32[1536]{0:T(1024)S(1)}, u32[]{:S(2)}) copy-start(f32[1536]{0:T(1024)S(1)} %get-tuple-element.353) | copy-start | bytes 18436
  126.8 40.4 %copy-start.150 = (s32[1,1,9]{2,1,0:T(1,128)S(1)}, s32[1,1,9]{2,1,0:T(1,128)}, u32[]{:S(2)}) copy-start(s32[1,1,9]{2,1,0:T(1,128)} %param.25) | copy-start | bytes 112
  139.3 28.0 %copy-start.87 = (bf16[512,1536]{1,0:T(8,128)(2,1)}, bf16[512,1536]{1,0:T(8,128)(2,1)S(1)}, u32[]{:S(2)}) copy-start(bf16[512,1536]{1,0:T(8,128)(2,1)S(1)} %get-tuple-element.185) | copy-start | bytes 4718596
  139.3 46.6 %copy-start.39 = (bf16[512,512]{1,0:T(8,128)(2,1)}, bf16[512,512]{1,0:T(8,128)(2,1)S(1)}, u32[]{:S(2)}) copy-start(bf16[512,512]{1,0:T(8,128)(2,1)S(1)} %get-tuple-element.366.v_ref) | copy-start | bytes 1572868
  139.4 46.6 %copy-start.41 = (bf16[512,512]{1,0:T(8,128)(2,1)}, bf16[512,512]{1,0:T(8,128)(2,1)S(1)}, u32[]{:S(2)}) copy-start(bf16[512,512]{1,0:T(8,128)(2,1)S(1)} %get-tuple-element.367.k_ref) | copy-start | bytes 1572868
  139.4 51.7 %collective-permute-start = (bf16[512,512]{1,0:T(8,128)(2,1)S(1)}, bf16[512,512]{1,0:T(8,128)(2,1)S(1)}, u32[]{:S(2)}, u32[]{:S(2)}) collective-permute-start(bf16[512,512]{1,0:T(8,128)(2,1)S(1)} %get-tuple-element.367.k_ref), channel_id=1, source_target_pairs={{0,4},{4,8},{8,12},{1,5},{5,9},{9,13},{2,6},{6,10},{10,14},{3,7},{... | collective-permute-start | bytes 1572872 | tf_op jit(solution)/shard_map/ppermute | solution.py:1105
  164.5 41.5 %collective-permute-start.3 = (bf16[512,512]{1,0:T(8,128)(2,1)S(1)}, bf16[512,512]{1,0:T(8,128)(2,1)}, u32[]{:S(2)}, u32[]{:S(2)}) collective-permute-start(bf16[512,512]{1,0:T(8,128)(2,1)S(1)} %get-tuple-element.366.v_ref), channel_id=1, source_target_pairs={{0,4},{4,8},{8,12},{1,5},{5,9},{9,13},{2,6},{6,10},{10,14},{3,7},{... | collective-permute-start | bytes 1572872 | tf_op jit(solution)/shard_map/ppermute | solution.py:1105
  167.3 69.3 %copy-start.63 = (s32[2,512]{1,0:T(2,128)}, s32[2,512]{1,0:T(2,128)S(1)}, u32[]{:S(2)}) copy-start(s32[2,512]{1,0:T(2,128)S(1)} %pad_add_fusion.place_ref) | copy-start | bytes 12292
  167.5 39.2 %copy-start.71 = (s32[2]{0:T(128)}, s32[2]{0:T(128)S(1)}, u32[]{:S(2)}) copy-start(s32[2]{0:T(128)S(1)} %get-tuple-element.379.flag_ref) | copy-start | bytes 28
  191.1 24.2 %copy-start.73 = (s32[2]{0:T(128)}, s32[2]{0:T(128)S(1)}, u32[]{:S(2)}) copy-start(s32[2]{0:T(128)S(1)} %get-tuple-element.380.flag_ref) | copy-start | bytes 28
  191.1 45.6 %copy-start.75 = (s32[2]{0:T(128)}, s32[2]{0:T(128)S(1)}, u32[]{:S(2)}) copy-start(s32[2]{0:T(128)S(1)} %get-tuple-element.381.flag_ref) | copy-start | bytes 28
  191.1 22.6 %copy-start.77 = (bf16[512,512]{1,0:T(8,128)(2,1)}, bf16[512,512]{1,0:T(8,128)(2,1)S(1)}, u32[]{:S(2)}) copy-start(bf16[512,512]{1,0:T(8,128)(2,1)S(1)} %collective-permute-done.k_ref) | copy-start | bytes 1572868
  191.1 22.6 %collective-permute-start.1 = (bf16[512,512]{1,0:T(8,128)(2,1)S(1)}, bf16[512,512]{1,0:T(8,128)(2,1)S(1)}, u32[]{:S(2)}, u32[]{:S(2)}) collective-permute-start(bf16[512,512]{1,0:T(8,128)(2,1)S(1)} %collective-permute-done.k_ref), channel_id=1, source_target_pairs={{4,8},{8,12},{5,9},{9,13},{6,10},{10,14},{7,11},{11,15},{20,24},{2... | collective-permute-start | bytes 1572872 | tf_op jit(solution)/shard_map/ppermute | solution.py:1105
  206.0 8.4 collective-permute-start.4
  213.7 5.6 collective-permute-start.2
  214.5 4.9 collective-permute-start.5
  215.2 11.0 %collective-permute-start.8 = (bf16[512,1664]{1,0:T(8,128)(2,1)}, bf16[512,1664]{1,0:T(8,128)(2,1)}, u32[]{:S(2)}, u32[]{:S(2)}) collective-permute-start(bf16[512,1664]{1,0:T(8,128)(2,1)} %collective-permute-done.7), channel_id=1, source_target_pairs={{0,1},{1,0},{2,3},{3,2},{4,5},{5,4},{6,7},{7,6},{8,9},{9,8},{10,11... | collective-permute-start | bytes 5111816 | tf_op jit(solution)/shard_map/ppermute | solution.py:1012
  219.4 369.6 %reduce-scatter.3.cloned.1.call-start = ((), (), s32[]{:S(2)}) async-start(), calls=%async_computation.2 | async-start | bytes 10616832 | tf_op jit(solution)/shard_map/reduce_scatter | solution.py:1155
  240.6 348.4 %copy-start.108 = (f32[4,6,512]{2,1,0:T(8,128)}, f32[4,6,512]{2,1,0:T(8,128)S(1)}, u32[]{:S(2)}) copy-start(f32[4,6,512]{2,1,0:T(8,128)S(1)} %get-tuple-element.167.lse_ref) | copy-start | bytes 147460
  245.4 243.6 %copy-start.113 = (bf16[512,1536]{1,0:T(8,128)(2,1)}, bf16[512,1536]{1,0:T(8,128)(2,1)S(1)}, u32[]{:S(2)}) copy-start(bf16[512,1536]{1,0:T(8,128)(2,1)S(1)} %multiply_convert_fusion) | copy-start | bytes 4718596
  245.4 3.7 collective-permute-start.9
  245.9 37.2 %collective-permute-start.10 = (bf16[512,1536]{1,0:T(8,128)(2,1)S(1)}, bf16[512,1536]{1,0:T(8,128)(2,1)S(1)}, u32[]{:S(2)}, u32[]{:S(2)}) collective-permute-start(bf16[512,1536]{1,0:T(8,128)(2,1)S(1)} %multiply_convert_fusion), channel_id=1, source_target_pairs={{0,2},{1,3},{2,0},{3,1},{4,6},{5,7},{6,4},{7,5},{8,10},{9,11},{10,... | collective-permute-start | bytes 4718600 | tf_op jit(solution)/shard_map/ppermute | solution.py:1016
  283.1 55.4 %copy-start.132 = (bf16[512,1536]{1,0:T(8,128)(2,1)}, bf16[512,1536]{1,0:T(8,128)(2,1)S(1)}, u32[]{:S(2)}) copy-start(bf16[512,1536]{1,0:T(8,128)(2,1)S(1)} %collective-permute-done.10) | copy-start | bytes 4718596
  283.1 3.5 collective-permute-start.11
  360.0 518.5 %reduce-scatter.5.cloned.1.call-start = ((), (), s32[]{:S(2)}) async-start(), calls=%async_computation.3 | async-start | bytes 10616832 | tf_op jit(solution)/shard_map/reduce_scatter | solution.py:1155
  443.5 3.7 collective-permute-start.12
  447.6 39.4 %collective-permute-start.13 = (bf16[512,1664]{1,0:T(8,128)(2,1)S(1)}, bf16[512,1664]{1,0:T(8,128)(2,1)}, u32[]{:S(2)}, u32[]{:S(2)}) collective-permute-start(bf16[512,1664]{1,0:T(8,128)(2,1)S(1)} %add_convert_fusion), channel_id=1, source_target_pairs={{0,2},{1,3},{2,0},{3,1},{4,6},{5,7},{6,4},{7,5},{8,10},{9,11},{10,... | collective-permute-start | bytes 5111816 | tf_op jit(solution)/shard_map/ppermute | solution.py:1016
  488.7 3.7 collective-permute-start.14
  563.8 10.9 %collective-permute-start.18 = (bf16[512,512]{1,0:T(8,128)(2,1)S(1)}, bf16[512,512]{1,0:T(8,128)(2,1)S(1)}, u32[]{:S(2)}, u32[]{:S(2)}) collective-permute-start(bf16[512,512]{1,0:T(8,128)(2,1)S(1)} %get-tuple-element.365), channel_id=1, source_target_pairs={{12,8},{13,9},{14,10},{15,11},{28,24},{29,25},{30,26},{31,27}} | collective-permute-start | bytes 1572872 | tf_op jit(solution)/shard_map/ppermute | solution.py:1261
  564.5 10.2 %collective-permute-start.19 = (bf16[512,512]{1,0:T(8,128)(2,1)S(1)}, bf16[512,512]{1,0:T(8,128)(2,1)S(1)}, u32[]{:S(2)}, u32[]{:S(2)}) collective-permute-start(bf16[512,512]{1,0:T(8,128)(2,1)S(1)} %get-tuple-element.364), channel_id=1, source_target_pairs={{12,8},{13,9},{14,10},{15,11},{28,24},{29,25},{30,26},{31,27}} | collective-permute-start | bytes 1572872 | tf_op jit(solution)/shard_map/ppermute | solution.py:1261
  567.9 18.1 %collective-permute-start.15 = (bf16[512,1536]{1,0:T(8,128)(2,1)S(1)}, bf16[512,1536]{1,0:T(8,128)(2,1)S(1)}, u32[]{:S(2)}, u32[]{:S(2)}) collective-permute-start(bf16[512,1536]{1,0:T(8,128)(2,1)S(1)} %slice.238), channel_id=1, source_target_pairs={{0,1},{1,0},{2,3},{3,2},{4,5},{5,4},{6,7},{7,6},{8,9},{9,8},{10,11... | collective-permute-start | bytes 4718600 | tf_op jit(solution)/shard_map/ppermute | solution.py:1012
  569.5 167.9 %collective-permute-start.17 = (bf16[512,1536]{1,0:T(8,128)(2,1)}, bf16[512,1536]{1,0:T(8,128)(2,1)}, u32[]{:S(2)}, u32[]{:S(2)}) collective-permute-start(bf16[512,1536]{1,0:T(8,128)(2,1)} %slice.239), channel_id=1, source_target_pairs={{0,1},{1,0},{2,3},{3,2},{4,5},{5,4},{6,7},{7,6},{8,9},{9,8},{10,11... | collective-permute-start | bytes 4718600 | tf_op jit(solution)/shard_map/ppermute | solution.py:1012
  582.9 17.5 %collective-permute-start.20 = (bf16[512,512]{1,0:T(8,128)(2,1)}, bf16[512,512]{1,0:T(8,128)(2,1)}, u32[]{:S(2)}, u32[]{:S(2)}) collective-permute-start(bf16[512,512]{1,0:T(8,128)(2,1)} %get-tuple-element.362), channel_id=1, source_target_pairs={{8,4},{12,8},{9,5},{13,9},{10,6},{14,10},{11,7},{15,11},{24,20},{2... | collective-permute-start | bytes 1572872 | tf_op jit(solution)/shard_map/ppermute | solution.py:1261
  584.5 16.0 %collective-permute-start.21 = (bf16[512,512]{1,0:T(8,128)(2,1)}, bf16[512,512]{1,0:T(8,128)(2,1)}, u32[]{:S(2)}, u32[]{:S(2)}) collective-permute-start(bf16[512,512]{1,0:T(8,128)(2,1)} %get-tuple-element.363), channel_id=1, source_target_pairs={{8,4},{12,8},{9,5},{13,9},{10,6},{14,10},{11,7},{15,11},{24,20},{2... | collective-permute-start | bytes 1572872 | tf_op jit(solution)/shard_map/ppermute | solution.py:1261
  587.6 149.8 %collective-permute-start.16 = (bf16[512,1536]{1,0:T(8,128)(2,1)}, bf16[512,1536]{1,0:T(8,128)(2,1)}, u32[]{:S(2)}, u32[]{:S(2)}) collective-permute-start(bf16[512,1536]{1,0:T(8,128)(2,1)} %add_convert_fusion.2), channel_id=1, source_target_pairs={{0,2},{1,3},{2,0},{3,1},{4,6},{5,7},{6,4},{7,5},{8,10},{9,11},{10,... | collective-permute-start | bytes 4718600 | tf_op jit(solution)/shard_map/ppermute | solution.py:1016
  604.0 111.8 %collective-permute-start.22 = (bf16[512,512]{1,0:T(8,128)(2,1)}, bf16[512,512]{1,0:T(8,128)(2,1)}, u32[]{:S(2)}, u32[]{:S(2)}) collective-permute-start(bf16[512,512]{1,0:T(8,128)(2,1)} %get-tuple-element.360), channel_id=1, source_target_pairs={{4,0},{8,4},{12,8},{5,1},{9,5},{13,9},{6,2},{10,6},{14,10},{7,3},{... | collective-permute-start | bytes 1572872 | tf_op jit(solution)/shard_map/ppermute | solution.py:1261
  605.2 120.7 %collective-permute-start.23 = (bf16[512,512]{1,0:T(8,128)(2,1)}, bf16[512,512]{1,0:T(8,128)(2,1)}, u32[]{:S(2)}, u32[]{:S(2)}) collective-permute-start(bf16[512,512]{1,0:T(8,128)(2,1)} %get-tuple-element.361), channel_id=1, source_target_pairs={{4,0},{8,4},{12,8},{5,1},{9,5},{13,9},{6,2},{10,6},{14,10},{7,3},{... | collective-permute-start | bytes 1572872 | tf_op jit(solution)/shard_map/ppermute | solution.py:1261
  649.8 87.3 %copy-start.99 = (bf16[512,1536]{1,0:T(8,128)(2,1)}, bf16[512,1536]{1,0:T(8,128)(2,1)S(1)}, u32[]{:S(2)}) copy-start(bf16[512,1536]{1,0:T(8,128)(2,1)S(1)} %get-tuple-element.180) | copy-start | bytes 4718596
  649.8 77.8 %copy-start.10 = (bf16[1,1,512,1536]{3,2,1,0:T(8,128)(2,1)S(1)}, bf16[1,1,512,1536]{3,2,1,0:T(8,128)(2,1)}, u32[]{:S(2)}) copy-start(bf16[1,1,512,1536]{3,2,1,0:T(8,128)(2,1)} %param.23) | copy-start | bytes 4718596
  649.8 77.8 %copy-start.145 = (f32[1536]{0:T(1024)S(1)}, f32[1536]{0:T(1024)}, u32[]{:S(2)}) copy-start(f32[1536]{0:T(1024)} %get-tuple-element.352) | copy-start | bytes 18436
  745.8 125.6 %copy-start.112 = (f32[512,1536]{1,0:T(8,128)S(1)}, f32[512,1536]{1,0:T(8,128)}, u32[]{:S(2)}) copy-start(f32[512,1536]{1,0:T(8,128)} %copy-done.110) | copy-start | bytes 9437188
  (139 other events, 581.8 us)
Sparse Core Ops, SparseCore 0:
  12.1 190.7 all-gather.4
  219.5 190.0 all-gather.6
  413.2 169.6 reduce-scatter.2
  586.3 200.5 reduce-scatter.4
